TPU v7x, 32 devices: a whole 2x2x4 slice. The times are simulated.
32 devices in a mesh: parts: 1, tile: 16 (over z, y, core), face: 2 (over x), sub: 1.
Axes of the slice: x: 2, y: 2, z: 4, core: 2. Of those that a mesh axis runs over, the one named last changes fastest.
Arguments:
- fields: bfloat16 [96, 4, 32, 96], P('sub', 'face', 'tile', 'parts'), may hold values from -6 to 6
- upstream: bfloat16 [96, 4, 32, 96], P('sub', 'face', 'tile', 'parts'), may hold values from -6 to 6
- kernel_one: bfloat16 [3, 3, 96, 96], replicated, may hold values from -0.21875 to 0.21875
- kernel_two: bfloat16 [3, 3, 96, 96], replicated, may hold values from -0.21875 to 0.21875
Outputs:
- result: bfloat16 [96, 4, 32, 96], P('sub', 'face', 'tile', 'parts')
- fields_grad: bfloat16 [96, 4, 32, 96], P('sub', 'face', 'tile', 'parts')
- kernel_one_grad: float32 [3, 3, 96, 96], P('parts', None, None, 'sub')
- kernel_two_grad: float32 [3, 3, 96, 96], P('parts', None, None, 'sub')
All inputs are finite; a program needn't handle non-finite values.
Results may differ from a plain program's by a relative error of at most 0.0049.
Values may be sent and summed in bfloat16 or wider, within the bound.
No kernel may reach another device: no remote copies, remote signals or barrier semaphores. Data moves between devices by JAX's collectives and lax.ppermute only.
A program may use at most 128 MiB of HBM per device.

v0:
```python
import functools

import jax
import jax.numpy as jnp
import numpy as np
from jax import lax
from jax.experimental import pallas as pl
from jax.experimental.pallas import tpu as pltpu
from jax.sharding import PartitionSpec as P

BOTH = ("tile", "face")
F32 = jnp.float32
BF16 = jnp.bfloat16
GELU_A = 0.7978845608028654
GELU_B = 0.044715


def up_to(value, step):
    return -(-value // step) * step


class Plan:
    def __init__(self, mesh_shape, block):
        self.tiles = mesh_shape["tile"]
        self.faces = mesh_shape["face"]
        self.stacks, self.cols, self.height = block[1:4]
        self.side = self.height // 3
        self.lanes = up_to(self.height + 2, 128)
        self.channels = block[0] * mesh_shape["sub"]
        self.own = block[0]
        w = self.cols
        self.a_line, self.b_line = 0, w + 2
        self.a_row, self.b_row = 2 * (w + 2), 2 * (w + 2) + w
        self.cells = up_to(4 * w + 4, 16)
        self.kinds = 2 if self.stacks > 1 else 1
        self.near = 2
        self.mid = 2 * self.faces
        self.far = self.tiles // 4
        self.terms = 2 * 9 * self.channels
        self.piece = up_to(-(-self.terms // (self.near * self.mid)), 16)

    def send_table(self):
        t, k, c = self.tiles, self.kinds, self.cells
        g, w, n = self.stacks, self.cols, self.lanes
        table = np.zeros((t, k, c, g, w, n), np.float32)
        for dest in range(t):
            for kind in range(k):
                same = kind == 0 and k == 2
                from_a = 1 if same else 0
                from_b = 0 if same else g - 1
                for e in range(w + 2):
                    row = w * dest - 1 + e
                    if row >= 0:
                        table[dest, kind, self.a_line + e, from_a, 0, row] = 1
                    row = 2 * self.side + w * dest - 1 + e
                    if row < self.height:
                        table[dest, kind, self.b_line + e, from_b, w - 1, row] = 1
                for e in range(w):
                    table[dest, kind, self.a_row + e, from_a, e, self.height - 1] = 1
                    table[dest, kind, self.b_row + e, from_b, e, 0] = 1
        return jnp.asarray(table.reshape(t * k * c, g * w * n), BF16)

    def take_tables(self):
        t, c, w, n = self.tiles, self.cells, self.cols, self.lanes
        from_a = np.zeros((t, c, 2 * n), np.float32)
        from_b = np.zeros((t, c, 2 * n), np.float32)
        for src in range(t):
            for e in range(w):
                from_a[src, self.a_row + e, 2 * self.side + src * w + e] = 1
                from_b[src, self.b_row + e, src * w + e] = 1
        for e in range(w + 2):
            from_a[0, self.a_line + e, n + e] = 1
            from_b[t - 1, self.b_line + e, n + e] = 1
        shape = (t * c, 2 * n)
        return jnp.asarray(from_a.reshape(shape), BF16), jnp.asarray(from_b.reshape(shape), BF16)


def pack_blocks(plan, face, columns, table, blocks_ref):
    t, c = plan.tiles, plan.cells
    for k in range(2):
        flat = jnp.concatenate([x for per in columns[k] for x in per], axis=1)
        picked = lax.dot_general(
            table, flat, (((1,), (1,)), ((), ())), preferred_element_type=F32
        ).astype(BF16)
        picked = picked.reshape(t, plan.kinds, c, flat.shape[0])
        for dest in range(plan.faces):
            if plan.kinds == 2:
                block = jnp.where(face == dest, picked[:, 0], picked[:, 1])
            else:
                block = picked[:, 0]
            blocks_ref[:, dest, k * c : (k + 1) * c, :] = block


def shift(x, by):
    return pltpu.roll(x, by % x.shape[1], 1)


def halos(plan, ids_ref, k, left_ref, right_ref, cross_ref, got_ref, tab_a, tab_b):
    first = ids_ref[0] == 0
    last = ids_ref[0] == plan.tiles - 1
    face = ids_ref[1]
    after = lax.rem(face + 1, plan.faces)
    before = lax.rem(face + plan.faces - 1, plan.faces)
    c = plan.cells
    result = []
    for g in range(plan.stacks):
        face_a = face if g < plan.stacks - 1 else after
        face_b = face if g > 0 else before
        seams = []
        for at, table in ((face_a, tab_a), (face_b, tab_b)):
            rows = got_ref[:, at, k * c : (k + 1) * c, :]
            rows = rows.reshape(plan.tiles * c, rows.shape[-1])
            seams.append(
                lax.dot_general(
                    rows, table, (((0,), (0,)), ((), ())), preferred_element_type=F32
                )
            )
        end_l = left_ref[k, g - 1] if g > 0 else cross_ref[k]
        end_r = right_ref[k, g + 1] if g < plan.stacks - 1 else cross_ref[k]
        n = plan.lanes
        result.append(
            dict(
                first=first,
                last=last,
                left=left_ref[k, g].astype(F32),
                right=right_ref[k, g].astype(F32),
                row_l=seams[1][:, :n],
                row_r=seams[0][:, :n],
                col_l=shift(end_l.astype(F32), plan.side),
                col_r=shift(end_r.astype(F32), -plan.side),
                top=[seams[0][:, n + e : n + e + 1] for e in range(plan.cols + 2)],
                bottom=[seams[1][:, n + e : n + e + 1] for e in range(plan.cols + 2)],
            )
        )
    return result


def forward_operand(plan, own, halo, taps_ref):
    w, n, side, height = plan.cols, plan.lanes, plan.side, plan.height
    c = plan.channels
    lane = lax.broadcasted_iota(jnp.int32, (c, n), 1)
    for g in range(plan.stacks):
        h = halo[g]
        edge_l = jnp.where(lane < side, h["row_l"], jnp.where(lane < height, h["col_l"], 0.0))
        edge_r = jnp.where(
            lane < 2 * side, h["col_r"], jnp.where(lane < height, h["row_r"], 0.0)
        )
        columns = [h["left"]] + own[g] + [h["right"]]
        for j in range(w + 2):
            x = jnp.where(lane == height, h["bottom"][j], columns[j])
            x = jnp.where(lane == n - 1, h["top"][j], x)
            if j == 0:
                x = jnp.where(h["first"], edge_l, x)
            if j == w + 1:
                x = jnp.where(h["last"], edge_r, x)
            for b in range(3):
                y = (x if b == 1 else shift(x, 1 - b)).astype(BF16)
                for a in range(3):
                    out = j - a
                    if 0 <= out < w:
                        at = (g * w + out) * n
                        row = (a * 3 + b) * c
                        taps_ref[row : row + c, at : at + n] = y


def backward_operand(plan, own, halo, taps_ref):
    w, n, side, height = plan.cols, plan.lanes, plan.side, plan.height
    c = plan.channels
    lane = lax.broadcasted_iota(jnp.int32, (c, n), 1)
    zero = jnp.zeros((c, n), BF16)
    for g in range(plan.stacks):
        h = halo[g]
        first, last = h["first"], h["last"]
        edge_l = jnp.where((lane >= side) & (lane <= height), h["col_l"], 0.0)
        edge_r = jnp.where((lane < 2 * side) | (lane == n - 1), h["col_r"], 0.0)
        columns = [jnp.where(first, edge_l, h["left"])] + own[g]
        columns += [jnp.where(last, edge_r, h["right"])]
        keep_l = (lane >= side) | jnp.logical_not(first)
        keep_r = (lane < 2 * side) | jnp.logical_not(last)
        for j in range(w + 2):
            for b in range(3):
                y = columns[j] if b == 1 else shift(columns[j], b - 1)
                if j == 0:
                    y = jnp.where(keep_l, y, 0.0)
                if j == w + 1:
                    y = jnp.where(keep_r, y, 0.0)
                y = y.astype(BF16)
                for a in range(3):
                    out = j - 2 + a
                    if 0 <= out < w:
                        at = (g * w + out) * n
                        row = (a * 3 + b) * c
                        taps_ref[row : row + c, at : at + n] = y
        seam_l = first & (lane < side)
        seam_r = last & (lane >= 2 * side) & (lane < height)
        for out in range(w):
            at = (g * w + out) * n
            for b in range(3):
                y = jnp.where(lane == 0, h["top"][out + 2 - b], 0.0).astype(BF16)
                taps_ref[(9 + b) * c : (10 + b) * c, at : at + n] = y
                y = jnp.where(lane == height - 1, h["bottom"][out + 2 - b], 0.0).astype(BF16)
                taps_ref[(12 + b) * c : (13 + b) * c, at : at + n] = y
                y = zero
                if out == 0:
                    y = jnp.where(seam_l, shift(h["row_l"], b - 1), 0.0).astype(BF16)
                taps_ref[(15 + b) * c : (16 + b) * c, at : at + n] = y
                y = zero
                if out == w - 1:
                    y = jnp.where(seam_r, shift(h["row_r"], b - 1), 0.0).astype(BF16)
                taps_ref[(18 + b) * c : (19 + b) * c, at : at + n] = y


def own_columns(plan, refs, k):
    return [
        [refs[w][k, g].astype(F32) for w in range(plan.cols)] for g in range(plan.stacks)
    ]


def first_kernel(plan, ids_ref, table_ref, *refs):
    columns = refs[: plan.cols]
    blocks_ref = refs[plan.cols]
    parts = [
        [[columns[w][k, g] for w in range(plan.cols)] for g in range(plan.stacks)]
        for k in range(2)
    ]
    pack_blocks(plan, ids_ref[1], parts, table_ref[...], blocks_ref)


def middle_kernel(plan, ids_ref, *refs):
    w, n, g_count, c = plan.cols, plan.lanes, plan.stacks, plan.channels
    columns, refs = refs[:w], refs[w:]
    left, right, cross, got, table, tab_a, tab_b, w_one, w_two = refs[:9]
    refs = refs[9:]
    new_columns, refs = refs[:w], refs[w:]
    blocks_ref, mine_ref, theirs_ref, fwd_ref, bwd_ref, sums_ref = refs
    tab_a, tab_b = tab_a[...], tab_b[...]
    halo = halos(plan, ids_ref, 0, left, right, cross, got, tab_a, tab_b)
    forward_operand(plan, own_columns(plan, columns, 0), halo, fwd_ref)
    halo = halos(plan, ids_ref, 1, left, right, cross, got, tab_a, tab_b)
    upstream = own_columns(plan, columns, 1)
    backward_operand(plan, upstream, halo, bwd_ref)
    pre = jnp.dot(w_one[...], fwd_ref[...], preferred_element_type=F32)
    grad = jnp.dot(w_two[...], bwd_ref[...], preferred_element_type=F32)
    lane = lax.broadcasted_iota(jnp.int32, pre.shape, 1) % n
    inside = lane < plan.height
    bend = jnp.tanh(GELU_A * (pre + GELU_B * (pre * pre * pre)))
    half = 0.5 * (1.0 + bend)
    slope = half + 0.5 * pre * (1.0 - bend * bend) * (
        GELU_A * (1.0 + (3.0 * GELU_B) * (pre * pre))
    )
    hidden = jnp.where(inside, pre * half, 0.0).astype(BF16)
    pre_grad = jnp.where(inside, grad * slope, 0.0).astype(BF16)
    both = (hidden, pre_grad)
    parts = [
        [[both[k][:, (g * w + i) * n : (g * w + i + 1) * n] for i in range(w)] for g in range(g_count)]
        for k in range(2)
    ]
    for k in range(2):
        for g in range(g_count):
            for i in range(w):
                new_columns[i][k, g] = parts[k][g][i]
    pack_blocks(plan, ids_ref[1], parts, table[...], blocks_ref)
    own = plan.own
    half_at = ids_ref[2]
    cot = pre_grad
    terms = lax.dot_general(
        fwd_ref[...], cot, (((1,), (1,)), ((), ())), preferred_element_type=F32
    )
    turned = lax.dot_general(
        bwd_ref[...], hidden, (((1,), (1,)), ((), ())), preferred_element_type=F32
    )
    tap = [turned[i * c : (i + 1) * c] for i in range(21)]
    for b in range(3):
        tap[b] = tap[b] + tap[9 + b]
        tap[6 + b] = tap[6 + b] + tap[12 + b]
    for a in range(3):
        tap[3 * a] = tap[3 * a] + tap[15 + a]
        tap[3 * a + 2] = tap[3 * a + 2] + tap[18 + a]
    sums_ref[0 : 9 * c, :] = terms
    for i in range(9):
        sums_ref[(9 + i) * c : (10 + i) * c, :] = jnp.transpose(tap[i])
    rest = sums_ref.shape[0] - 18 * c
    if rest:
        sums_ref[18 * c :, :] = jnp.zeros((rest, c), F32)
    near, mid = ids_ref[3], ids_ref[4]
    for d in range(plan.mid):
        spot = jnp.bitwise_xor(mid, d)
        for other, ref in ((0, mine_ref), (1, theirs_ref)):
            at = (jnp.bitwise_xor(near, other) * plan.mid + spot) * plan.piece
            rows = sums_ref[pl.ds(pl.multiple_of(at, 16), plan.piece), :]
            ref[d] = rows.astype(ref.dtype)


def last_kernel(plan, ids_ref, *refs):
    w, n = plan.cols, plan.lanes
    columns, refs = refs[:w], refs[w:]
    left, right, cross, got, tab_a, tab_b, w_two, w_one, out_ref, back_ref, fwd_ref, bwd_ref = refs
    tab_a, tab_b = tab_a[...], tab_b[...]
    halo = halos(plan, ids_ref, 0, left, right, cross, got, tab_a, tab_b)
    forward_operand(plan, own_columns(plan, columns, 0), halo, fwd_ref)
    halo = halos(plan, ids_ref, 1, left, right, cross, got, tab_a, tab_b)
    backward_operand(plan, own_columns(plan, columns, 1), halo, bwd_ref)
    out = jnp.dot(w_two[...], fwd_ref[...], preferred_element_type=F32).astype(BF16)
    back = jnp.dot(w_one[...], bwd_ref[...], preferred_element_type=F32).astype(BF16)
    for g in range(plan.stacks):
        for i in range(w):
            at = (g * w + i) * n
            out_ref[g, i] = out[:, at : at + plan.height]
            back_ref[g, i] = back[:, at : at + plan.height]


def sum_kernel(plan, scale, ids_ref, mine_ref, theirs_ref, sums_ref):
    near, mid = ids_ref[3], ids_ref[4]
    for d in range(plan.mid):
        spot = jnp.bitwise_xor(mid, d)
        for other, ref in ((0, mine_ref), (1, theirs_ref)):
            at = (jnp.bitwise_xor(near, other) * plan.mid + spot) * plan.piece
            sums_ref[pl.ds(pl.multiple_of(at, 16), plan.piece), :] = ref[d].astype(F32) * scale


VMEM = pl.BlockSpec(memory_space=pltpu.VMEM)
SMEM = pl.BlockSpec(memory_space=pltpu.SMEM)


def call(body, ids, inputs, outs, scratch=()):
    return pl.pallas_call(
        body,
        out_shape=outs,
        in_specs=[SMEM] + [VMEM] * len(inputs),
        out_specs=[VMEM] * len(outs),
        scratch_shapes=list(scratch),
        compiler_params=pltpu.CompilerParams(vmem_limit_bytes=48 * 2**20),
    )(ids, *inputs)


def tile_ring(plan, x, step):
    count = plan.tiles
    pairs = [(i, (i + step) % count) for i in range(count)]
    if plan.stacks == 1:
        pairs = [(i, j) for i, j in pairs if j == i + step]
    return lax.ppermute(x, "tile", pairs)


def swap_ends(plan, columns):
    t, f = plan.tiles, plan.faces
    first = lax.axis_index("tile") == 0
    sent = jnp.where(first, columns[0][:, 0], columns[-1][:, plan.stacks - 1])
    pairs = [((t - 1) * f + i, (i + 1) % f) for i in range(f)]
    pairs += [((i + 1) % f, (t - 1) * f + i) for i in range(f)]
    return lax.ppermute(sent, BOTH, pairs)


def exchange(plan, columns, blocks):
    left = tile_ring(plan, columns[-1], 1)
    right = tile_ring(plan, columns[0], -1)
    cross = swap_ends(plan, columns)
    count = plan.tiles * plan.faces
    flat = blocks.reshape((count,) + blocks.shape[2:])
    got = lax.all_to_all(flat, BOTH, 0, 0, tiled=True).reshape(blocks.shape)
    return left, right, cross, got


def swapped(plan, x, near=0, mid=0, far=0):
    f = plan.faces
    pairs = []
    for i in range(plan.tiles * f):
        tile, face = i // f, i % f
        tile = tile ^ near ^ ((mid // f) << 1) ^ (far << 2)
        pairs.append((i, tile * f + (face ^ (mid % f))))
    return lax.ppermute(x, BOTH, pairs)


def tree_sum(values):
    while len(values) > 1:
        values = [a + b for a, b in zip(values[::2], values[1::2])]
    return values[0]


def sum_all(plan, mine, theirs):
    half = mine + swapped(plan, theirs, near=1).astype(F32)
    short = half.astype(BF16)
    got = [swapped(plan, short[d], mid=d).astype(F32) for d in range(1, plan.mid)]
    piece = tree_sum([half[0]] + got).astype(BF16)
    got = [swapped(plan, piece, far=d) for d in range(1, plan.far)]
    piece = tree_sum([x.astype(F32) for x in [piece] + got]).astype(BF16)
    pieces = [piece] + [swapped(plan, piece, mid=d) for d in range(1, plan.mid)]
    half = jnp.stack(pieces)
    return half, swapped(plan, half, near=1)


def seam_weights(kernel):
    lines = [kernel.reshape(kernel.shape[0], 9, -1), kernel[:, 0], kernel[:, 2]]
    lines += [kernel[:, :, 0], kernel[:, :, 2]]
    return jnp.concatenate(lines, axis=1).reshape(kernel.shape[0], -1)


def on_device(mesh_shape, fields, upstream, kernel_one, kernel_two):
    plan = Plan(mesh_shape, fields.shape)
    c, own, w, n = plan.channels, plan.own, plan.cols, plan.lanes
    g, h = plan.stacks, plan.height
    tile, face = lax.axis_index("tile"), lax.axis_index("face")
    sub = lax.axis_index("sub")
    mid = ((tile >> 1) & 1) * plan.faces + face
    ids = jnp.stack([tile, face, sub, tile & 1, mid]).astype(jnp.int32)
    if mesh_shape["sub"] > 1:
        fields = lax.all_gather(fields, "sub", axis=0, tiled=True)
        upstream = lax.all_gather(upstream, "sub", axis=0, tiled=True)

    def column(at):
        both = jnp.stack([fields[:, :, at], upstream[:, :, at]])
        return jnp.pad(both.transpose(0, 2, 1, 3), ((0, 0), (0, 0), (0, 0), (0, n - h)))

    columns = [column(i) for i in range(w)]
    table = plan.send_table()
    tab_a, tab_b = plan.take_tables()
    blocks_shape = jax.ShapeDtypeStruct((plan.tiles, plan.faces, 2 * plan.cells, c), BF16)
    (blocks,) = call(
        functools.partial(first_kernel, plan), ids, [table] + columns, [blocks_shape]
    )
    halo = exchange(plan, columns, blocks)

    fwd_one = kernel_one.transpose(3, 0, 1, 2).reshape(c, -1)
    bwd_two = seam_weights(kernel_two.transpose(2, 0, 1, 3))
    fwd_two = lax.dynamic_slice_in_dim(kernel_two, sub * own, own, 3)
    fwd_two = fwd_two.transpose(3, 0, 1, 2).reshape(own, -1)
    bwd_one = lax.dynamic_slice_in_dim(kernel_one, sub * own, own, 2)
    bwd_one = seam_weights(bwd_one.transpose(2, 0, 1, 3))

    taps = [
        pltpu.VMEM((9 * c, g * w * n), BF16),
        pltpu.VMEM((21 * c, g * w * n), BF16),
    ]
    column_shape = jax.ShapeDtypeStruct((2, g, c, n), BF16)
    piece = (plan.mid, plan.piece, c)
    rows = plan.near * plan.mid * plan.piece
    results = call(
        functools.partial(middle_kernel, plan),
        ids,
        columns + list(halo) + [table, tab_a, tab_b, fwd_one, bwd_two],
        [column_shape] * w
        + [blocks_shape, jax.ShapeDtypeStruct(piece, F32), jax.ShapeDtypeStruct(piece, BF16)],
        taps + [pltpu.VMEM((rows, c), F32)],
    )
    columns, (blocks, mine, theirs) = list(results[:w]), results[w:]
    halo = exchange(plan, columns, blocks)
    mine, theirs = sum_all(plan, mine, theirs)
    out_shape = jax.ShapeDtypeStruct((g, w, own, h), BF16)
    result, fields_grad = call(
        functools.partial(last_kernel, plan),
        ids,
        columns + list(halo) + [tab_a, tab_b, fwd_two, bwd_one],
        [out_shape, out_shape],
        taps,
    )
    scale = 1.0 / (plan.side * 12.0**0.5)
    (sums,) = call(
        functools.partial(sum_kernel, plan, scale),
        ids,
        [mine, theirs],
        [jax.ShapeDtypeStruct((rows, c), F32)],
    )
    grads = []
    for i in range(2):
        grad = sums[9 * c * i : 9 * c * (i + 1)].reshape(3, 3, c, c)
        grads.append(lax.dynamic_slice_in_dim(grad, sub * own, own, 3))
    return (
        result.transpose(2, 0, 1, 3),
        fields_grad.transpose(2, 0, 1, 3),
        grads[0],
        grads[1],
    )


def solution(mesh):
    placed = (P("sub", "face", "tile", "parts"), P("sub", "face", "tile", "parts"), P(), P())
    return jax.shard_map(
        functools.partial(on_device, dict(mesh.shape)),
        mesh=mesh,
        in_specs=placed,
        out_specs=(
            P("sub", "face", "tile", "parts"),
            P("sub", "face", "tile", "parts"),
            P("parts", None, None, "sub"),
            P("parts", None, None, "sub"),
        ),
        check_vma=False,
    )
```

profile of v0, /device:TPU:0, one launch (start us, length us, event | category | flops | bytes accessed | tf_op | source)
XLA Modules:
  0.0 71.9 jit_solution(10495498857282606972)
XLA Ops:
  0.6 1.1 %fusion.7 = (bf16[96,2,1,96]{3,2,1,0:T(2,128)(2,1)S(1)}, bf16[96,2,1,96]{3,2,1,0:T(2,128)(2,1)S(1)}) fusion(bf16[96,2,2,96]{3,2,1,0:T(2,128)(2,1)} %param.8), kind=kLoop, calls=%fused_computation.30 | loop fusion | bytes 147456 | tf_op jit(solution)/shard_map/slice | solution.py:410
  1.8 0.1 fusion.6
  2.1 0.5 collective-permute-start
  2.6 5.1 %collective-permute-start.1 = (bf16[2,2,96,128]{3,2,0,1:T(8,128)(2,1)S(1)}, bf16[2,2,96,128]{3,2,0,1:T(8,128)(2,1)S(1)}, u32[]{:S(2)}, u32[]{:S(2)}) collective-permute-start(bf16[2,2,96,128]{3,2,0,1:T(8,128)(2,1)S(1)} %pad.7), channel_id=1, source_target_pairs={{0,30},{2,0},{4,2},{6,4},{8,6},{10,8},{12,10},{14,12},{16,14},{18,... | collective-permute-start | bytes 294920 | tf_op jit(solution)/shard_map/ppermute | solution.py:341
  7.7 3.5 %collective-permute-start.2 = (bf16[2,96,128]{2,1,0:T(8,128)(2,1)S(1)}, bf16[2,96,128]{2,1,0:T(8,128)(2,1)S(1)}, u32[]{:S(2)}, u32[]{:S(2)}) collective-permute-start(bf16[2,96,128]{2,1,0:T(8,128)(2,1)S(1)} %select_bitcast_fusion), channel_id=1, source_target_pairs={{30,1},{31,0},{1,30},{0,31}} | collective-permute-start | bytes 147464 | tf_op jit(solution)/shard_map/ppermute | solution.py:350
  11.3 0.1 stack.41.ids_ref
  11.4 1.7 %shard_map.102 = bf16[16,2,32,96]{3,2,1,0:T(8,128)(2,1)} custom-call(s32[5]{0:T(128)S(1)} %stack.41.ids_ref, bf16[512,512]{1,0:T(8,128)(2,1)S(1)} %copy-done, bf16[2,2,96,128]{3,2,1,0:T(8,128)(2,1)S(1)} %copy.48.refs_0_, bf16[2,2,96,128]{3,2,1,0:T(8,128)(2,1)S(1)} %copy.49.refs_1_), custom_call_target="tpu_custom_call" | custom-call | tf_op jit(solution)/shard_map/pallas_call | solution.py:326
  13.1 4.5 %all-to-all-start = ((bf16[32,32,96]{2,1,0:T(8,128)(2,1)}), bf16[32,32,96]{2,1,0:T(8,128)(2,1)S(1)}, u32[]{:S(2)}, u32[]{:S(2)}) async-start(bf16[32,32,96]{2,1,0:T(8,128)(2,1)} %bitcast.11), calls=%async_computation | async-start | bytes 524288 | tf_op jit(solution)/shard_map/all_to_all | solution.py:359
  17.6 0.0 copy-start.4
  17.7 0.9 %copy-done.4 = bf16[3,3,96,96]{3,2,1,0:T(8,128)(2,1)S(1)} copy-done((bf16[3,3,96,96]{3,2,1,0:T(8,128)(2,1)S(1)}, bf16[3,3,96,96]{3,2,1,0:T(8,128)(2,1)}, u32[]{:S(2)}) %copy-start.4) | copy-done | bytes 165912
  18.6 0.2 copy.52.refs_9_
  18.7 0.1 copy.43
  18.9 0.1 copy.44
  18.9 0.1 copy.45
  19.0 0.1 copy.46
  19.0 0.1 copy.47
  19.1 1.4 %concatenate.6 = bf16[96,21,96]{2,1,0:T(8,128)(2,1)S(1)} concatenate(bf16[96,9,96]{2,1,0:T(8,128)(2,1)S(1)} %copy.43, bf16[96,3,96]{2,1,0:T(4,128)(2,1)S(1)} %copy.44, bf16[96,3,96]{2,1,0:T(4,128)(2,1)S(1)} %copy.45, bf16[96,3,96]{2,1,0:T(4,128)(2,1)S(1)} %copy.46, bf16[96,3,96]{2,1,0:T(4,128)(2,1)S(1)} %copy.47), dimensions={1} | concatenate | bytes 774144 | tf_op jit(solution)/shard_map/concatenate | solution.py:394
  20.5 0.4 reshape.52.refs_10_
  20.9 0.0 copy-start.2
  20.9 0.0 copy-start.1
  20.9 0.0 collective-permute-done.1
  20.9 0.0 collective-permute-done.2.refs_4_
  21.0 7.3 %all-to-all-done = bf16[32,32,96]{2,1,0:T(8,128)(2,1)S(1)} async-done(((bf16[32,32,96]{2,1,0:T(8,128)(2,1)}), bf16[32,32,96]{2,1,0:T(8,128)(2,1)S(1)}, u32[]{:S(2)}, u32[]{:S(2)}) %all-to-all-start) | async-done | bytes 196640 | tf_op jit(solution)/shard_map/all_to_all | solution.py:359
  28.3 3.1 %shard_map.103 = (bf16[2,2,96,128]{3,2,1,0:T(8,128)(2,1)S(1)}, bf16[2,2,96,128]{3,2,1,0:T(8,128)(2,1)S(1)}, bf16[16,2,32,96]{3,2,1,0:T(8,128)(2,1)}, f32[4,224,96]{2,1,0:T(8,128)S(1)}, bf16[4,224,96]{2,1,0:T(8,128)(2,1)S(1)}) custom-call(s32[5]{0:T(128)S(1)} %stack.41.ids_ref, bf16[2,2,96,128]{3,2,1,0:T(8,128)(2,1)S(1)} %copy.48.refs_0_, ...), custom_call_target="tpu_custom_call" | custom-call | tf_op jit(solution)/shard_map/pallas_call | solution.py:326
  31.4 0.2 collective-permute-start.6
  31.6 1.4 %collective-permute-done.6 = bf16[4,224,96]{2,1,0:T(8,128)(2,1)S(1)} collective-permute-done((bf16[4,224,96]{2,1,0:T(8,128)(2,1)S(1)}, bf16[4,224,96]{2,1,0:T(8,128)(2,1)S(1)}, u32[]{:S(2)}, u32[]{:S(2)}) %collective-permute-start.6) | collective-permute-done | bytes 172064 | tf_op jit(solution)/shard_map/ppermute | solution.py:370
  33.0 0.1 fusion.4
  33.1 1.2 %collective-permute-start.9 = (bf16[224,96]{1,0:T(8,128)(2,1)S(1)}, bf16[224,96]{1,0:T(8,128)(2,1)S(1)}, u32[]{:S(2)}, u32[]{:S(2)}) collective-permute-start(bf16[224,96]{1,0:T(8,128)(2,1)S(1)} %get-tuple-element.31), channel_id=1, source_target_pairs={{0,5},{1,4},{2,7},{3,6},{4,1},{5,0},{6,3},{7,2},{8,13},{9,12},{10,... | collective-permute-start | bytes 129032 | tf_op jit(solution)/shard_map/ppermute | solution.py:370
  34.2 1.2 %collective-permute-start.8 = (bf16[224,96]{1,0:T(8,128)(2,1)S(1)}, bf16[224,96]{1,0:T(8,128)(2,1)S(1)}, u32[]{:S(2)}, u32[]{:S(2)}) collective-permute-start(bf16[224,96]{1,0:T(8,128)(2,1)S(1)} %get-tuple-element.32), channel_id=1, source_target_pairs={{0,4},{1,5},{2,6},{3,7},{4,0},{5,1},{6,2},{7,3},{8,12},{9,13},{10,... | collective-permute-start | bytes 129032 | tf_op jit(solution)/shard_map/ppermute | solution.py:370
  35.4 1.2 %collective-permute-start.7 = (bf16[224,96]{1,0:T(8,128)(2,1)S(1)}, bf16[224,96]{1,0:T(8,128)(2,1)S(1)}, u32[]{:S(2)}, u32[]{:S(2)}) collective-permute-start(bf16[224,96]{1,0:T(8,128)(2,1)S(1)} %get-tuple-element.30), channel_id=1, source_target_pairs={{0,1},{1,0},{2,3},{3,2},{4,5},{5,4},{6,7},{7,6},{8,9},{9,8},{10,11... | collective-permute-start | bytes 129032 | tf_op jit(solution)/shard_map/ppermute | solution.py:370
  36.6 1.9 %collective-permute-done.9 = bf16[224,96]{1,0:T(8,128)(2,1)S(1)} collective-permute-done((bf16[224,96]{1,0:T(8,128)(2,1)S(1)}, bf16[224,96]{1,0:T(8,128)(2,1)S(1)}, u32[]{:S(2)}, u32[]{:S(2)}) %collective-permute-start.9) | collective-permute-done | bytes 43040 | tf_op jit(solution)/shard_map/ppermute | solution.py:370
  38.6 0.6 collective-permute-done.8
  39.2 0.5 collective-permute-done.7
  39.6 1.6 %collective-permute-start.12 = (bf16[224,96]{1,0:T(8,128)(2,1)S(1)}, bf16[224,96]{1,0:T(8,128)(2,1)S(1)}, u32[]{:S(2)}, u32[]{:S(2)}) collective-permute-start(bf16[224,96]{1,0:T(8,128)(2,1)S(1)} %fusion.2), channel_id=1, source_target_pairs={{0,24},{1,25},{2,26},{3,27},{4,28},{5,29},{6,30},{7,31},{8,16},{9,... | collective-permute-start | bytes 129032 | tf_op jit(solution)/shard_map/ppermute | solution.py:370
  41.2 0.7 collective-permute-start.11
  41.9 2.2 %collective-permute-start.10 = (bf16[224,96]{1,0:T(8,128)(2,1)S(1)}, bf16[224,96]{1,0:T(8,128)(2,1)S(1)}, u32[]{:S(2)}, u32[]{:S(2)}) collective-permute-start(bf16[224,96]{1,0:T(8,128)(2,1)S(1)} %fusion.2), channel_id=1, source_target_pairs={{0,8},{1,9},{2,10},{3,11},{4,12},{5,13},{6,14},{7,15},{8,0},{9,1},... | collective-permute-start | bytes 129032 | tf_op jit(solution)/shard_map/ppermute | solution.py:370
  44.1 0.1 collective-permute-start.3
  44.2 4.4 %collective-permute-start.4 = (bf16[2,2,96,128]{3,2,1,0:T(8,128)(2,1)S(1)}, bf16[2,2,96,128]{3,2,1,0:T(8,128)(2,1)S(1)}, u32[]{:S(2)}, u32[]{:S(2)}) collective-permute-start(bf16[2,2,96,128]{3,2,1,0:T(8,128)(2,1)S(1)} %get-tuple-element.11.refs_0_), channel_id=1, source_target_pairs={{0,30},{2,0},{4,2},{6,4},{8,6},{10,8},{12,10},{14,12},{16,14},{18,... | collective-permute-start | bytes 294920 | tf_op jit(solution)/shard_map/ppermute | solution.py:341
  48.6 2.6 %all-to-all-start.1 = ((bf16[32,32,96]{2,1,0:T(8,128)(2,1)}), bf16[32,32,96]{2,1,0:T(8,128)(2,1)S(1)}, u32[]{:S(2)}, u32[]{:S(2)}) async-start(bf16[32,32,96]{2,1,0:T(8,128)(2,1)} %bitcast.22), calls=%async_computation.1 | async-start | bytes 524288 | tf_op jit(solution)/shard_map/all_to_all | solution.py:359
  51.2 0.0 collective-permute-done.12
  51.2 0.0 collective-permute-done.11
  51.3 2.6 %collective-permute-start.15 = (bf16[224,96]{1,0:T(8,128)(2,1)S(1)}, bf16[224,96]{1,0:T(8,128)(2,1)S(1)}, u32[]{:S(2)}, u32[]{:S(2)}) collective-permute-start(bf16[224,96]{1,0:T(8,128)(2,1)S(1)} %add_convert_fusion), channel_id=1, source_target_pairs={{0,5},{1,4},{2,7},{3,6},{4,1},{5,0},{6,3},{7,2},{8,13},{9,12},{10,... | collective-permute-start | bytes 129032 | tf_op jit(solution)/shard_map/ppermute | solution.py:370
  53.9 0.5 collective-permute-start.14
  54.4 0.4 collective-permute-start.13
  54.8 3.2 %collective-permute-done.15 = bf16[224,96]{1,0:T(8,128)(2,1)S(1)} collective-permute-done((bf16[224,96]{1,0:T(8,128)(2,1)S(1)}, bf16[224,96]{1,0:T(8,128)(2,1)S(1)}, u32[]{:S(2)}, u32[]{:S(2)}) %collective-permute-start.15) | collective-permute-done | bytes 43040 | tf_op jit(solution)/shard_map/ppermute | solution.py:370
  58.1 4.9 %collective-permute-start.5 = (bf16[2,96,128]{2,1,0:T(8,128)(2,1)S(1)}, bf16[2,96,128]{2,1,0:T(8,128)(2,1)S(1)}, u32[]{:S(2)}, u32[]{:S(2)}) collective-permute-start(bf16[2,96,128]{2,1,0:T(8,128)(2,1)S(1)} %fusion.3), channel_id=1, source_target_pairs={{30,1},{31,0},{1,30},{0,31}} | collective-permute-start | bytes 147464 | tf_op jit(solution)/shard_map/ppermute | solution.py:350
  63.0 0.0 collective-permute-done.14
  63.0 0.1 pad_maximum_fusion.mine_ref
  63.1 0.1 collective-permute-start.16
  63.2 0.2 copy.60.refs_8_
  63.4 0.1 copy.55
  63.5 0.1 copy.56
  63.5 0.1 copy.57
  63.6 0.1 copy.58
  63.7 0.1 copy.59
  63.7 1.4 %concatenate.7 = bf16[96,21,96]{2,1,0:T(8,128)(2,1)S(1)} concatenate(bf16[96,9,96]{2,1,0:T(8,128)(2,1)S(1)} %copy.55, bf16[96,3,96]{2,1,0:T(4,128)(2,1)S(1)} %copy.56, bf16[96,3,96]{2,1,0:T(4,128)(2,1)S(1)} %copy.57, bf16[96,3,96]{2,1,0:T(4,128)(2,1)S(1)} %copy.58, bf16[96,3,96]{2,1,0:T(4,128)(2,1)S(1)} %copy.59), dimensions={1} | concatenate | bytes 774144 | tf_op jit(solution)/shard_map/concatenate | solution.py:394
  65.1 0.4 reshape.57.refs_9_
  65.5 1.6 %collective-permute-done.5.refs_4_ = bf16[2,96,128]{2,1,0:T(8,128)(2,1)S(1)} collective-permute-done((bf16[2,96,128]{2,1,0:T(8,128)(2,1)S(1)}, bf16[2,96,128]{2,1,0:T(8,128)(2,1)S(1)}, u32[]{:S(2)}, u32[]{:S(2)}) %collective-permute-start.5) | collective-permute-done | bytes 49184 | tf_op jit(solution)/shard_map/ppermute | solution.py:350
  67.1 0.0 collective-permute-done.3.refs_2_
  67.1 1.8 %shard_map.104 = (bf16[2,2,96,96]{3,2,1,0:T(8,128)(2,1)S(1)}, bf16[2,2,96,96]{3,2,1,0:T(8,128)(2,1)S(1)}) custom-call(s32[5]{0:T(128)S(1)} %stack.41.ids_ref, bf16[2,2,96,128]{3,2,1,0:T(8,128)(2,1)S(1)} %get-tuple-element.11.refs_0_, bf16[2,2,96,128]{3,2,1,0:T(8,128)(2,1)S(1)} %get-tuple-element.12.refs_1_, ...), custom_call_target="tpu_custom_call" | custom-call | tf_op jit(solution)/shard_map/pallas_call | solution.py:326
  68.9 0.7 copy.61
  69.6 0.7 copy.62
  70.3 0.6 shard_map.105
  70.9 1.0 %fusion.5 = (f32[864,96]{1,0:T(8,128)}, f32[864,96]{1,0:T(8,128)}) fusion(f32[1792,96]{1,0:T(8,128)S(1)} %shard_map.105), kind=kLoop, calls=%fused_computation.28 | loop fusion | bytes 1327104 | tf_op jit(solution)/shard_map/slice | solution.py:464
  (33 shorter events, 0.4 us)
Async XLA Ops:
  0.6 1.2 %copy-start.5 = (bf16[96,2,2,96]{3,2,1,0:T(2,128)(2,1)S(1)}, bf16[96,2,2,96]{3,2,1,0:T(2,128)(2,1)}, u32[]{:S(2)}) copy-start(bf16[96,2,2,96]{3,2,1,0:T(2,128)(2,1)} %param.7) | copy-start | bytes 221188
  2.1 18.8 %collective-permute-start = (bf16[2,2,96,128]{3,2,0,1:T(8,128)(2,1)S(1)}, bf16[2,2,96,128]{3,2,0,1:T(8,128)(2,1)S(1)}, u32[]{:S(2)}, u32[]{:S(2)}) collective-permute-start(bf16[2,2,96,128]{3,2,0,1:T(8,128)(2,1)S(1)} %pad.8), channel_id=1, source_target_pairs={{0,2},{2,4},{4,6},{6,8},{8,10},{10,12},{12,14},{14,16},{16,18},{18... | collective-permute-start | bytes 294920 | tf_op jit(solution)/shard_map/ppermute | solution.py:341
  2.6 8.8 %copy-start = (bf16[512,512]{1,0:T(8,128)(2,1)S(1)}, bf16[512,512]{1,0:T(8,128)(2,1)}, u32[]{:S(2)}) copy-start(bf16[512,512]{1,0:T(8,128)(2,1)} %constant.27.clone.table_ref.refs_6_) | copy-start | bytes 1572868
  2.6 18.3 %collective-permute-start.1 = (bf16[2,2,96,128]{3,2,0,1:T(8,128)(2,1)S(1)}, bf16[2,2,96,128]{3,2,0,1:T(8,128)(2,1)S(1)}, u32[]{:S(2)}, u32[]{:S(2)}) collective-permute-start(bf16[2,2,96,128]{3,2,0,1:T(8,128)(2,1)S(1)} %pad.7), channel_id=1, source_target_pairs={{0,30},{2,0},{4,2},{6,4},{8,6},{10,8},{12,10},{14,12},{16,14},{18,... | collective-permute-start | bytes 294920 | tf_op jit(solution)/shard_map/ppermute | solution.py:341
  7.7 13.2 %collective-permute-start.2 = (bf16[2,96,128]{2,1,0:T(8,128)(2,1)S(1)}, bf16[2,96,128]{2,1,0:T(8,128)(2,1)S(1)}, u32[]{:S(2)}, u32[]{:S(2)}) collective-permute-start(bf16[2,96,128]{2,1,0:T(8,128)(2,1)S(1)} %select_bitcast_fusion), channel_id=1, source_target_pairs={{30,1},{31,0},{1,30},{0,31}} | collective-permute-start | bytes 147464 | tf_op jit(solution)/shard_map/ppermute | solution.py:350
  13.0 4.6 %copy-start.3 = (bf16[3,3,96,96]{3,2,1,0:T(8,128)(2,1)S(1)}, bf16[3,3,96,96]{3,2,1,0:T(8,128)(2,1)}, u32[]{:S(2)}) copy-start(bf16[3,3,96,96]{3,2,1,0:T(8,128)(2,1)} %param.10) | copy-start | bytes 497668
  13.1 15.2 %all-to-all-start = ((bf16[32,32,96]{2,1,0:T(8,128)(2,1)}), bf16[32,32,96]{2,1,0:T(8,128)(2,1)S(1)}, u32[]{:S(2)}, u32[]{:S(2)}) async-start(bf16[32,32,96]{2,1,0:T(8,128)(2,1)} %bitcast.11), calls=%async_computation | async-start | bytes 524288 | tf_op jit(solution)/shard_map/all_to_all | solution.py:359
  17.6 0.9 %copy-start.4 = (bf16[3,3,96,96]{3,2,1,0:T(8,128)(2,1)S(1)}, bf16[3,3,96,96]{3,2,1,0:T(8,128)(2,1)}, u32[]{:S(2)}) copy-start(bf16[3,3,96,96]{3,2,1,0:T(8,128)(2,1)} %param.9) | copy-start | bytes 497668
  20.9 7.4 %copy-start.2 = (bf16[256,256]{1,0:T(8,128)(2,1)S(1)}, bf16[256,256]{1,0:T(8,128)(2,1)}, u32[]{:S(2)}) copy-start(bf16[256,256]{1,0:T(8,128)(2,1)} %constant.29.clone.refs_8_.refs_7_) | copy-start | bytes 393220
  20.9 7.4 %copy-start.1 = (bf16[256,256]{1,0:T(8,128)(2,1)S(1)}, bf16[256,256]{1,0:T(8,128)(2,1)}, u32[]{:S(2)}) copy-start(bf16[256,256]{1,0:T(8,128)(2,1)} %constant.28.clone.refs_7_.refs_6_) | copy-start | bytes 393220
  31.4 1.6 %collective-permute-start.6 = (bf16[4,224,96]{2,1,0:T(8,128)(2,1)S(1)}, bf16[4,224,96]{2,1,0:T(8,128)(2,1)S(1)}, u32[]{:S(2)}, u32[]{:S(2)}) collective-permute-start(bf16[4,224,96]{2,1,0:T(8,128)(2,1)S(1)} %get-tuple-element.17), channel_id=1, source_target_pairs={{0,2},{1,3},{2,0},{3,1},{4,6},{5,7},{6,4},{7,5},{8,10},{9,11},{10,... | collective-permute-start | bytes 516104 | tf_op jit(solution)/shard_map/ppermute | solution.py:370
  33.1 5.5 %collective-permute-start.9 = (bf16[224,96]{1,0:T(8,128)(2,1)S(1)}, bf16[224,96]{1,0:T(8,128)(2,1)S(1)}, u32[]{:S(2)}, u32[]{:S(2)}) collective-permute-start(bf16[224,96]{1,0:T(8,128)(2,1)S(1)} %get-tuple-element.31), channel_id=1, source_target_pairs={{0,5},{1,4},{2,7},{3,6},{4,1},{5,0},{6,3},{7,2},{8,13},{9,12},{10,... | collective-permute-start | bytes 129032 | tf_op jit(solution)/shard_map/ppermute | solution.py:370
  34.2 4.9 %collective-permute-start.8 = (bf16[224,96]{1,0:T(8,128)(2,1)S(1)}, bf16[224,96]{1,0:T(8,128)(2,1)S(1)}, u32[]{:S(2)}, u32[]{:S(2)}) collective-permute-start(bf16[224,96]{1,0:T(8,128)(2,1)S(1)} %get-tuple-element.32), channel_id=1, source_target_pairs={{0,4},{1,5},{2,6},{3,7},{4,0},{5,1},{6,2},{7,3},{8,12},{9,13},{10,... | collective-permute-start | bytes 129032 | tf_op jit(solution)/shard_map/ppermute | solution.py:370
  35.4 4.2 %collective-permute-start.7 = (bf16[224,96]{1,0:T(8,128)(2,1)S(1)}, bf16[224,96]{1,0:T(8,128)(2,1)S(1)}, u32[]{:S(2)}, u32[]{:S(2)}) collective-permute-start(bf16[224,96]{1,0:T(8,128)(2,1)S(1)} %get-tuple-element.30), channel_id=1, source_target_pairs={{0,1},{1,0},{2,3},{3,2},{4,5},{5,4},{6,7},{7,6},{8,9},{9,8},{10,11... | collective-permute-start | bytes 129032 | tf_op jit(solution)/shard_map/ppermute | solution.py:370
  39.6 11.6 %collective-permute-start.12 = (bf16[224,96]{1,0:T(8,128)(2,1)S(1)}, bf16[224,96]{1,0:T(8,128)(2,1)S(1)}, u32[]{:S(2)}, u32[]{:S(2)}) collective-permute-start(bf16[224,96]{1,0:T(8,128)(2,1)S(1)} %fusion.2), channel_id=1, source_target_pairs={{0,24},{1,25},{2,26},{3,27},{4,28},{5,29},{6,30},{7,31},{8,16},{9,... | collective-permute-start | bytes 129032 | tf_op jit(solution)/shard_map/ppermute | solution.py:370
  41.2 10.0 %collective-permute-start.11 = (bf16[224,96]{1,0:T(8,128)(2,1)S(1)}, bf16[224,96]{1,0:T(8,128)(2,1)S(1)}, u32[]{:S(2)}, u32[]{:S(2)}) collective-permute-start(bf16[224,96]{1,0:T(8,128)(2,1)S(1)} %fusion.2), channel_id=1, source_target_pairs={{0,16},{1,17},{2,18},{3,19},{4,20},{5,21},{6,22},{7,23},{8,24},{9,... | collective-permute-start | bytes 129032 | tf_op jit(solution)/shard_map/ppermute | solution.py:370
  41.9 9.3 %collective-permute-start.10 = (bf16[224,96]{1,0:T(8,128)(2,1)S(1)}, bf16[224,96]{1,0:T(8,128)(2,1)S(1)}, u32[]{:S(2)}, u32[]{:S(2)}) collective-permute-start(bf16[224,96]{1,0:T(8,128)(2,1)S(1)} %fusion.2), channel_id=1, source_target_pairs={{0,8},{1,9},{2,10},{3,11},{4,12},{5,13},{6,14},{7,15},{8,0},{9,1},... | collective-permute-start | bytes 129032 | tf_op jit(solution)/shard_map/ppermute | solution.py:370
  44.1 22.9 %collective-permute-start.3 = (bf16[2,2,96,128]{3,2,1,0:T(8,128)(2,1)S(1)}, bf16[2,2,96,128]{3,2,1,0:T(8,128)(2,1)S(1)}, u32[]{:S(2)}, u32[]{:S(2)}) collective-permute-start(bf16[2,2,96,128]{3,2,1,0:T(8,128)(2,1)S(1)} %get-tuple-element.12.refs_1_), channel_id=1, source_target_pairs={{0,2},{2,4},{4,6},{6,8},{8,10},{10,12},{12,14},{14,16},{16,18},{18... | collective-permute-start | bytes 294920 | tf_op jit(solution)/shard_map/ppermute | solution.py:341
  44.2 22.9 %collective-permute-start.4 = (bf16[2,2,96,128]{3,2,1,0:T(8,128)(2,1)S(1)}, bf16[2,2,96,128]{3,2,1,0:T(8,128)(2,1)S(1)}, u32[]{:S(2)}, u32[]{:S(2)}) collective-permute-start(bf16[2,2,96,128]{3,2,1,0:T(8,128)(2,1)S(1)} %get-tuple-element.11.refs_0_), channel_id=1, source_target_pairs={{0,30},{2,0},{4,2},{6,4},{8,6},{10,8},{12,10},{14,12},{16,14},{18,... | collective-permute-start | bytes 294920 | tf_op jit(solution)/shard_map/ppermute | solution.py:341
  48.6 18.5 %all-to-all-start.1 = ((bf16[32,32,96]{2,1,0:T(8,128)(2,1)}), bf16[32,32,96]{2,1,0:T(8,128)(2,1)S(1)}, u32[]{:S(2)}, u32[]{:S(2)}) async-start(bf16[32,32,96]{2,1,0:T(8,128)(2,1)} %bitcast.22), calls=%async_computation.1 | async-start | bytes 524288 | tf_op jit(solution)/shard_map/all_to_all | solution.py:359
  51.3 6.8 %collective-permute-start.15 = (bf16[224,96]{1,0:T(8,128)(2,1)S(1)}, bf16[224,96]{1,0:T(8,128)(2,1)S(1)}, u32[]{:S(2)}, u32[]{:S(2)}) collective-permute-start(bf16[224,96]{1,0:T(8,128)(2,1)S(1)} %add_convert_fusion), channel_id=1, source_target_pairs={{0,5},{1,4},{2,7},{3,6},{4,1},{5,0},{6,3},{7,2},{8,13},{9,12},{10,... | collective-permute-start | bytes 129032 | tf_op jit(solution)/shard_map/ppermute | solution.py:370
  53.9 9.1 %collective-permute-start.14 = (bf16[224,96]{1,0:T(8,128)(2,1)S(1)}, bf16[224,96]{1,0:T(8,128)(2,1)S(1)}, u32[]{:S(2)}, u32[]{:S(2)}) collective-permute-start(bf16[224,96]{1,0:T(8,128)(2,1)S(1)} %add_convert_fusion), channel_id=1, source_target_pairs={{0,4},{1,5},{2,6},{3,7},{4,0},{5,1},{6,2},{7,3},{8,12},{9,13},{10,... | collective-permute-start | bytes 129032 | tf_op jit(solution)/shard_map/ppermute | solution.py:370
  54.4 8.6 %collective-permute-start.13 = (bf16[224,96]{1,0:T(8,128)(2,1)S(1)}, bf16[224,96]{1,0:T(8,128)(2,1)S(1)}, u32[]{:S(2)}, u32[]{:S(2)}) collective-permute-start(bf16[224,96]{1,0:T(8,128)(2,1)S(1)} %add_convert_fusion), channel_id=1, source_target_pairs={{0,1},{1,0},{2,3},{3,2},{4,5},{5,4},{6,7},{7,6},{8,9},{9,8},{10,11... | collective-permute-start | bytes 129032 | tf_op jit(solution)/shard_map/ppermute | solution.py:370
  58.1 9.0 %collective-permute-start.5 = (bf16[2,96,128]{2,1,0:T(8,128)(2,1)S(1)}, bf16[2,96,128]{2,1,0:T(8,128)(2,1)S(1)}, u32[]{:S(2)}, u32[]{:S(2)}) collective-permute-start(bf16[2,96,128]{2,1,0:T(8,128)(2,1)S(1)} %fusion.3), channel_id=1, source_target_pairs={{30,1},{31,0},{1,30},{0,31}} | collective-permute-start | bytes 147464 | tf_op jit(solution)/shard_map/ppermute | solution.py:350
  63.1 7.2 %collective-permute-start.16 = (bf16[4,224,96]{2,1,0:T(8,128)(2,1)S(1)}, bf16[4,224,96]{2,1,0:T(8,128)(2,1)S(1)}, u32[]{:S(2)}, u32[]{:S(2)}) collective-permute-start(bf16[4,224,96]{2,1,0:T(8,128)(2,1)S(1)} %pad_maximum_fusion.mine_ref), channel_id=1, source_target_pairs={{0,2},{1,3},{2,0},{3,1},{4,6},{5,7},{6,4},{7,5},{8,10},{9,11},{10,... | collective-permute-start | bytes 516104 | tf_op jit(solution)/shard_map/ppermute | solution.py:370
where the time goes:
time: 72.3 us; the launch traced here: 71.9 us
  starting transfers between devices  37.5 us (52%)
  waiting for transfers between devices  16.5 us (23%)
  local copies, waits for them, and re-layouts  9.36 us (13%)
  Pallas kernels  7.22 us (10%)
  between operations  1.09 us (2%)
    ppermute x11, starting transfers between devices, swapped(): return lax.ppermute(x, BOTH, pairs)  11.8 us
    ppermute x4, starting transfers between devices, tile_ring(): return lax.ppermute(x, 'tile', pairs)  10.1 us
    ppermute x2, starting transfers between devices, swap_ends(): return lax.ppermute(sent, BOTH, pairs)  8.46 us
    ppermute x11, waiting for transfers between devices, swapped(): return lax.ppermute(x, BOTH, pairs)  7.56 us
    all_to_all x2, waiting for transfers between devices, exchange(): got = lax.all_to_all(flat, BOTH, 0, 0, tiled=True).reshape(blocks.shape)  7.35 us
    pallas_call x4, Pallas kernels, call(): pl.pallas_call(body, out_shape=outs, in_specs=[SMEM] + [VMEM] * len(input...  7.22 us
    all_to_all x2, starting transfers between devices, exchange(): got = lax.all_to_all(flat, BOTH, 0, 0, tiled=True).reshape(blocks.shape)  7.14 us
    concatenate x2, local copies, waits for them, and re-layouts, seam_weights(): return jnp.concatenate(lines, axis=1).reshape(kernel.shape[0], -1)  2.7 us
  transfers between devices with their start and end apart: 19, of which 7 were waited for; matrix products, arithmetic and copies ran while one was open for 9% of the time, Pallas kernels for 5%

commit v1 on v0

--- a/solution.py
+++ b/solution.py
@@ -29,59 +29,96 @@
         self.channels = block[0] * mesh_shape["sub"]
         self.own = block[0]
         w = self.cols
-        self.a_line, self.b_line = 0, w + 2
-        self.a_row, self.b_row = 2 * (w + 2), 2 * (w + 2) + w
-        self.cells = up_to(4 * w + 4, 16)
+        self.reach = w + 4
+        self.line = (0, self.reach)
+        self.row = (2 * self.reach, 2 * self.reach + w)
+        self.cells = up_to(2 * self.reach + 2 * w, 16)
+        self.poles = up_to(2 * 3 * self.stacks, 16)
+        self.block = 2 * self.cells + self.poles
         self.kinds = 2 if self.stacks > 1 else 1
+        self.segments = self.stacks * (w + 2) + 1
+        self.rim = up_to(2 * self.stacks * 8, 1)
         self.near = 2
         self.mid = 2 * self.faces
         self.far = self.tiles // 4
         self.terms = 2 * 9 * self.channels
         self.piece = up_to(-(-self.terms // (self.near * self.mid)), 16)
 
-    def send_table(self):
+    def segment(self, stack, slot):
+        if 1 <= slot <= self.cols:
+            return stack * self.cols + slot - 1
+        return self.stacks * self.cols + 2 * stack + (1 if slot else 0)
+
+    def send_tables(self):
         t, k, c = self.tiles, self.kinds, self.cells
         g, w, n = self.stacks, self.cols, self.lanes
-        table = np.zeros((t, k, c, g, w, n), np.float32)
+        high = self.height - 1
+        table = np.zeros((2, t, k, c, g, w, n), np.float32)
+        poles = np.zeros((2, self.poles // 2, g, w, n), np.float32)
         for dest in range(t):
             for kind in range(k):
                 same = kind == 0 and k == 2
                 from_a = 1 if same else 0
                 from_b = 0 if same else g - 1
-                for e in range(w + 2):
-                    row = w * dest - 1 + e
-                    if row >= 0:
-                        table[dest, kind, self.a_line + e, from_a, 0, row] = 1
-                    row = 2 * self.side + w * dest - 1 + e
-                    if row < self.height:
-                        table[dest, kind, self.b_line + e, from_b, w - 1, row] = 1
+                for e in range(self.reach):
+                    for depth in range(2):
+                        spot = self.line[depth] + e
+                        row = w * dest - 2 + e
+                        if 0 <= row:
+                            table[0, dest, kind, spot, from_a, depth, row] = 1
+                        row = 2 * self.side + w * dest - 2 + e
+                        if row <= high:
+                            table[1, dest, kind, spot, from_b, w - 1 - depth, row] = 1
                 for e in range(w):
-                    table[dest, kind, self.a_row + e, from_a, e, self.height - 1] = 1
-                    table[dest, kind, self.b_row + e, from_b, e, 0] = 1
-        return jnp.asarray(table.reshape(t * k * c, g * w * n), BF16)
+                    for depth in range(2):
+                        spot = self.row[depth] + e
+                        if dest == 0:
+                            table[:, dest, kind, spot, from_b, e, depth] = 1
+                        if dest == t - 1:
+                            table[:, dest, kind, spot, from_a, e, high - depth] = 1
+        for stack in range(g):
+            for i, (col, row) in enumerate(((0, 0), (1, 0), (0, 1))):
+                poles[0, 3 * stack + i, stack, col, row] = 1
+                poles[1, 3 * stack + i, stack, w - 1 - col, high - row] = 1
+        return (
+            jnp.asarray(table.reshape(2, t * k * c, g * w * n), BF16),
+            jnp.asarray(poles.reshape(2, -1, g * w * n), BF16),
+        )
 
     def take_tables(self):
         t, c, w, n = self.tiles, self.cells, self.cols, self.lanes
-        from_a = np.zeros((t, c, 2 * n), np.float32)
-        from_b = np.zeros((t, c, 2 * n), np.float32)
-        for src in range(t):
-            for e in range(w):
-                from_a[src, self.a_row + e, 2 * self.side + src * w + e] = 1
-                from_b[src, self.b_row + e, src * w + e] = 1
-        for e in range(w + 2):
-            from_a[0, self.a_line + e, n + e] = 1
-            from_b[t - 1, self.b_line + e, n + e] = 1
-        shape = (t * c, 2 * n)
-        return jnp.asarray(from_a.reshape(shape), BF16), jnp.asarray(from_b.reshape(shape), BF16)
-
-
-def pack_blocks(plan, face, columns, table, blocks_ref):
-    t, c = plan.tiles, plan.cells
+        from_a = np.zeros((t, c, 4, n), np.float32)
+        from_b = np.zeros((t, c, 4, n), np.float32)
+        for depth in range(2):
+            for src in range(t):
+                for e in range(w):
+                    spot = self.row[depth] + e
+                    from_a[src, spot, depth, 2 * self.side + src * w + e] = 1
+                    from_b[src, spot, depth, src * w + e] = 1
+            for e in range(self.reach):
+                from_a[0, self.line[depth] + e, 2 + depth, e] = 1
+                from_b[t - 1, self.line[depth] + e, 2 + depth, 8 + e] = 1
+        ends = np.zeros((self.reach, n, n), np.float32)
+        for e in range(self.reach):
+            ends[e, 0, e] = 1
+            ends[e, self.height - 1, 8 + e] = 1
+        shape = (t * c, 4 * n)
+        return (
+            jnp.asarray(from_a.reshape(shape), BF16),
+            jnp.asarray(from_b.reshape(shape), BF16),
+            jnp.asarray(ends.reshape(-1, n), BF16),
+            jnp.asarray(np.eye(2 * self.poles, n), BF16),
+        )
+
+
+def first_kernel(plan, ids_ref, table_ref, poles_ref, columns_ref, blocks_ref):
+    t, c, g, w = plan.tiles, plan.cells, plan.stacks, plan.cols
+    face = ids_ref[1]
+    end = jnp.where(ids_ref[0] == plan.tiles - 1, 1, 0)
+    poles = []
     for k in range(2):
-        flat = jnp.concatenate([x for per in columns[k] for x in per], axis=1)
-        picked = lax.dot_general(
-            table, flat, (((1,), (1,)), ((), ())), preferred_element_type=F32
-        ).astype(BF16)
+        flat = jnp.concatenate([columns_ref[i, k, j] for j in range(g) for i in range(w)], axis=1)
+        picked = product(table_ref[end], flat, 1, 1).astype(BF16)
         picked = picked.reshape(t, plan.kinds, c, flat.shape[0])
         for dest in range(plan.faces):
             if plan.kinds == 2:
@@ -89,47 +126,288 @@
             else:
                 block = picked[:, 0]
             blocks_ref[:, dest, k * c : (k + 1) * c, :] = block
+        poles.append(product(poles_ref[end], flat, 1, 1))
+    poles = jnp.concatenate(poles, axis=0).astype(BF16)
+    for dest in range(plan.faces):
+        blocks_ref[:, dest, 2 * c :, :] = jnp.broadcast_to(poles[None], (t,) + poles.shape)
+
+
+def product(x, y, x_dim, y_dim):
+    return lax.dot_general(x, y, (((x_dim,), (y_dim,)), ((), ())), preferred_element_type=F32)
 
 
 def shift(x, by):
     return pltpu.roll(x, by % x.shape[1], 1)
 
 
-def halos(plan, ids_ref, k, left_ref, right_ref, cross_ref, got_ref, tab_a, tab_b):
+def surroundings(plan, ids_ref, k, columns_ref, near_l, near_r, wrap_ref, cross_ref, got_ref, tables):
+    w, n, c = plan.cols, plan.lanes, plan.cells
+    high, g_count = plan.height, plan.stacks
     first = ids_ref[0] == 0
     last = ids_ref[0] == plan.tiles - 1
     face = ids_ref[1]
     after = lax.rem(face + 1, plan.faces)
     before = lax.rem(face + plan.faces - 1, plan.faces)
-    c = plan.cells
-    result = []
-    for g in range(plan.stacks):
-        face_a = face if g < plan.stacks - 1 else after
+    across = lax.rem(face + 2 // g_count, plan.faces)
+    tab_a, tab_b, tab_ends, tab_eye = tables
+    pole_rows = [got_ref[at, across, 2 * c :, :] for at in (0, plan.tiles - 1)]
+    poles = product(jnp.concatenate(pole_rows, axis=0), tab_eye, 0, 0)
+    shape = (plan.channels, n)
+    lane = lax.broadcasted_iota(jnp.int32, shape, 1)
+    stacks = []
+    line, deep, ends = [jnp.zeros(shape, F32) for _ in range(3)]
+    for g in range(g_count):
+        face_a = face if g < g_count - 1 else after
         face_b = face if g > 0 else before
         seams = []
         for at, table in ((face_a, tab_a), (face_b, tab_b)):
             rows = got_ref[:, at, k * c : (k + 1) * c, :]
             rows = rows.reshape(plan.tiles * c, rows.shape[-1])
-            seams.append(
-                lax.dot_general(
-                    rows, table, (((0,), (0,)), ((), ())), preferred_element_type=F32
-                )
+            out = product(rows, table, 0, 0)
+            seams.append([out[:, i * n : (i + 1) * n] for i in range(4)])
+        line += shift(seams[0][2] + seams[1][2], 16 * g)
+        deep += shift(seams[0][3] + seams[1][3], 16 * g)
+        raw = [near_l[i, k, g] for i in range(2)]
+        raw += [columns_ref[i, k, g] for i in range(w)]
+        raw += [near_r[i, k, g] for i in range(2)]
+        ends += shift(product(jnp.concatenate(raw, axis=1), tab_ends, 1, 0), 16 * g)
+        end_l = [(wrap_ref[i, k, g - 1] if g > 0 else cross_ref[i, k]) for i in range(2)]
+        end_r = [(wrap_ref[i, k, g] if g < g_count - 1 else cross_ref[i, k]) for i in range(2)]
+        pole = []
+        for at in range(2):
+            base = at * plan.poles + k * (plan.poles // 2) + 3 * g
+            pole.append([poles[:, base + i : base + i + 1] for i in range(3)])
+        stacks.append(
+            dict(
+                raw=[x.astype(F32) for x in raw],
+                row_l=seams[1][:2],
+                row_r=seams[0][:2],
+                col_l=[shift(x.astype(F32), plan.side) for x in end_l],
+                col_r=[shift(x.astype(F32), -plan.side) for x in end_r],
+                north=pole[0],
+                south=pole[1],
             )
-        end_l = left_ref[k, g - 1] if g > 0 else cross_ref[k]
-        end_r = right_ref[k, g + 1] if g < plan.stacks - 1 else cross_ref[k]
-        n = plan.lanes
+        )
+    spot = lane % 8
+    ends = jnp.where(first & (spot < 2), 0.0, ends)
+    ends = jnp.where(last & (spot >= w + 2), 0.0, ends)
+    rim = dict(line=line, deep=deep, ends=ends, spot=spot, is_top=(lane % 16) < 8)
+    return stacks, rim, lane, first, last
+
+
+def rim_cell(plan, lane, g, bottom, e):
+    return lane == 16 * g + 8 * bottom + e
+
+
+def wide_forward(plan, found, taps_ref):
+    stacks, rim, lane, first, last = found
+    w, n, side, high, c = plan.cols, plan.lanes, plan.side, plan.height, plan.channels
+
+    def put(a, b, segment, value):
+        row = (a * 3 + b) * c
+        taps_ref[row : row + c, segment * n : (segment + 1) * n] = value.astype(BF16)
+
+    rows_r = (lane >= 2 * side) & (lane < high)
+    for g, h in enumerate(stacks):
+        raw = h["raw"]
+        x = []
+        for q in range(w + 4):
+            at = 16 * g + q
+            y = jnp.where(lane == high, rim["line"][:, at + 8 : at + 9], raw[q])
+            x.append(jnp.where(lane == n - 1, rim["line"][:, at : at + 1], y))
+        edge_l = jnp.where(lane < side, h["row_l"][0], jnp.where(lane < high, h["col_l"][1], 0.0))
+        edge_r = jnp.where(lane < 2 * side, h["col_r"][0], jnp.where(rows_r, h["row_r"][0], 0.0))
+        x[0] = jnp.where(first, h["col_l"][0], x[0])
+        x[1] = jnp.where(first, edge_l, x[1])
+        x[w + 2] = jnp.where(last, edge_r, x[w + 2])
+        x[w + 3] = jnp.where(last, h["col_r"][1], x[w + 3])
+        moved = [[shift(y, 1 - b) if b != 1 else y for b in range(3)] for y in x]
+        own0, own1, own30, own31 = raw[2], raw[3], raw[w], raw[w + 1]
+        north, south = h["north"], h["south"]
+        turned_l = [jnp.where(lane < side, own0, 0.0)]
+        turned_r = []
+        for d in range(2):
+            y = jnp.where(lane < side, h["row_l"][d], shift(own0, -d))
+            turned_l.append(jnp.where(lane == n - 1, north[d], y))
+            y = jnp.where(rows_r, h["row_r"][d], shift(own31, d))
+            turned_r.append(jnp.where(lane == high, south[d], y))
+        turned_l[1:] = [
+            jnp.where((lane > side) & (lane < n - 1), 0.0, y) for y in turned_l[1:]
+        ]
+        turned_r = [turned_r[1], turned_r[0], jnp.where(rows_r, own31, 0.0)]
+        for b in range(3):
+            for a in range(3):
+                for j in range(1, w + 1):
+                    put(a, b, plan.segment(g, j), moved[j + a][b])
+                y = shift(h["col_l"][1], 1 - b) if a == 1 else moved[a][b]
+                y = jnp.where(lane < side, shift(turned_l[b], 1 - a), y)
+                if b == 0:
+                    over = shift(own0, 2 - a) if a < 2 else 0.0
+                    y = jnp.where(lane == side, over, y)
+                elif a == 2:
+                    y = jnp.where(lane == high, shift((own0, own1)[b - 1], 1), y)
+                    if b == 2:
+                        y = jnp.where(lane == high - 1, own0, y)
+                put(a, b, plan.segment(g, 0), jnp.where(first, y, moved[a][b]))
+                y = shift(h["col_r"][0], 1 - b) if a == 1 else moved[w + 1 + a][b]
+                y = jnp.where(rows_r, shift(turned_r[b], 1 - a), y)
+                if b == 2:
+                    over = shift(own31, -a) if a > 0 else 0.0
+                    y = jnp.where(lane == 2 * side - 1, over, y)
+                if a == 0:
+                    if b == 0:
+                        y = jnp.where(lane == 0, own31, y)
+                    y = jnp.where(lane == n - 1, shift(own30 if b == 0 else own31, -1), y)
+                put(a, b, plan.segment(g, w + 1), jnp.where(last, y, moved[w + 1 + a][b]))
+    line, deep, ends = rim["line"], rim["deep"], rim["ends"]
+    is_top, spot = rim["is_top"], rim["spot"]
+    ends = jnp.where(last & is_top & (spot == w + 2), shift(ends, 1), ends)
+    ends = jnp.where(first & jnp.logical_not(is_top) & (spot == 1), shift(ends, -1), ends)
+    for g, h in enumerate(stacks):
+        north = first & rim_cell(plan, lane, g, 0, 1)
+        south = last & rim_cell(plan, lane, g, 1, w + 2)
+        line = jnp.where(north, h["north"][0], line)
+        deep = jnp.where(north, h["north"][2], deep)
+        line = jnp.where(south, h["south"][0], line)
+        deep = jnp.where(south, h["south"][2], deep)
+    by_a = (jnp.where(is_top, ends, deep), line, jnp.where(is_top, deep, ends))
+    for a in range(3):
+        for b in range(3):
+            put(a, b, plan.segments - 1, shift(by_a[a], -b) if b else by_a[a])
+
+
+def wide_backward(plan, found, taps_ref):
+    stacks, rim, lane, first, last = found
+    w, n, side, high, c = plan.cols, plan.lanes, plan.side, plan.height, plan.channels
+
+    def put(row, segment, value):
+        taps_ref[row * c : (row + 1) * c, segment * n : (segment + 1) * n] = value.astype(BF16)
+
+    zero = jnp.zeros(lane.shape, F32)
+    rows_l = lane < side
+    rows_r = (lane >= 2 * side) & (lane < high)
+    for g, h in enumerate(stacks):
+        raw = h["raw"]
+        z = list(raw)
+        edge_l = jnp.where((lane >= side) & (lane <= high), h["col_l"][1], 0.0)
+        edge_r = jnp.where((lane < 2 * side) | (lane == n - 1), h["col_r"][0], 0.0)
+        z[1] = jnp.where(first, edge_l, z[1])
+        z[w + 2] = jnp.where(last, edge_r, z[w + 2])
+        moved = [[shift(y, b - 1) if b != 1 else y for b in range(3)] for y in z]
+        keep_l = (lane >= side) | jnp.logical_not(first)
+        keep_r = (lane < 2 * side) | jnp.logical_not(last)
+        own0, own1, own30, own31 = raw[2], raw[3], raw[w], raw[w + 1]
+        north, south = h["north"], h["south"]
+        line_l = [jnp.where(rows_l, y, 0.0) for y in h["row_l"]]
+        line_r = [jnp.where(rows_r, y, 0.0) for y in h["row_r"]]
+        line_l = [line_l[1], line_l[0], zero]
+        line_r = [zero, line_r[0], line_r[1]]
+        keep = (lane >= side) & (lane <= high + 1)
+        deep_l = [zero] + [jnp.where(keep, h["col_l"][i], 0.0) for i in (1, 0)]
+        keep = (lane < 2 * side) | (lane >= n - 2)
+        deep_r = [jnp.where(keep, h["col_r"][i], 0.0) for i in (1, 0)] + [zero]
+        for b in range(3):
+            for a in range(3):
+                tap = a * 3 + b
+                for j in range(1, w + 1):
+                    y = moved[j + 2 - a][b]
+                    if j == 1 and a == 2:
+                        y = jnp.where(keep_l, y, 0.0)
+                    if j == w and a == 0:
+                        y = jnp.where(keep_r, y, 0.0)
+                    put(tap, plan.segment(g, j), y)
+                y = jnp.where(rows_l, shift(line_l[b], a - 1), shift(deep_l[a], b - 1))
+                if a == 0:
+                    y = jnp.where(lane == side - 1, shift(own0, b - 2), y)
+                    y = jnp.where(lane == side, shift(own0, b), y)
+                put(tap, plan.segment(g, 0), jnp.where(first, y, moved[2 - a][b]))
+                y = jnp.where(rows_r, shift(line_r[b], a - 1), shift(deep_r[a], b - 1))
+                if a == 2:
+                    y = jnp.where(lane == 2 * side - 1, shift(own31, b - 2), y)
+                    y = jnp.where(lane == 2 * side, shift(own31, b), y)
+                put(tap, plan.segment(g, w + 1), jnp.where(last, y, moved[w + 3 - a][b]))
+        for j in range(w + 2):
+            segment = plan.segment(g, j)
+            for b in range(3):
+                at = 16 * g + j + 2 - b
+                top = jnp.where(lane == 0, rim["line"][:, at : at + 1], 0.0)
+                bottom = jnp.where(lane == high - 1, rim["line"][:, at + 8 : at + 9], 0.0)
+                left = right = zero
+                if j == 0:
+                    own = jnp.where(lane < high, shift(own0, b - 1), 0.0)
+                    top = jnp.where(first, own, top)
+                    bottom = jnp.where(first, 0.0, bottom)
+                    if b < 2:
+                        left = jnp.where(first & (lane == 0), north[1 - b], 0.0)
+                        right = jnp.where(first & (lane == high), shift((own1, own0)[b], 1), 0.0)
+                if j == 1:
+                    left = jnp.where(first & rows_l, shift(line_l[1], b - 1), 0.0)
+                if j == w:
+                    right = jnp.where(last & rows_r, shift(line_r[1], b - 1), 0.0)
+                if j == w + 1:
+                    own = jnp.where(lane < high, shift(own31, b - 1), 0.0)
+                    bottom = jnp.where(last, own, bottom)
+                    top = jnp.where(last, 0.0, top)
+                    if b > 0:
+                        over = shift((own31, own30)[b - 1], -1)
+                        left = jnp.where(last & (lane == n - 1), over, 0.0)
+                        right = jnp.where(last & (lane == high - 1), south[b - 1], 0.0)
+                for i, y in enumerate((top, bottom, left, right)):
+                    put(9 + 3 * i + b, segment, y)
+    line, deep, ends = rim["line"], rim["deep"], rim["ends"]
+    is_top = rim["is_top"]
+    tops = [jnp.where(is_top, y, 0.0) for y in (deep, ends)]
+    bottoms = [jnp.where(is_top, 0.0, y) for y in (deep, ends)]
+    by_a = (tops[0], line, bottoms[0])
+    segment = plan.segments - 1
+    for b in range(3):
+        for a in range(3):
+            put(a * 3 + b, segment, shift(by_a[a], b - 2))
+        top = bottom = zero
+        for g, h in enumerate(stacks):
+            if b < 2:
+                over = h["north"][2 * (1 - b)]
+                top = jnp.where(first & rim_cell(plan, lane, g, 0, 1), over, top)
+            if b > 0:
+                over = h["south"][2 * (b - 1)]
+                bottom = jnp.where(last & rim_cell(plan, lane, g, 1, w), over, bottom)
+        put(9 + b, segment, top)
+        put(12 + b, segment, bottom)
+        put(15 + b, segment, shift(tops[1], b - 2))
+        put(18 + b, segment, shift(bottoms[1], b - 2))
+
+
+def second_halos(plan, ids_ref, ref):
+    w, n, high, side = plan.cols, plan.lanes, plan.height, plan.side
+    first = ids_ref[0] == 0
+    last = ids_ref[0] == plan.tiles - 1
+    start = (plan.segments - 1) * n
+    rim = ref[:, start : start + n].astype(F32)
+    lane = lax.broadcasted_iota(jnp.int32, rim.shape, 1)
+    result = []
+    for g in range(plan.stacks):
+        left, right = [
+            ref[:, plan.segment(g, j) * n : (plan.segment(g, j) + 1) * n].astype(F32)
+            for j in (0, w + 1)
+        ]
+        top = [rim[:, 16 * g + e : 16 * g + e + 1] for e in range(w + 2)]
+        bottom = [rim[:, 16 * g + 8 + e : 16 * g + 9 + e] for e in range(w + 2)]
+        top[0] = jnp.where(first, 0.0, top[0])
+        bottom[0] = jnp.where(first, left[:, high - 1 : high], bottom[0])
+        top[w + 1] = jnp.where(last, right[:, 0:1], top[w + 1])
+        bottom[w + 1] = jnp.where(last, 0.0, bottom[w + 1])
         result.append(
             dict(
                 first=first,
                 last=last,
-                left=left_ref[k, g].astype(F32),
-                right=right_ref[k, g].astype(F32),
-                row_l=seams[1][:, :n],
-                row_r=seams[0][:, :n],
-                col_l=shift(end_l.astype(F32), plan.side),
-                col_r=shift(end_r.astype(F32), -plan.side),
-                top=[seams[0][:, n + e : n + e + 1] for e in range(plan.cols + 2)],
-                bottom=[seams[1][:, n + e : n + e + 1] for e in range(plan.cols + 2)],
+                left=left,
+                right=right,
+                row_l=jnp.where(lane < side, left, 0.0),
+                row_r=jnp.where((lane >= 2 * side) & (lane < high), right, 0.0),
+                col_l=left,
+                col_r=right,
+                top=top,
+                bottom=bottom,
             )
         )
     return result
@@ -210,65 +488,45 @@
                 taps_ref[(18 + b) * c : (19 + b) * c, at : at + n] = y
 
 
-def own_columns(plan, refs, k):
+def own_columns(plan, ref):
+    w, n = plan.cols, plan.lanes
     return [
-        [refs[w][k, g].astype(F32) for w in range(plan.cols)] for g in range(plan.stacks)
+        [ref[:, (g * w + i) * n : (g * w + i + 1) * n].astype(F32) for i in range(w)]
+        for g in range(plan.stacks)
     ]
-
-
-def first_kernel(plan, ids_ref, table_ref, *refs):
-    columns = refs[: plan.cols]
-    blocks_ref = refs[plan.cols]
-    parts = [
-        [[columns[w][k, g] for w in range(plan.cols)] for g in range(plan.stacks)]
-        for k in range(2)
-    ]
-    pack_blocks(plan, ids_ref[1], parts, table_ref[...], blocks_ref)
 
 
 def middle_kernel(plan, ids_ref, *refs):
     w, n, g_count, c = plan.cols, plan.lanes, plan.stacks, plan.channels
-    columns, refs = refs[:w], refs[w:]
-    left, right, cross, got, table, tab_a, tab_b, w_one, w_two = refs[:9]
-    refs = refs[9:]
-    new_columns, refs = refs[:w], refs[w:]
-    blocks_ref, mine_ref, theirs_ref, fwd_ref, bwd_ref, sums_ref = refs
-    tab_a, tab_b = tab_a[...], tab_b[...]
-    halo = halos(plan, ids_ref, 0, left, right, cross, got, tab_a, tab_b)
-    forward_operand(plan, own_columns(plan, columns, 0), halo, fwd_ref)
-    halo = halos(plan, ids_ref, 1, left, right, cross, got, tab_a, tab_b)
-    upstream = own_columns(plan, columns, 1)
-    backward_operand(plan, upstream, halo, bwd_ref)
+    around, tables, (w_one, w_two), refs = refs[:6], refs[6:10], refs[10:12], refs[12:]
+    hidden_ref, pre_grad_ref, mine_ref, theirs_ref, fwd_ref, bwd_ref, sums_ref = refs
+    tables = [x[...] for x in tables]
+    wide_forward(plan, surroundings(plan, ids_ref, 0, *around, tables), fwd_ref)
+    wide_backward(plan, surroundings(plan, ids_ref, 1, *around, tables), bwd_ref)
     pre = jnp.dot(w_one[...], fwd_ref[...], preferred_element_type=F32)
     grad = jnp.dot(w_two[...], bwd_ref[...], preferred_element_type=F32)
-    lane = lax.broadcasted_iota(jnp.int32, pre.shape, 1) % n
-    inside = lane < plan.height
     bend = jnp.tanh(GELU_A * (pre + GELU_B * (pre * pre * pre)))
     half = 0.5 * (1.0 + bend)
     slope = half + 0.5 * pre * (1.0 - bend * bend) * (
         GELU_A * (1.0 + (3.0 * GELU_B) * (pre * pre))
     )
+    first = ids_ref[0] == 0
+    last = ids_ref[0] == plan.tiles - 1
+    flat = lax.broadcasted_iota(jnp.int32, pre.shape, 1)
+    segment, lane = flat // n, flat % n
+    own_end = g_count * w
+    left = (segment >= own_end) & ((segment - own_end) % 2 == 0)
+    right = (segment >= own_end) & ((segment - own_end) % 2 == 1)
+    inside = (lane < plan.height) | (segment == plan.segments - 1)
+    inside = inside | (left & first & (lane == plan.height))
+    inside = inside | (right & last & (lane == n - 1))
     hidden = jnp.where(inside, pre * half, 0.0).astype(BF16)
     pre_grad = jnp.where(inside, grad * slope, 0.0).astype(BF16)
-    both = (hidden, pre_grad)
-    parts = [
-        [[both[k][:, (g * w + i) * n : (g * w + i + 1) * n] for i in range(w)] for g in range(g_count)]
-        for k in range(2)
-    ]
-    for k in range(2):
-        for g in range(g_count):
-            for i in range(w):
-                new_columns[i][k, g] = parts[k][g][i]
-    pack_blocks(plan, ids_ref[1], parts, table[...], blocks_ref)
-    own = plan.own
-    half_at = ids_ref[2]
-    cot = pre_grad
-    terms = lax.dot_general(
-        fwd_ref[...], cot, (((1,), (1,)), ((), ())), preferred_element_type=F32
-    )
-    turned = lax.dot_general(
-        bwd_ref[...], hidden, (((1,), (1,)), ((), ())), preferred_element_type=F32
-    )
+    hidden_ref[...] = hidden
+    pre_grad_ref[...] = pre_grad
+    own_end *= n
+    terms = product(fwd_ref[:, :own_end], pre_grad[:, :own_end], 1, 1)
+    turned = product(bwd_ref[:, :own_end], hidden[:, :own_end], 1, 1)
     tap = [turned[i * c : (i + 1) * c] for i in range(21)]
     for b in range(3):
         tap[b] = tap[b] + tap[9 + b]
@@ -291,15 +549,13 @@
             ref[d] = rows.astype(ref.dtype)
 
 
-def last_kernel(plan, ids_ref, *refs):
+def last_kernel(plan, ids_ref, hidden_ref, pre_grad_ref, w_two, w_one, *refs):
+    out_ref, back_ref, fwd_ref, bwd_ref = refs
     w, n = plan.cols, plan.lanes
-    columns, refs = refs[:w], refs[w:]
-    left, right, cross, got, tab_a, tab_b, w_two, w_one, out_ref, back_ref, fwd_ref, bwd_ref = refs
-    tab_a, tab_b = tab_a[...], tab_b[...]
-    halo = halos(plan, ids_ref, 0, left, right, cross, got, tab_a, tab_b)
-    forward_operand(plan, own_columns(plan, columns, 0), halo, fwd_ref)
-    halo = halos(plan, ids_ref, 1, left, right, cross, got, tab_a, tab_b)
-    backward_operand(plan, own_columns(plan, columns, 1), halo, bwd_ref)
+    halo = second_halos(plan, ids_ref, hidden_ref)
+    forward_operand(plan, own_columns(plan, hidden_ref), halo, fwd_ref)
+    halo = second_halos(plan, ids_ref, pre_grad_ref)
+    backward_operand(plan, own_columns(plan, pre_grad_ref), halo, bwd_ref)
     out = jnp.dot(w_two[...], fwd_ref[...], preferred_element_type=F32).astype(BF16)
     back = jnp.dot(w_one[...], bwd_ref[...], preferred_element_type=F32).astype(BF16)
     for g in range(plan.stacks):
@@ -334,30 +590,31 @@
 
 
 def tile_ring(plan, x, step):
-    count = plan.tiles
-    pairs = [(i, (i + step) % count) for i in range(count)]
-    if plan.stacks == 1:
-        pairs = [(i, j) for i, j in pairs if j == i + step]
+    pairs = [(i, i + step) for i in range(plan.tiles) if 0 <= i + step < plan.tiles]
     return lax.ppermute(x, "tile", pairs)
 
 
 def swap_ends(plan, columns):
-    t, f = plan.tiles, plan.faces
+    t, f, g = plan.tiles, plan.faces, plan.stacks
     first = lax.axis_index("tile") == 0
-    sent = jnp.where(first, columns[0][:, 0], columns[-1][:, plan.stacks - 1])
+    head, tail = columns[:2], columns[plan.cols - 2 :]
     pairs = [((t - 1) * f + i, (i + 1) % f) for i in range(f)]
     pairs += [((i + 1) % f, (t - 1) * f + i) for i in range(f)]
-    return lax.ppermute(sent, BOTH, pairs)
+    cross = lax.ppermute(jnp.where(first, head[:, :, 0], tail[:, :, g - 1]), BOTH, pairs)
+    if g == 1:
+        return cross[:, :, None], cross
+    sent = jnp.where(first, head[:, :, 1:], tail[:, :, : g - 1])
+    return lax.ppermute(sent, "tile", [(0, t - 1), (t - 1, 0)]), cross
 
 
 def exchange(plan, columns, blocks):
-    left = tile_ring(plan, columns[-1], 1)
-    right = tile_ring(plan, columns[0], -1)
-    cross = swap_ends(plan, columns)
+    left = tile_ring(plan, columns[plan.cols - 2 :], 1)
+    right = tile_ring(plan, columns[:2], -1)
+    wrap, cross = swap_ends(plan, columns)
     count = plan.tiles * plan.faces
     flat = blocks.reshape((count,) + blocks.shape[2:])
     got = lax.all_to_all(flat, BOTH, 0, 0, tiled=True).reshape(blocks.shape)
-    return left, right, cross, got
+    return left, right, wrap, cross, got
 
 
 def swapped(plan, x, near=0, mid=0, far=0):
@@ -406,16 +663,14 @@
         fields = lax.all_gather(fields, "sub", axis=0, tiled=True)
         upstream = lax.all_gather(upstream, "sub", axis=0, tiled=True)
 
-    def column(at):
-        both = jnp.stack([fields[:, :, at], upstream[:, :, at]])
-        return jnp.pad(both.transpose(0, 2, 1, 3), ((0, 0), (0, 0), (0, 0), (0, n - h)))
-
-    columns = [column(i) for i in range(w)]
-    table = plan.send_table()
-    tab_a, tab_b = plan.take_tables()
-    blocks_shape = jax.ShapeDtypeStruct((plan.tiles, plan.faces, 2 * plan.cells, c), BF16)
+    both = jnp.stack([fields, upstream]).transpose(3, 0, 2, 1, 4)
+    columns = jnp.pad(both, ((0, 0),) * 4 + ((0, n - h),))
+    blocks_shape = jax.ShapeDtypeStruct((plan.tiles, plan.faces, plan.block, c), BF16)
     (blocks,) = call(
-        functools.partial(first_kernel, plan), ids, [table] + columns, [blocks_shape]
+        functools.partial(first_kernel, plan),
+        ids,
+        [*plan.send_tables(), columns],
+        [blocks_shape],
     )
     halo = exchange(plan, columns, blocks)
 
@@ -426,31 +681,28 @@
     bwd_one = lax.dynamic_slice_in_dim(kernel_one, sub * own, own, 2)
     bwd_one = seam_weights(bwd_one.transpose(2, 0, 1, 3))
 
-    taps = [
-        pltpu.VMEM((9 * c, g * w * n), BF16),
-        pltpu.VMEM((21 * c, g * w * n), BF16),
-    ]
-    column_shape = jax.ShapeDtypeStruct((2, g, c, n), BF16)
+    def taps(width):
+        return [pltpu.VMEM((9 * c, width), BF16), pltpu.VMEM((21 * c, width), BF16)]
+
     piece = (plan.mid, plan.piece, c)
     rows = plan.near * plan.mid * plan.piece
-    results = call(
+    wide = plan.segments * n
+    hidden, pre_grad, mine, theirs = call(
         functools.partial(middle_kernel, plan),
         ids,
-        columns + list(halo) + [table, tab_a, tab_b, fwd_one, bwd_two],
-        [column_shape] * w
-        + [blocks_shape, jax.ShapeDtypeStruct(piece, F32), jax.ShapeDtypeStruct(piece, BF16)],
-        taps + [pltpu.VMEM((rows, c), F32)],
+        [columns, *halo, *plan.take_tables(), fwd_one, bwd_two],
+        [jax.ShapeDtypeStruct((c, wide), BF16)] * 2
+        + [jax.ShapeDtypeStruct(piece, F32), jax.ShapeDtypeStruct(piece, BF16)],
+        taps(wide) + [pltpu.VMEM((rows, c), F32)],
     )
-    columns, (blocks, mine, theirs) = list(results[:w]), results[w:]
-    halo = exchange(plan, columns, blocks)
     mine, theirs = sum_all(plan, mine, theirs)
     out_shape = jax.ShapeDtypeStruct((g, w, own, h), BF16)
     result, fields_grad = call(
         functools.partial(last_kernel, plan),
         ids,
-        columns + list(halo) + [tab_a, tab_b, fwd_two, bwd_one],
+        [hidden, pre_grad, fwd_two, bwd_one],
         [out_shape, out_shape],
-        taps,
+        taps(g * w * n),
     )
     scale = 1.0 / (plan.side * 12.0**0.5)
     (sums,) = call(

time: 72.3 us -> 69.1 us (0.956)
  starting transfers between devices: 37.5 us -> 34 us
  waiting for transfers between devices: 16.5 us -> 13.1 us
  Pallas kernels: 7.22 us -> 9.23 us
  local copies, waits for them, and re-layouts: 9.36 us -> 10.3 us
    all_to_all x2 -> x1, waiting for transfers between devices: 7.35 us -> 0.01 us  [exchange(): got = lax.all_to_all(flat, BOTH, 0, 0, tiled=True).reshape(blocks.shape)]
    ppermute x4 -> x2, starting transfers between devices: 10.1 us -> 3.66 us  [tile_ring(): return lax.ppermute(x, 'tile', pairs)]
    ppermute x11, waiting for transfers between devices: 7.56 us -> 10.8 us  [swapped(): return lax.ppermute(x, BOTH, pairs)]
    all_to_all x2 -> x1, starting transfers between devices: 7.14 us -> 9.2 us  [exchange(): got = lax.all_to_all(flat, BOTH, 0, 0, tiled=True).reshape(blocks.shape)]
    pallas_call x4, Pallas kernels: 7.22 us -> 9.23 us  [call(): pl.pallas_call(body, out_shape=outs, in_specs=[SMEM] + [VMEM] * len(input...]
    slice x2 -> x0, local copies, waits for them, and re-layouts: 1.29 us -> none  [column(): both = jnp.stack([fields[:, :, at], upstream[:, :, at]])]
    another operation x2 -> x1, local copies, waits for them, and re-layouts: 0.04 us -> 1.06 us  [on_device(): both = jnp.stack([fields, upstream]).transpose(3, 0, 2, 1, 4)]
    ppermute x2, local copies, waits for them, and re-layouts: 0.02 us -> 1.02 us  [tile_ring(): return lax.ppermute(x, 'tile', pairs)]
  transfers between devices with their start and end apart: 19 -> 16, of which waited for: 7 -> 9; matrix products, arithmetic and copies ran while one was open for 9% -> 11% of each run, Pallas kernels for 5% -> 5%
where the time goes in v1:
time: 69.1 us; the launch traced here: 68.6 us
  starting transfers between devices  34 us (49%)
  waiting for transfers between devices  13.1 us (19%)
  local copies, waits for them, and re-layouts  10.3 us (15%)
  Pallas kernels  9.23 us (13%)
  between operations  1.05 us (2%)
  other arithmetic  0.94 us (1%)
    ppermute x11, starting transfers between devices, swapped(): return lax.ppermute(x, BOTH, pairs)  11.7 us
    ppermute x11, waiting for transfers between devices, swapped(): return lax.ppermute(x, BOTH, pairs)  10.8 us
    pallas_call x4, Pallas kernels, call(): pl.pallas_call(body, out_shape=outs, in_specs=[SMEM] + [VMEM] * len(input...  9.23 us
    all_to_all x1, starting transfers between devices, exchange(): got = lax.all_to_all(flat, BOTH, 0, 0, tiled=True).reshape(blocks.shape)  9.2 us
    ppermute x1, starting transfers between devices, swap_ends(): return (lax.ppermute(sent, 'tile', [(0, t - 1), (t - 1, 0)]), cross)  6.2 us
    ppermute x2, starting transfers between devices, tile_ring(): return lax.ppermute(x, 'tile', pairs)  3.66 us
    ppermute x1, starting transfers between devices, swap_ends(): lax.ppermute(jnp.where(first, head[:, :, 0], tail[:, :, g - 1]), BOTH, pa...  3.25 us
    concatenate x2, local copies, waits for them, and re-layouts, seam_weights(): return jnp.concatenate(lines, axis=1).reshape(kernel.shape[0], -1)  2.7 us
  transfers between devices with their start and end apart: 16, of which 9 were waited for; matrix products, arithmetic and copies ran while one was open for 11% of the time, Pallas kernels for 5%

profile of v1, /device:TPU:0, one launch (start us, length us, event | category | flops | bytes accessed | tf_op | source)
XLA Modules:
  0.0 68.6 jit_solution(9497121149513142167)
XLA Ops:
  0.6 0.0 copy-start
  0.6 1.1 %copy_bitcast_fusion = (bf16[1,96,2,2,96]{4,1,0,3,2:T(8,128)(2,1)S(1)}, bf16[1,96,2,2,96]{4,1,0,3,2:T(8,128)(2,1)S(1)}) fusion(bf16[96,2,2,96]{3,2,1,0:T(2,128)(2,1)} %param.11, bf16[96,2,2,96]{3,2,1,0:T(2,128)(2,1)} %param.10), kind=kLoop, calls=%fused_computation.8 | loop fusion | bytes 294912 | tf_op jit(solution)/shard_map/stack | solution.py:666
  1.8 2.4 %collective-permute-start = (bf16[2,2,2,96,128]{4,3,1,0,2:T(8,128)(2,1)S(1)}, bf16[2,2,2,96,128]{4,3,1,0,2:T(8,128)(2,1)S(1)}, u32[]{:S(2)}, u32[]{:S(2)}) collective-permute-start(bf16[2,2,2,96,128]{4,3,1,0,2:T(8,128)(2,1)S(1)} %pad.4), channel_id=1, source_target_pairs={{0,2},{2,4},{4,6},{6,8},{8,10},{10,12},{12,14},{14,16},{16,18},{18... | collective-permute-start | bytes 589832 | tf_op jit(solution)/shard_map/ppermute | solution.py:594
  4.2 1.3 %collective-permute-start.1 = (bf16[2,2,2,96,128]{4,3,1,0,2:T(8,128)(2,1)S(1)}, bf16[2,2,2,96,128]{4,3,1,0,2:T(8,128)(2,1)}, u32[]{:S(2)}, u32[]{:S(2)}) collective-permute-start(bf16[2,2,2,96,128]{4,3,1,0,2:T(8,128)(2,1)S(1)} %pad.4), channel_id=1, source_target_pairs={{2,0},{4,2},{6,4},{8,6},{10,8},{12,10},{14,12},{16,14},{18,16},{20... | collective-permute-start | bytes 589832 | tf_op jit(solution)/shard_map/ppermute | solution.py:594
  5.5 0.0 copy-start.4
  5.5 0.1 stack.44.ids_ref
  5.6 0.6 copy-done.4
  6.2 1.8 %shard_map.129 = bf16[16,2,48,96]{3,2,1,0:T(8,128)(2,1)} custom-call(s32[5]{0:T(128)S(1)} %stack.44.ids_ref, bf16[2,512,512]{2,1,0:T(8,128)(2,1)S(1)} %copy-done, bf16[2,8,512]{2,1,0:T(8,128)(2,1)S(1)} %copy-done.4, bf16[2,2,2,96,128]{4,3,2,1,0:T(8,128)(2,1)S(1)} %copy.43.columns_ref.refs_0_), custom_call_target="tpu_custom_call" | custom-call | tf_op jit(solution)/shard_map/pallas_call | solution.py:582
  8.0 9.2 %all-to-all-start = ((bf16[32,48,96]{2,1,0:T(8,128)(2,1)}), bf16[32,48,96]{2,1,0:T(8,128)(2,1)S(1)}, u32[]{:S(2)}, u32[]{:S(2)}) async-start(bf16[32,48,96]{2,1,0:T(8,128)(2,1)} %bitcast.9), calls=%async_computation | async-start | bytes 786432 | tf_op jit(solution)/shard_map/all_to_all | solution.py:616
  17.2 0.0 copy-start.7
  17.2 0.7 %select_bitcast_fusion = (bf16[2,2,96,128]{3,2,1,0:T(8,128)(2,1)S(1)}, bf16[2,2,1,96,128]{4,3,1,0,2:T(8,128)(2,1)}) fusion(pred[]{:T(512)S(6)} %eq.3, bf16[2,2,2,96,96]{4,3,1,0,2:T(8,128)(2,1)S(1)} %maximum_bitcast_fusion), kind=kLoop, calls=%fused_computation.10 | loop fusion | flops 98304 | bytes 344065 | tf_op jit(solution)/shard_map/jit(_where)/select_n | solution.py:603
  17.9 6.2 %collective-permute-start.2 = (bf16[2,2,1,96,128]{4,3,1,0,2:T(8,128)(2,1)}, bf16[2,2,1,96,128]{4,3,1,0,2:T(8,128)(2,1)S(1)}, u32[]{:S(2)}, u32[]{:S(2)}) collective-permute-start(bf16[2,2,1,96,128]{4,3,1,0,2:T(8,128)(2,1)} %get-tuple-element.40), channel_id=1, source_target_pairs={{0,30},{30,0},{1,31},{31,1}} | collective-permute-start | bytes 294920 | tf_op jit(solution)/shard_map/ppermute | solution.py:607
  24.1 3.2 %collective-permute-start.3 = (bf16[2,2,96,128]{3,2,1,0:T(8,128)(2,1)S(1)}, bf16[2,2,96,128]{3,2,1,0:T(8,128)(2,1)S(1)}, u32[]{:S(2)}, u32[]{:S(2)}) collective-permute-start(bf16[2,2,96,128]{3,2,1,0:T(8,128)(2,1)S(1)} %get-tuple-element.39), channel_id=1, source_target_pairs={{30,1},{31,0},{1,30},{0,31}} | collective-permute-start | bytes 294920 | tf_op jit(solution)/shard_map/ppermute | solution.py:603
  27.4 0.1 copy.39
  27.5 0.1 copy.40
  27.5 0.1 copy.41
  27.6 0.1 copy.42
  27.7 0.1 copy.38
  27.8 1.4 %concatenate.6 = bf16[96,21,96]{2,1,0:T(8,128)(2,1)S(1)} concatenate(bf16[96,9,96]{2,1,0:T(8,128)(2,1)S(1)} %copy.38, bf16[96,3,96]{2,1,0:T(4,128)(2,1)S(1)} %copy.39, bf16[96,3,96]{2,1,0:T(4,128)(2,1)S(1)} %copy.40, bf16[96,3,96]{2,1,0:T(4,128)(2,1)S(1)} %copy.41, bf16[96,3,96]{2,1,0:T(4,128)(2,1)S(1)} %copy.42), dimensions={1} | concatenate | bytes 774144 | tf_op jit(solution)/shard_map/concatenate | solution.py:651
  29.1 0.0 copy-start.6
  29.2 0.4 reshape.44.refs_11_
  29.6 0.5 copy-done.6
  30.1 0.2 copy.47.refs_10_
  30.2 0.0 copy-start.2
  30.3 0.0 copy-start.3
  30.3 0.0 copy-start.1
  30.3 0.0 collective-permute-done.1
  30.3 0.0 copy-start.5
  30.3 1.0 %copy.45.refs_2_ = bf16[2,2,2,96,128]{4,3,2,1,0:T(8,128)(2,1)S(1)} copy(bf16[2,2,2,96,128]{4,3,1,0,2:T(8,128)(2,1)} %collective-permute-done.1) | data formatting | bytes 393216 | tf_op jit(solution)/shard_map/ppermute | solution.py:594
  31.4 2.3 %collective-permute-done.3.refs_4_ = bf16[2,2,96,128]{3,2,1,0:T(8,128)(2,1)S(1)} collective-permute-done((bf16[2,2,96,128]{3,2,1,0:T(8,128)(2,1)S(1)}, bf16[2,2,96,128]{3,2,1,0:T(8,128)(2,1)S(1)}, u32[]{:S(2)}, u32[]{:S(2)}) %collective-permute-start.3) | collective-permute-done | bytes 98336 | tf_op jit(solution)/shard_map/ppermute | solution.py:603
  33.6 0.0 all-to-all-done
  33.7 5.0 %shard_map.130 = (bf16[96,1152]{1,0:T(8,128)(2,1)S(1)}, bf16[96,1152]{1,0:T(8,128)(2,1)S(1)}, f32[4,224,96]{2,1,0:T(8,128)S(1)}, bf16[4,224,96]{2,1,0:T(8,128)(2,1)S(1)}) custom-call(s32[5]{0:T(128)S(1)} %stack.44.ids_ref, bf16[2,2,2,96,128]{4,3,2,1,0:T(8,128)(2,1)S(1)} %copy.43.columns_ref.refs_0_, bf16[2,2,2,96,128]{4,3,2,1,0:T(8,128)(2,1)S(1)} %copy.44.refs_1_, ...), custom_call_target="tpu_custom_call" | custom-call | tf_op jit(solution)/shard_map/pallas_call | solution.py:582
  38.6 0.1 collective-permute-start.4
  38.7 1.5 %collective-permute-done.4 = bf16[4,224,96]{2,1,0:T(8,128)(2,1)S(1)} collective-permute-done((bf16[4,224,96]{2,1,0:T(8,128)(2,1)S(1)}, bf16[4,224,96]{2,1,0:T(8,128)(2,1)S(1)}, u32[]{:S(2)}, u32[]{:S(2)}) %collective-permute-start.4) | collective-permute-done | bytes 172064 | tf_op jit(solution)/shard_map/ppermute | solution.py:627
  40.2 0.1 fusion.3
  40.3 1.5 %collective-permute-start.5 = (bf16[224,96]{1,0:T(8,128)(2,1)S(1)}, bf16[224,96]{1,0:T(8,128)(2,1)S(1)}, u32[]{:S(2)}, u32[]{:S(2)}) collective-permute-start(bf16[224,96]{1,0:T(8,128)(2,1)S(1)} %get-tuple-element.28), channel_id=1, source_target_pairs={{0,1},{1,0},{2,3},{3,2},{4,5},{5,4},{6,7},{7,6},{8,9},{9,8},{10,11... | collective-permute-start | bytes 129032 | tf_op jit(solution)/shard_map/ppermute | solution.py:627
  41.8 2.0 %collective-permute-start.7 = (bf16[224,96]{1,0:T(8,128)(2,1)S(1)}, bf16[224,96]{1,0:T(8,128)(2,1)S(1)}, u32[]{:S(2)}, u32[]{:S(2)}) collective-permute-start(bf16[224,96]{1,0:T(8,128)(2,1)S(1)} %get-tuple-element.29), channel_id=1, source_target_pairs={{0,5},{1,4},{2,7},{3,6},{4,1},{5,0},{6,3},{7,2},{8,13},{9,12},{10,... | collective-permute-start | bytes 129032 | tf_op jit(solution)/shard_map/ppermute | solution.py:627
  43.8 0.7 %collective-permute-done.5 = bf16[224,96]{1,0:T(8,128)(2,1)S(1)} collective-permute-done((bf16[224,96]{1,0:T(8,128)(2,1)S(1)}, bf16[224,96]{1,0:T(8,128)(2,1)S(1)}, u32[]{:S(2)}, u32[]{:S(2)}) %collective-permute-start.5) | collective-permute-done | bytes 43040 | tf_op jit(solution)/shard_map/ppermute | solution.py:627
  44.5 2.5 %collective-permute-done.6 = bf16[224,96]{1,0:T(8,128)(2,1)S(1)} collective-permute-done((bf16[224,96]{1,0:T(8,128)(2,1)S(1)}, bf16[224,96]{1,0:T(8,128)(2,1)S(1)}, u32[]{:S(2)}, u32[]{:S(2)}) %collective-permute-start.6) | collective-permute-done | bytes 43040 | tf_op jit(solution)/shard_map/ppermute | solution.py:627
  47.1 1.4 %collective-permute-start.10 = (bf16[224,96]{1,0:T(8,128)(2,1)S(1)}, bf16[224,96]{1,0:T(8,128)(2,1)S(1)}, u32[]{:S(2)}, u32[]{:S(2)}) collective-permute-start(bf16[224,96]{1,0:T(8,128)(2,1)S(1)} %fusion.2), channel_id=1, source_target_pairs={{0,24},{1,25},{2,26},{3,27},{4,28},{5,29},{6,30},{7,31},{8,16},{9,... | collective-permute-start | bytes 129032 | tf_op jit(solution)/shard_map/ppermute | solution.py:627
  48.5 3.0 %collective-permute-start.9 = (bf16[224,96]{1,0:T(8,128)(2,1)S(1)}, bf16[224,96]{1,0:T(8,128)(2,1)S(1)}, u32[]{:S(2)}, u32[]{:S(2)}) collective-permute-start(bf16[224,96]{1,0:T(8,128)(2,1)S(1)} %fusion.2), channel_id=1, source_target_pairs={{0,16},{1,17},{2,18},{3,19},{4,20},{5,21},{6,22},{7,23},{8,24},{9,... | collective-permute-start | bytes 129032 | tf_op jit(solution)/shard_map/ppermute | solution.py:627
  51.5 1.7 %collective-permute-done.10 = bf16[224,96]{1,0:T(8,128)(2,1)S(1)} collective-permute-done((bf16[224,96]{1,0:T(8,128)(2,1)S(1)}, bf16[224,96]{1,0:T(8,128)(2,1)S(1)}, u32[]{:S(2)}, u32[]{:S(2)}) %collective-permute-start.10) | collective-permute-done | bytes 43040 | tf_op jit(solution)/shard_map/ppermute | solution.py:627
  53.2 0.7 %collective-permute-done.8 = bf16[224,96]{1,0:T(8,128)(2,1)S(1)} collective-permute-done((bf16[224,96]{1,0:T(8,128)(2,1)S(1)}, bf16[224,96]{1,0:T(8,128)(2,1)S(1)}, u32[]{:S(2)}, u32[]{:S(2)}) %collective-permute-start.8) | collective-permute-done | bytes 43040 | tf_op jit(solution)/shard_map/ppermute | solution.py:627
  54.0 1.3 %collective-permute-start.11 = (bf16[224,96]{1,0:T(8,128)(2,1)S(1)}, bf16[224,96]{1,0:T(8,128)(2,1)S(1)}, u32[]{:S(2)}, u32[]{:S(2)}) collective-permute-start(bf16[224,96]{1,0:T(8,128)(2,1)S(1)} %add_convert_fusion), channel_id=1, source_target_pairs={{0,1},{1,0},{2,3},{3,2},{4,5},{5,4},{6,7},{7,6},{8,9},{9,8},{10,11... | collective-permute-start | bytes 129032 | tf_op jit(solution)/shard_map/ppermute | solution.py:627
  55.2 1.0 %collective-permute-start.12 = (bf16[224,96]{1,0:T(8,128)(2,1)S(1)}, bf16[224,96]{1,0:T(8,128)(2,1)S(1)}, u32[]{:S(2)}, u32[]{:S(2)}) collective-permute-start(bf16[224,96]{1,0:T(8,128)(2,1)S(1)} %add_convert_fusion), channel_id=1, source_target_pairs={{0,4},{1,5},{2,6},{3,7},{4,0},{5,1},{6,2},{7,3},{8,12},{9,13},{10,... | collective-permute-start | bytes 129032 | tf_op jit(solution)/shard_map/ppermute | solution.py:627
  56.3 1.2 %collective-permute-start.13 = (bf16[224,96]{1,0:T(8,128)(2,1)S(1)}, bf16[224,96]{1,0:T(8,128)(2,1)S(1)}, u32[]{:S(2)}, u32[]{:S(2)}) collective-permute-start(bf16[224,96]{1,0:T(8,128)(2,1)S(1)} %add_convert_fusion), channel_id=1, source_target_pairs={{0,5},{1,4},{2,7},{3,6},{4,1},{5,0},{6,3},{7,2},{8,13},{9,12},{10,... | collective-permute-start | bytes 129032 | tf_op jit(solution)/shard_map/ppermute | solution.py:627
  57.5 0.1 copy.49
  57.6 0.1 copy.50
  57.6 0.6 collective-permute-done.11
  58.2 1.2 %collective-permute-done.12 = bf16[224,96]{1,0:T(8,128)(2,1)S(1)} collective-permute-done((bf16[224,96]{1,0:T(8,128)(2,1)S(1)}, bf16[224,96]{1,0:T(8,128)(2,1)S(1)}, u32[]{:S(2)}, u32[]{:S(2)}) %collective-permute-start.12) | collective-permute-done | bytes 43040 | tf_op jit(solution)/shard_map/ppermute | solution.py:627
  59.4 1.9 %collective-permute-done.13 = bf16[224,96]{1,0:T(8,128)(2,1)S(1)} collective-permute-done((bf16[224,96]{1,0:T(8,128)(2,1)S(1)}, bf16[224,96]{1,0:T(8,128)(2,1)S(1)}, u32[]{:S(2)}, u32[]{:S(2)}) %collective-permute-start.13) | collective-permute-done | bytes 43040 | tf_op jit(solution)/shard_map/ppermute | solution.py:627
  61.4 0.1 pad_maximum_fusion.mine_ref
  61.4 0.1 collective-permute-start.14
  61.5 0.1 copy.51
  61.6 0.1 copy.52
  61.6 0.1 copy.48
  61.8 1.4 %concatenate.7 = bf16[96,21,96]{2,1,0:T(8,128)(2,1)S(1)} concatenate(bf16[96,9,96]{2,1,0:T(8,128)(2,1)S(1)} %copy.48, bf16[96,3,96]{2,1,0:T(4,128)(2,1)S(1)} %copy.49, bf16[96,3,96]{2,1,0:T(4,128)(2,1)S(1)} %copy.50, bf16[96,3,96]{2,1,0:T(4,128)(2,1)S(1)} %copy.51, bf16[96,3,96]{2,1,0:T(4,128)(2,1)S(1)} %copy.52), dimensions={1} | concatenate | bytes 774144 | tf_op jit(solution)/shard_map/concatenate | solution.py:651
  63.1 0.4 reshape.47.w_one
  63.5 0.2 copy.53.w_two
  63.7 1.9 %shard_map.131 = (bf16[2,2,96,96]{3,2,1,0:T(8,128)(2,1)S(1)}, bf16[2,2,96,96]{3,2,1,0:T(8,128)(2,1)S(1)}) custom-call(s32[5]{0:T(128)S(1)} %stack.44.ids_ref, bf16[96,1152]{1,0:T(8,128)(2,1)S(1)} %get-tuple-element.10.hidden_ref, bf16[96,1152]{1,0:T(8,128)(2,1)S(1)} %get-tuple-element.11.pre_grad_ref, bf16[96,864]{1,0:T(8,128)(2,1)S(1)} %copy.53.w_two, ...), custom_call_target="tpu_custom_call" | custom-call | tf_op jit(solution)/shard_map/pallas_call | solution.py:582
  65.6 0.7 %copy.54 = bf16[96,2,2,96]{3,2,1,0:T(2,128)(2,1)} copy(bf16[96,2,2,96]{3,0,2,1:T(8,128)(2,1)S(1)} %bitcast.68) | data formatting | bytes 147456
  66.3 0.7 %copy.55 = bf16[96,2,2,96]{3,2,1,0:T(2,128)(2,1)} copy(bf16[96,2,2,96]{3,0,2,1:T(8,128)(2,1)S(1)} %bitcast.67) | data formatting | bytes 147456
  67.0 0.6 shard_map.132
  67.7 1.0 %fusion.4 = (f32[864,96]{1,0:T(8,128)}, f32[864,96]{1,0:T(8,128)}) fusion(f32[1792,96]{1,0:T(8,128)S(1)} %shard_map.132), kind=kLoop, calls=%fused_computation.24 | loop fusion | bytes 1327104 | tf_op jit(solution)/shard_map/slice | solution.py:716
  (24 shorter events, 0.3 us)
Async XLA Ops:
  0.6 5.0 %copy-start = (bf16[2,512,512]{2,1,0:T(8,128)(2,1)S(1)}, bf16[2,512,512]{2,1,0:T(8,128)(2,1)}, u32[]{:S(2)}) copy-start(bf16[2,512,512]{2,1,0:T(8,128)(2,1)} %constant.33.clone.table_ref) | copy-start | bytes 3145732
  1.8 28.4 %collective-permute-start = (bf16[2,2,2,96,128]{4,3,1,0,2:T(8,128)(2,1)S(1)}, bf16[2,2,2,96,128]{4,3,1,0,2:T(8,128)(2,1)S(1)}, u32[]{:S(2)}, u32[]{:S(2)}) collective-permute-start(bf16[2,2,2,96,128]{4,3,1,0,2:T(8,128)(2,1)S(1)} %pad.4), channel_id=1, source_target_pairs={{0,2},{2,4},{4,6},{6,8},{8,10},{10,12},{12,14},{14,16},{16,18},{18... | collective-permute-start | bytes 589832 | tf_op jit(solution)/shard_map/ppermute | solution.py:594
  4.2 26.1 %collective-permute-start.1 = (bf16[2,2,2,96,128]{4,3,1,0,2:T(8,128)(2,1)S(1)}, bf16[2,2,2,96,128]{4,3,1,0,2:T(8,128)(2,1)}, u32[]{:S(2)}, u32[]{:S(2)}) collective-permute-start(bf16[2,2,2,96,128]{4,3,1,0,2:T(8,128)(2,1)S(1)} %pad.4), channel_id=1, source_target_pairs={{2,0},{4,2},{6,4},{8,6},{10,8},{12,10},{14,12},{16,14},{18,16},{20... | collective-permute-start | bytes 589832 | tf_op jit(solution)/shard_map/ppermute | solution.py:594
  5.5 0.7 %copy-start.4 = (bf16[2,8,512]{2,1,0:T(8,128)(2,1)S(1)}, bf16[2,8,512]{2,1,0:T(8,128)(2,1)}, u32[]{:S(2)}) copy-start(bf16[2,8,512]{2,1,0:T(8,128)(2,1)} %constant.34.clone.poles_ref) | copy-start | bytes 49156
  8.0 25.7 %all-to-all-start = ((bf16[32,48,96]{2,1,0:T(8,128)(2,1)}), bf16[32,48,96]{2,1,0:T(8,128)(2,1)S(1)}, u32[]{:S(2)}, u32[]{:S(2)}) async-start(bf16[32,48,96]{2,1,0:T(8,128)(2,1)} %bitcast.9), calls=%async_computation | async-start | bytes 786432 | tf_op jit(solution)/shard_map/all_to_all | solution.py:616
  17.2 10.2 %copy-start.7 = (bf16[3,3,96,96]{3,2,1,0:T(8,128)(2,1)S(1)}, bf16[3,3,96,96]{3,2,1,0:T(8,128)(2,1)}, u32[]{:S(2)}) copy-start(bf16[3,3,96,96]{3,2,1,0:T(8,128)(2,1)} %param.13) | copy-start | bytes 497668
  17.9 13.4 %collective-permute-start.2 = (bf16[2,2,1,96,128]{4,3,1,0,2:T(8,128)(2,1)}, bf16[2,2,1,96,128]{4,3,1,0,2:T(8,128)(2,1)S(1)}, u32[]{:S(2)}, u32[]{:S(2)}) collective-permute-start(bf16[2,2,1,96,128]{4,3,1,0,2:T(8,128)(2,1)} %get-tuple-element.40), channel_id=1, source_target_pairs={{0,30},{30,0},{1,31},{31,1}} | collective-permute-start | bytes 294920 | tf_op jit(solution)/shard_map/ppermute | solution.py:607
  24.1 9.5 %collective-permute-start.3 = (bf16[2,2,96,128]{3,2,1,0:T(8,128)(2,1)S(1)}, bf16[2,2,96,128]{3,2,1,0:T(8,128)(2,1)S(1)}, u32[]{:S(2)}, u32[]{:S(2)}) collective-permute-start(bf16[2,2,96,128]{3,2,1,0:T(8,128)(2,1)S(1)} %get-tuple-element.39), channel_id=1, source_target_pairs={{30,1},{31,0},{1,30},{0,31}} | collective-permute-start | bytes 294920 | tf_op jit(solution)/shard_map/ppermute | solution.py:603
  29.1 0.9 %copy-start.6 = (bf16[3,3,96,96]{3,2,1,0:T(8,128)(2,1)S(1)}, bf16[3,3,96,96]{3,2,1,0:T(8,128)(2,1)}, u32[]{:S(2)}) copy-start(bf16[3,3,96,96]{3,2,1,0:T(8,128)(2,1)} %param.12) | copy-start | bytes 497668
  30.2 3.4 %copy-start.2 = (bf16[256,512]{1,0:T(8,128)(2,1)S(1)}, bf16[256,512]{1,0:T(8,128)(2,1)}, u32[]{:S(2)}) copy-start(bf16[256,512]{1,0:T(8,128)(2,1)} %constant.36.clone.refs_7_) | copy-start | bytes 786436
  30.3 3.4 %copy-start.3 = (bf16[768,128]{1,0:T(8,128)(2,1)S(1)}, bf16[768,128]{1,0:T(8,128)(2,1)}, u32[]{:S(2)}) copy-start(bf16[768,128]{1,0:T(8,128)(2,1)} %constant.37.clone.refs_8_) | copy-start | bytes 589828
  30.3 3.4 %copy-start.1 = (bf16[256,512]{1,0:T(8,128)(2,1)S(1)}, bf16[256,512]{1,0:T(8,128)(2,1)}, u32[]{:S(2)}) copy-start(bf16[256,512]{1,0:T(8,128)(2,1)} %constant.35.clone.refs_6_) | copy-start | bytes 786436
  30.3 3.4 %copy-start.5 = (bf16[32,128]{1,0:T(8,128)(2,1)S(1)}, bf16[32,128]{1,0:T(8,128)(2,1)}, u32[]{:S(2)}) copy-start(bf16[32,128]{1,0:T(8,128)(2,1)} %constant.38.clone.refs_9_) | copy-start | bytes 24580
  38.6 1.6 %collective-permute-start.4 = (bf16[4,224,96]{2,1,0:T(8,128)(2,1)S(1)}, bf16[4,224,96]{2,1,0:T(8,128)(2,1)S(1)}, u32[]{:S(2)}, u32[]{:S(2)}) collective-permute-start(bf16[4,224,96]{2,1,0:T(8,128)(2,1)S(1)} %get-tuple-element.15), channel_id=1, source_target_pairs={{0,2},{1,3},{2,0},{3,1},{4,6},{5,7},{6,4},{7,5},{8,10},{9,11},{10,... | collective-permute-start | bytes 516104 | tf_op jit(solution)/shard_map/ppermute | solution.py:627
  40.3 4.2 %collective-permute-start.5 = (bf16[224,96]{1,0:T(8,128)(2,1)S(1)}, bf16[224,96]{1,0:T(8,128)(2,1)S(1)}, u32[]{:S(2)}, u32[]{:S(2)}) collective-permute-start(bf16[224,96]{1,0:T(8,128)(2,1)S(1)} %get-tuple-element.28), channel_id=1, source_target_pairs={{0,1},{1,0},{2,3},{3,2},{4,5},{5,4},{6,7},{7,6},{8,9},{9,8},{10,11... | collective-permute-start | bytes 129032 | tf_op jit(solution)/shard_map/ppermute | solution.py:627
  41.8 5.2 %collective-permute-start.6 = (bf16[224,96]{1,0:T(8,128)(2,1)S(1)}, bf16[224,96]{1,0:T(8,128)(2,1)S(1)}, u32[]{:S(2)}, u32[]{:S(2)}) collective-permute-start(bf16[224,96]{1,0:T(8,128)(2,1)S(1)} %get-tuple-element.30), channel_id=1, source_target_pairs={{0,4},{1,5},{2,6},{3,7},{4,0},{5,1},{6,2},{7,3},{8,12},{9,13},{10,... | collective-permute-start | bytes 129032 | tf_op jit(solution)/shard_map/ppermute | solution.py:627
  41.8 5.2 %collective-permute-start.7 = (bf16[224,96]{1,0:T(8,128)(2,1)S(1)}, bf16[224,96]{1,0:T(8,128)(2,1)S(1)}, u32[]{:S(2)}, u32[]{:S(2)}) collective-permute-start(bf16[224,96]{1,0:T(8,128)(2,1)S(1)} %get-tuple-element.29), channel_id=1, source_target_pairs={{0,5},{1,4},{2,7},{3,6},{4,1},{5,0},{6,3},{7,2},{8,13},{9,12},{10,... | collective-permute-start | bytes 129032 | tf_op jit(solution)/shard_map/ppermute | solution.py:627
  47.1 6.1 %collective-permute-start.10 = (bf16[224,96]{1,0:T(8,128)(2,1)S(1)}, bf16[224,96]{1,0:T(8,128)(2,1)S(1)}, u32[]{:S(2)}, u32[]{:S(2)}) collective-permute-start(bf16[224,96]{1,0:T(8,128)(2,1)S(1)} %fusion.2), channel_id=1, source_target_pairs={{0,24},{1,25},{2,26},{3,27},{4,28},{5,29},{6,30},{7,31},{8,16},{9,... | collective-permute-start | bytes 129032 | tf_op jit(solution)/shard_map/ppermute | solution.py:627
  48.5 5.4 %collective-permute-start.8 = (bf16[224,96]{1,0:T(8,128)(2,1)S(1)}, bf16[224,96]{1,0:T(8,128)(2,1)S(1)}, u32[]{:S(2)}, u32[]{:S(2)}) collective-permute-start(bf16[224,96]{1,0:T(8,128)(2,1)S(1)} %fusion.2), channel_id=1, source_target_pairs={{0,8},{1,9},{2,10},{3,11},{4,12},{5,13},{6,14},{7,15},{8,0},{9,1},... | collective-permute-start | bytes 129032 | tf_op jit(solution)/shard_map/ppermute | solution.py:627
  48.5 5.4 %collective-permute-start.9 = (bf16[224,96]{1,0:T(8,128)(2,1)S(1)}, bf16[224,96]{1,0:T(8,128)(2,1)S(1)}, u32[]{:S(2)}, u32[]{:S(2)}) collective-permute-start(bf16[224,96]{1,0:T(8,128)(2,1)S(1)} %fusion.2), channel_id=1, source_target_pairs={{0,16},{1,17},{2,18},{3,19},{4,20},{5,21},{6,22},{7,23},{8,24},{9,... | collective-permute-start | bytes 129032 | tf_op jit(solution)/shard_map/ppermute | solution.py:627
  54.0 4.2 %collective-permute-start.11 = (bf16[224,96]{1,0:T(8,128)(2,1)S(1)}, bf16[224,96]{1,0:T(8,128)(2,1)S(1)}, u32[]{:S(2)}, u32[]{:S(2)}) collective-permute-start(bf16[224,96]{1,0:T(8,128)(2,1)S(1)} %add_convert_fusion), channel_id=1, source_target_pairs={{0,1},{1,0},{2,3},{3,2},{4,5},{5,4},{6,7},{7,6},{8,9},{9,8},{10,11... | collective-permute-start | bytes 129032 | tf_op jit(solution)/shard_map/ppermute | solution.py:627
  55.2 4.2 %collective-permute-start.12 = (bf16[224,96]{1,0:T(8,128)(2,1)S(1)}, bf16[224,96]{1,0:T(8,128)(2,1)S(1)}, u32[]{:S(2)}, u32[]{:S(2)}) collective-permute-start(bf16[224,96]{1,0:T(8,128)(2,1)S(1)} %add_convert_fusion), channel_id=1, source_target_pairs={{0,4},{1,5},{2,6},{3,7},{4,0},{5,1},{6,2},{7,3},{8,12},{9,13},{10,... | collective-permute-start | bytes 129032 | tf_op jit(solution)/shard_map/ppermute | solution.py:627
  56.3 5.1 %collective-permute-start.13 = (bf16[224,96]{1,0:T(8,128)(2,1)S(1)}, bf16[224,96]{1,0:T(8,128)(2,1)S(1)}, u32[]{:S(2)}, u32[]{:S(2)}) collective-permute-start(bf16[224,96]{1,0:T(8,128)(2,1)S(1)} %add_convert_fusion), channel_id=1, source_target_pairs={{0,5},{1,4},{2,7},{3,6},{4,1},{5,0},{6,3},{7,2},{8,13},{9,12},{10,... | collective-permute-start | bytes 129032 | tf_op jit(solution)/shard_map/ppermute | solution.py:627
  61.4 5.6 %collective-permute-start.14 = (bf16[4,224,96]{2,1,0:T(8,128)(2,1)S(1)}, bf16[4,224,96]{2,1,0:T(8,128)(2,1)S(1)}, u32[]{:S(2)}, u32[]{:S(2)}) collective-permute-start(bf16[4,224,96]{2,1,0:T(8,128)(2,1)S(1)} %pad_maximum_fusion.mine_ref), channel_id=1, source_target_pairs={{0,2},{1,3},{2,0},{3,1},{4,6},{5,7},{6,4},{7,5},{8,10},{9,11},{10,... | collective-permute-start | bytes 516104 | tf_op jit(solution)/shard_map/ppermute | solution.py:627

commit v2 on v1

--- a/solution.py
+++ b/solution.py
@@ -140,11 +140,12 @@
     return pltpu.roll(x, by % x.shape[1], 1)
 
 
-def surroundings(plan, ids_ref, k, columns_ref, near_l, near_r, wrap_ref, cross_ref, got_ref, tables):
+def surroundings(plan, ids_ref, k, columns_ref, inner_ref, outer_ref, got_ref, tables):
     w, n, c = plan.cols, plan.lanes, plan.cells
     high, g_count = plan.height, plan.stacks
     first = ids_ref[0] == 0
     last = ids_ref[0] == plan.tiles - 1
+    even = lax.rem(ids_ref[0], 2) == 0
     face = ids_ref[1]
     after = lax.rem(face + 1, plan.faces)
     before = lax.rem(face + plan.faces - 1, plan.faces)
@@ -167,23 +168,22 @@
             seams.append([out[:, i * n : (i + 1) * n] for i in range(4)])
         line += shift(seams[0][2] + seams[1][2], 16 * g)
         deep += shift(seams[0][3] + seams[1][3], 16 * g)
-        raw = [near_l[i, k, g] for i in range(2)]
+        raw = [jnp.where(even, outer_ref[i, k, g], inner_ref[i, k, g]) for i in range(2)]
         raw += [columns_ref[i, k, g] for i in range(w)]
-        raw += [near_r[i, k, g] for i in range(2)]
+        raw += [jnp.where(even, inner_ref[i, k, g], outer_ref[i, k, g]) for i in range(2)]
         ends += shift(product(jnp.concatenate(raw, axis=1), tab_ends, 1, 0), 16 * g)
-        end_l = [(wrap_ref[i, k, g - 1] if g > 0 else cross_ref[i, k]) for i in range(2)]
-        end_r = [(wrap_ref[i, k, g] if g < g_count - 1 else cross_ref[i, k]) for i in range(2)]
+        raw = [x.astype(F32) for x in raw]
         pole = []
         for at in range(2):
             base = at * plan.poles + k * (plan.poles // 2) + 3 * g
             pole.append([poles[:, base + i : base + i + 1] for i in range(3)])
         stacks.append(
             dict(
-                raw=[x.astype(F32) for x in raw],
+                raw=raw,
                 row_l=seams[1][:2],
                 row_r=seams[0][:2],
-                col_l=[shift(x.astype(F32), plan.side) for x in end_l],
-                col_r=[shift(x.astype(F32), -plan.side) for x in end_r],
+                col_l=[shift(x, plan.side) for x in raw[:2]],
+                col_r=[shift(x, -plan.side) for x in raw[w + 2 :]],
                 north=pole[0],
                 south=pole[1],
             )
@@ -488,6 +488,11 @@
                 taps_ref[(18 + b) * c : (19 + b) * c, at : at + n] = y
 
 
+def seam_weights(kernel_ref):
+    order = list(range(9)) + [0, 1, 2, 6, 7, 8, 0, 3, 6, 2, 5, 8]
+    return jnp.concatenate([kernel_ref[tap] for tap in order], axis=1)
+
+
 def own_columns(plan, ref):
     w, n = plan.cols, plan.lanes
     return [
@@ -498,13 +503,13 @@
 
 def middle_kernel(plan, ids_ref, *refs):
     w, n, g_count, c = plan.cols, plan.lanes, plan.stacks, plan.channels
-    around, tables, (w_one, w_two), refs = refs[:6], refs[6:10], refs[10:12], refs[12:]
+    around, tables, (w_one, w_two), refs = refs[:4], refs[4:8], refs[8:10], refs[10:]
     hidden_ref, pre_grad_ref, mine_ref, theirs_ref, fwd_ref, bwd_ref, sums_ref = refs
     tables = [x[...] for x in tables]
     wide_forward(plan, surroundings(plan, ids_ref, 0, *around, tables), fwd_ref)
     wide_backward(plan, surroundings(plan, ids_ref, 1, *around, tables), bwd_ref)
-    pre = jnp.dot(w_one[...], fwd_ref[...], preferred_element_type=F32)
-    grad = jnp.dot(w_two[...], bwd_ref[...], preferred_element_type=F32)
+    pre = product(w_one[...], fwd_ref[...], 0, 0)
+    grad = product(seam_weights(w_two), bwd_ref[...], 1, 0)
     bend = jnp.tanh(GELU_A * (pre + GELU_B * (pre * pre * pre)))
     half = 0.5 * (1.0 + bend)
     slope = half + 0.5 * pre * (1.0 - bend * bend) * (
@@ -556,22 +561,25 @@
     forward_operand(plan, own_columns(plan, hidden_ref), halo, fwd_ref)
     halo = second_halos(plan, ids_ref, pre_grad_ref)
     backward_operand(plan, own_columns(plan, pre_grad_ref), halo, bwd_ref)
-    out = jnp.dot(w_two[...], fwd_ref[...], preferred_element_type=F32).astype(BF16)
-    back = jnp.dot(w_one[...], bwd_ref[...], preferred_element_type=F32).astype(BF16)
+    out = product(w_two[...], fwd_ref[...], 0, 0).astype(BF16)
+    back = product(seam_weights(w_one), bwd_ref[...], 1, 0).astype(BF16)
     for g in range(plan.stacks):
         for i in range(w):
             at = (g * w + i) * n
-            out_ref[g, i] = out[:, at : at + plan.height]
-            back_ref[g, i] = back[:, at : at + plan.height]
-
-
-def sum_kernel(plan, scale, ids_ref, mine_ref, theirs_ref, sums_ref):
+            out_ref[:, g, i, :] = out[:, at : at + plan.height]
+            back_ref[:, g, i, :] = back[:, at : at + plan.height]
+
+
+def sum_kernel(plan, scale, ids_ref, mine_ref, theirs_ref, one_ref, two_ref, sums_ref):
     near, mid = ids_ref[3], ids_ref[4]
     for d in range(plan.mid):
         spot = jnp.bitwise_xor(mid, d)
         for other, ref in ((0, mine_ref), (1, theirs_ref)):
             at = (jnp.bitwise_xor(near, other) * plan.mid + spot) * plan.piece
             sums_ref[pl.ds(pl.multiple_of(at, 16), plan.piece), :] = ref[d].astype(F32) * scale
+    rows = one_ref.shape[0]
+    one_ref[...] = sums_ref[:rows]
+    two_ref[...] = sums_ref[rows : 2 * rows]
 
 
 VMEM = pl.BlockSpec(memory_space=pltpu.VMEM)
@@ -589,32 +597,35 @@
     )(ids, *inputs)
 
 
-def tile_ring(plan, x, step):
-    pairs = [(i, i + step) for i in range(plan.tiles) if 0 <= i + step < plan.tiles]
-    return lax.ppermute(x, "tile", pairs)
-
-
-def swap_ends(plan, columns):
-    t, f, g = plan.tiles, plan.faces, plan.stacks
+def end_stacks(plan, columns):
+    t, f = plan.tiles, plan.faces
     first = lax.axis_index("tile") == 0
+    sent = jnp.where(first, columns[:2, :, 0], columns[plan.cols - 2 :, :, plan.stacks - 1])
+    pairs = [((t - 1) * f + i, (t - 1) * f + (i + 1) % f) for i in range(f)]
+    pairs += [((i + 1) % f, i) for i in range(f)]
+    return lax.ppermute(sent, BOTH, pairs)
+
+
+def pair_up(plan, columns, passed):
+    t, g = plan.tiles, plan.stacks
+    tile = lax.axis_index("tile")
+    even = tile % 2 == 0
     head, tail = columns[:2], columns[plan.cols - 2 :]
-    pairs = [((t - 1) * f + i, (i + 1) % f) for i in range(f)]
-    pairs += [((i + 1) % f, (t - 1) * f + i) for i in range(f)]
-    cross = lax.ppermute(jnp.where(first, head[:, :, 0], tail[:, :, g - 1]), BOTH, pairs)
-    if g == 1:
-        return cross[:, :, None], cross
-    sent = jnp.where(first, head[:, :, 1:], tail[:, :, : g - 1])
-    return lax.ppermute(sent, "tile", [(0, t - 1), (t - 1, 0)]), cross
-
-
-def exchange(plan, columns, blocks):
-    left = tile_ring(plan, columns[plan.cols - 2 :], 1)
-    right = tile_ring(plan, columns[:2], -1)
-    wrap, cross = swap_ends(plan, columns)
+    inner = jnp.where(even, tail, head)
+    outer = jnp.where(even, head, tail)
+    passed = passed[:, :, None]
+    to_last = jnp.concatenate([head[:, :, 1:], passed], axis=2)
+    to_first = jnp.concatenate([passed, tail[:, :, : g - 1]], axis=2)
+    outer = jnp.where(tile == 0, to_last, jnp.where(tile == t - 1, to_first, outer))
+    inner = lax.ppermute(inner, "tile", [(i, i ^ 1) for i in range(t)])
+    outer = lax.ppermute(outer, "tile", [(i, ((i + 1) ^ 1) - 1 if i else t - 1) for i in range(t - 1)] + [(t - 1, 0)])
+    return inner, outer
+
+
+def spread_blocks(plan, blocks):
     count = plan.tiles * plan.faces
     flat = blocks.reshape((count,) + blocks.shape[2:])
-    got = lax.all_to_all(flat, BOTH, 0, 0, tiled=True).reshape(blocks.shape)
-    return left, right, wrap, cross, got
+    return lax.all_to_all(flat, BOTH, 0, 0, tiled=True).reshape(blocks.shape)
 
 
 def swapped(plan, x, near=0, mid=0, far=0):
@@ -633,22 +644,17 @@
     return values[0]
 
 
-def sum_all(plan, mine, theirs):
+def sum_all(plan, mine, theirs, beside):
     half = mine + swapped(plan, theirs, near=1).astype(F32)
     short = half.astype(BF16)
-    got = [swapped(plan, short[d], mid=d).astype(F32) for d in range(1, plan.mid)]
-    piece = tree_sum([half[0]] + got).astype(BF16)
+    got = [swapped(plan, short[d], mid=d) for d in range(1, plan.mid)]
+    got, beside = lax.optimization_barrier((got, beside))
+    piece = tree_sum([half[0]] + [x.astype(F32) for x in got]).astype(BF16)
     got = [swapped(plan, piece, far=d) for d in range(1, plan.far)]
     piece = tree_sum([x.astype(F32) for x in [piece] + got]).astype(BF16)
     pieces = [piece] + [swapped(plan, piece, mid=d) for d in range(1, plan.mid)]
     half = jnp.stack(pieces)
-    return half, swapped(plan, half, near=1)
-
-
-def seam_weights(kernel):
-    lines = [kernel.reshape(kernel.shape[0], 9, -1), kernel[:, 0], kernel[:, 2]]
-    lines += [kernel[:, :, 0], kernel[:, :, 2]]
-    return jnp.concatenate(lines, axis=1).reshape(kernel.shape[0], -1)
+    return half, swapped(plan, half, near=1), beside
 
 
 def on_device(mesh_shape, fields, upstream, kernel_one, kernel_two):
@@ -672,14 +678,15 @@
         [*plan.send_tables(), columns],
         [blocks_shape],
     )
-    halo = exchange(plan, columns, blocks)
-
-    fwd_one = kernel_one.transpose(3, 0, 1, 2).reshape(c, -1)
-    bwd_two = seam_weights(kernel_two.transpose(2, 0, 1, 3))
-    fwd_two = lax.dynamic_slice_in_dim(kernel_two, sub * own, own, 3)
-    fwd_two = fwd_two.transpose(3, 0, 1, 2).reshape(own, -1)
-    bwd_one = lax.dynamic_slice_in_dim(kernel_one, sub * own, own, 2)
-    bwd_one = seam_weights(bwd_one.transpose(2, 0, 1, 3))
+    passed = end_stacks(plan, columns)
+    got = spread_blocks(plan, blocks)
+    sent, passed, _ = lax.optimization_barrier((columns, passed, blocks))
+    halo = (*pair_up(plan, sent, passed), got)
+
+    fwd_one = kernel_one.reshape(9 * c, c)
+    bwd_two = kernel_two.reshape(9, c, c)
+    fwd_two = lax.dynamic_slice_in_dim(kernel_two, sub * own, own, 3).reshape(9 * c, own)
+    bwd_one = lax.dynamic_slice_in_dim(kernel_one, sub * own, own, 2).reshape(9, own, c)
 
     def taps(width):
         return [pltpu.VMEM((9 * c, width), BF16), pltpu.VMEM((21 * c, width), BF16)]
@@ -695,29 +702,30 @@
         + [jax.ShapeDtypeStruct(piece, F32), jax.ShapeDtypeStruct(piece, BF16)],
         taps(wide) + [pltpu.VMEM((rows, c), F32)],
     )
-    mine, theirs = sum_all(plan, mine, theirs)
-    out_shape = jax.ShapeDtypeStruct((g, w, own, h), BF16)
-    result, fields_grad = call(
+    out_shape = jax.ShapeDtypeStruct((own, g, w, h), BF16)
+    beside = call(
         functools.partial(last_kernel, plan),
         ids,
         [hidden, pre_grad, fwd_two, bwd_one],
         [out_shape, out_shape],
         taps(g * w * n),
     )
+    mine, theirs, (result, fields_grad) = sum_all(plan, mine, theirs, list(beside))
     scale = 1.0 / (plan.side * 12.0**0.5)
-    (sums,) = call(
+    sums = call(
         functools.partial(sum_kernel, plan, scale),
         ids,
         [mine, theirs],
-        [jax.ShapeDtypeStruct((rows, c), F32)],
+        [jax.ShapeDtypeStruct((9 * c, c), F32)] * 2,
+        [pltpu.VMEM((rows, c), F32)],
     )
     grads = []
     for i in range(2):
-        grad = sums[9 * c * i : 9 * c * (i + 1)].reshape(3, 3, c, c)
+        grad = sums[i].reshape(3, 3, c, c)
         grads.append(lax.dynamic_slice_in_dim(grad, sub * own, own, 3))
     return (
-        result.transpose(2, 0, 1, 3),
-        fields_grad.transpose(2, 0, 1, 3),
+        result,
+        fields_grad,
         grads[0],
         grads[1],
     )

time: 69.1 us -> 60.1 us (0.87)
  local copies, waits for them, and re-layouts: 10.3 us -> 1.82 us
  starting transfers between devices: 34 us -> 26.3 us
  waiting for transfers between devices: 13.1 us -> 19 us
  Pallas kernels: 9.23 us -> 11.4 us
    ppermute x4 -> x3, waiting for transfers between devices: 2.3 us -> 9.69 us  [the longest x1 9.69 us: pair_up(): lax.ppermute(outer, 'tile', [(i, (i + 1 ^ 1) - 1 if i else t - 1) for i i...]
    all_to_all x1, starting transfers between devices: 9.2 us -> 4.08 us  [spread_blocks(): return lax.all_to_all(flat, BOTH, 0, 0, tiled=True).reshape(blocks.shape)]
    ppermute x4 -> x3, starting transfers between devices: 13.1 us -> 9.22 us  [the longest x1 4.85 us: end_stacks(): return lax.ppermute(sent, BOTH, pairs)]
    concatenate x2 -> x0, local copies, waits for them, and re-layouts: 2.7 us -> none  [seam_weights(): return jnp.concatenate(lines, axis=1).reshape(kernel.shape[0], -1)]
    pallas_call x4, Pallas kernels: 9.23 us -> 11.4 us  [call(): pl.pallas_call(body, out_shape=outs, in_specs=[SMEM] + [VMEM] * len(input...]
    unnamed x18 -> x16, local copies, waits for them, and re-layouts: 2.61 us -> 0.61 us
    ppermute x11, waiting for transfers between devices: 10.8 us -> 9.3 us  [swapped(): return lax.ppermute(x, BOTH, pairs)]
    reshape x6 -> x0, local copies, waits for them, and re-layouts: 1.35 us -> none  [the longest x2 0.81 us: seam_weights(): return jnp.concatenate(lines, axis=1).reshape(kernel.shape[0], -1)]
  transfers between devices with their start and end apart: 16 -> 15, of which waited for: 9 -> 9; matrix products, arithmetic and copies ran while one was open for 11% -> 0% of each run, Pallas kernels for 5% -> 8%
where the time goes in v2:
time: 60.1 us; the launch traced here: 59.7 us
  starting transfers between devices  26.3 us (44%)
  waiting for transfers between devices  19 us (32%)
  Pallas kernels  11.4 us (19%)
  local copies, waits for them, and re-layouts  1.82 us (3%)
  between operations  0.87 us (1%)
    ppermute x11, starting transfers between devices, swapped(): return lax.ppermute(x, BOTH, pairs)  13 us
    pallas_call x4, Pallas kernels, call(): pl.pallas_call(body, out_shape=outs, in_specs=[SMEM] + [VMEM] * len(input...  11.4 us
    ppermute x1, waiting for transfers between devices, pair_up(): lax.ppermute(outer, 'tile', [(i, (i + 1 ^ 1) - 1 if i else t - 1) for i i...  9.69 us
    ppermute x11, waiting for transfers between devices, swapped(): return lax.ppermute(x, BOTH, pairs)  9.3 us
    ppermute x1, starting transfers between devices, end_stacks(): return lax.ppermute(sent, BOTH, pairs)  4.85 us
    ppermute x1, starting transfers between devices, pair_up(): lax.ppermute(outer, 'tile', [(i, (i + 1 ^ 1) - 1 if i else t - 1) for i i...  4.37 us
    all_to_all x1, starting transfers between devices, spread_blocks(): return lax.all_to_all(flat, BOTH, 0, 0, tiled=True).reshape(blocks.shape)  4.08 us
  transfers between devices with their start and end apart: 15, of which 9 were waited for; matrix products, arithmetic and copies ran while one was open for 0% of the time, Pallas kernels for 8%

profile of v2, /device:TPU:0, one launch (start us, length us, event | category | flops | bytes accessed | tf_op | source)
XLA Modules:
  0.0 59.7 jit_solution(11404873725194156609)
XLA Ops:
  0.6 0.0 copy-start
  0.7 1.1 %copy_bitcast_fusion = (bf16[1,96,2,2,96]{4,1,2,0,3:T(8,128)(2,1)S(1)}, bf16[1,96,2,2,96]{4,1,2,0,3:T(8,128)(2,1)S(1)}) fusion(bf16[96,2,2,96]{3,2,1,0:T(2,128)(2,1)} %param.11, bf16[96,2,2,96]{3,2,1,0:T(2,128)(2,1)} %param.10), kind=kLoop, calls=%fused_computation.12 | loop fusion | bytes 294912 | tf_op jit(solution)/shard_map/stack | solution.py:672
  1.8 4.8 %collective-permute-start = (bf16[2,2,96,128]{3,2,1,0:T(8,128)(2,1)S(1)}, bf16[2,2,96,128]{3,2,1,0:T(8,128)(2,1)S(1)}, u32[]{:S(2)}, u32[]{:S(2)}) collective-permute-start(bf16[2,2,96,128]{3,2,1,0:T(8,128)(2,1)S(1)} %fusion.3), channel_id=1, source_target_pairs={{30,31},{31,30},{1,0},{0,1}} | collective-permute-start | bytes 294920 | tf_op jit(solution)/shard_map/ppermute | solution.py:606
  6.7 0.0 copy-start.6
  6.7 0.1 stack.44.ids_ref
  6.8 0.0 copy-done
  6.8 0.6 copy-done.6
  7.4 1.8 %shard_map.129 = bf16[16,2,48,96]{3,2,1,0:T(8,128)(2,1)} custom-call(s32[5]{0:T(128)S(1)} %stack.44.ids_ref, bf16[2,512,512]{2,1,0:T(8,128)(2,1)S(1)} %copy-done, bf16[2,8,512]{2,1,0:T(8,128)(2,1)S(1)} %copy-done.6, bf16[2,2,2,96,128]{4,3,2,1,0:T(8,128)(2,1)S(1)} %pad.4.columns_ref.refs_0_), custom_call_target="tpu_custom_call" | custom-call | tf_op jit(solution)/shard_map/pallas_call | solution.py:590
  9.1 0.0 copy-start.5
  9.1 4.1 %all-to-all-start = ((bf16[32,48,96]{2,1,0:T(8,128)(2,1)}), bf16[32,48,96]{2,1,0:T(8,128)(2,1)S(1)}, u32[]{:S(2)}, u32[]{:S(2)}) async-start(bf16[32,48,96]{2,1,0:T(8,128)(2,1)} %bitcast.9), calls=%async_computation | async-start | bytes 786432 | tf_op jit(solution)/shard_map/all_to_all | solution.py:628
  13.2 0.0 collective-permute-done
  13.3 0.0 copy-start.3
  13.3 0.0 copy-start.4
  13.3 0.0 copy-start.1
  13.3 0.0 copy-start.2
  13.3 0.0 copy-start.7
  13.4 4.4 %collective-permute-start.2 = (bf16[2,2,2,96,128]{4,3,2,1,0:T(8,128)(2,1)S(1)}, bf16[2,2,2,96,128]{4,3,2,1,0:T(8,128)(2,1)S(1)}, u32[]{:S(2)}, u32[]{:S(2)}) collective-permute-start(bf16[2,2,2,96,128]{4,3,2,1,0:T(8,128)(2,1)S(1)} %maximum_select_fusion), channel_id=1, source_target_pairs={{0,30},{2,4},{4,2},{6,8},{8,6},{10,12},{12,10},{14,16},{16,14},{18... | collective-permute-start | bytes 589832 | tf_op jit(solution)/shard_map/ppermute | solution.py:621
  17.8 0.0 collective-permute-start.1
  17.8 9.7 %collective-permute-done.2.refs_2_ = bf16[2,2,2,96,128]{4,3,2,1,0:T(8,128)(2,1)S(1)} collective-permute-done((bf16[2,2,2,96,128]{4,3,2,1,0:T(8,128)(2,1)S(1)}, bf16[2,2,2,96,128]{4,3,2,1,0:T(8,128)(2,1)S(1)}, u32[]{:S(2)}, u32[]{:S(2)}) %collective-permute-start.2) | collective-permute-done | bytes 196640 | tf_op jit(solution)/shard_map/ppermute | solution.py:621
  27.4 0.0 collective-permute-done.1.refs_1_
  27.4 0.0 all-to-all-done
  27.5 0.0 copy-done.5
  27.5 0.0 copy-done.3
  27.5 0.0 copy-done.4
  27.5 0.0 copy-done.1
  27.5 0.0 copy-done.2
  27.5 0.0 copy-done.7
  27.5 4.9 %shard_map.130 = (bf16[96,1152]{1,0:T(8,128)(2,1)S(1)}, bf16[96,1152]{1,0:T(8,128)(2,1)S(1)}, f32[4,224,96]{2,1,0:T(8,128)S(1)}, bf16[4,224,96]{2,1,0:T(8,128)(2,1)S(1)}) custom-call(s32[5]{0:T(128)S(1)} %stack.44.ids_ref, bf16[2,2,2,96,128]{4,3,2,1,0:T(8,128)(2,1)S(1)} %pad.4.columns_ref.refs_0_, ...), custom_call_target="tpu_custom_call" | custom-call | tf_op jit(solution)/shard_map/pallas_call | solution.py:590
  32.4 1.4 %collective-permute-start.3 = (bf16[4,224,96]{2,1,0:T(8,128)(2,1)S(1)}, bf16[4,224,96]{2,1,0:T(8,128)(2,1)S(1)}, u32[]{:S(2)}, u32[]{:S(2)}) collective-permute-start(bf16[4,224,96]{2,1,0:T(8,128)(2,1)S(1)} %get-tuple-element.22), channel_id=1, source_target_pairs={{0,2},{1,3},{2,0},{3,1},{4,6},{5,7},{6,4},{7,5},{8,10},{9,11},{10,... | collective-permute-start | bytes 516104 | tf_op jit(solution)/shard_map/ppermute | solution.py:638
  33.8 1.1 %collective-permute-done.3 = bf16[4,224,96]{2,1,0:T(8,128)(2,1)S(1)} collective-permute-done((bf16[4,224,96]{2,1,0:T(8,128)(2,1)S(1)}, bf16[4,224,96]{2,1,0:T(8,128)(2,1)S(1)}, u32[]{:S(2)}, u32[]{:S(2)}) %collective-permute-start.3) | collective-permute-done | bytes 172064 | tf_op jit(solution)/shard_map/ppermute | solution.py:638
  35.0 0.1 fusion.4
  35.1 1.6 %collective-permute-start.6 = (bf16[224,96]{1,0:T(8,128)(2,1)S(1)}, bf16[224,96]{1,0:T(8,128)(2,1)S(1)}, u32[]{:S(2)}, u32[]{:S(2)}) collective-permute-start(bf16[224,96]{1,0:T(8,128)(2,1)S(1)} %get-tuple-element.36), channel_id=1, source_target_pairs={{0,5},{1,4},{2,7},{3,6},{4,1},{5,0},{6,3},{7,2},{8,13},{9,12},{10,... | collective-permute-start | bytes 129032 | tf_op jit(solution)/shard_map/ppermute | solution.py:638
  36.6 1.1 %collective-permute-start.5 = (bf16[224,96]{1,0:T(8,128)(2,1)S(1)}, bf16[224,96]{1,0:T(8,128)(2,1)S(1)}, u32[]{:S(2)}, u32[]{:S(2)}) collective-permute-start(bf16[224,96]{1,0:T(8,128)(2,1)S(1)} %get-tuple-element.37), channel_id=1, source_target_pairs={{0,4},{1,5},{2,6},{3,7},{4,0},{5,1},{6,2},{7,3},{8,12},{9,13},{10,... | collective-permute-start | bytes 129032 | tf_op jit(solution)/shard_map/ppermute | solution.py:638
  37.7 0.9 %collective-permute-start.4 = (bf16[224,96]{1,0:T(8,128)(2,1)S(1)}, bf16[224,96]{1,0:T(8,128)(2,1)S(1)}, u32[]{:S(2)}, u32[]{:S(2)}) collective-permute-start(bf16[224,96]{1,0:T(8,128)(2,1)S(1)} %get-tuple-element.38), channel_id=1, source_target_pairs={{0,1},{1,0},{2,3},{3,2},{4,5},{5,4},{6,7},{7,6},{8,9},{9,8},{10,11... | collective-permute-start | bytes 129032 | tf_op jit(solution)/shard_map/ppermute | solution.py:638
  38.6 3.1 %shard_map.131 = (bf16[96,2,2,96]{3,2,1,0:T(2,128)(2,1)}, bf16[96,2,2,96]{3,2,1,0:T(2,128)(2,1)}) custom-call(s32[5]{0:T(128)S(1)} %stack.44.ids_ref, bf16[96,1152]{1,0:T(8,128)(2,1)S(1)} %get-tuple-element.23.hidden_ref, bf16[96,1152]{1,0:T(8,128)(2,1)S(1)} %get-tuple-element.24.pre_grad_ref, bf16[864,96]{1,0:T(8,128)(2,1)S(1)} %bitcast.49, ...), custom_call_target="tpu_custom_call" | custom-call | tf_op jit(solution)/shard_map/pallas_call | solution.py:590
  41.8 0.0 collective-permute-done.6
  41.8 0.0 collective-permute-done.5
  41.8 0.1 collective-permute-done.4
  41.9 1.0 %collective-permute-start.9 = (bf16[224,96]{1,0:T(8,128)(2,1)S(1)}, bf16[224,96]{1,0:T(8,128)(2,1)S(1)}, u32[]{:S(2)}, u32[]{:S(2)}) collective-permute-start(bf16[224,96]{1,0:T(8,128)(2,1)S(1)} %fusion.2), channel_id=1, source_target_pairs={{0,24},{1,25},{2,26},{3,27},{4,28},{5,29},{6,30},{7,31},{8,16},{9,... | collective-permute-start | bytes 129032 | tf_op jit(solution)/shard_map/ppermute | solution.py:638
  42.9 1.4 %collective-permute-start.8 = (bf16[224,96]{1,0:T(8,128)(2,1)S(1)}, bf16[224,96]{1,0:T(8,128)(2,1)S(1)}, u32[]{:S(2)}, u32[]{:S(2)}) collective-permute-start(bf16[224,96]{1,0:T(8,128)(2,1)S(1)} %fusion.2), channel_id=1, source_target_pairs={{0,16},{1,17},{2,18},{3,19},{4,20},{5,21},{6,22},{7,23},{8,24},{9,... | collective-permute-start | bytes 129032 | tf_op jit(solution)/shard_map/ppermute | solution.py:638
  44.3 2.1 %collective-permute-start.7 = (bf16[224,96]{1,0:T(8,128)(2,1)S(1)}, bf16[224,96]{1,0:T(8,128)(2,1)S(1)}, u32[]{:S(2)}, u32[]{:S(2)}) collective-permute-start(bf16[224,96]{1,0:T(8,128)(2,1)S(1)} %fusion.2), channel_id=1, source_target_pairs={{0,8},{1,9},{2,10},{3,11},{4,12},{5,13},{6,14},{7,15},{8,0},{9,1},... | collective-permute-start | bytes 129032 | tf_op jit(solution)/shard_map/ppermute | solution.py:638
  46.3 2.2 %collective-permute-done.9 = bf16[224,96]{1,0:T(8,128)(2,1)S(1)} collective-permute-done((bf16[224,96]{1,0:T(8,128)(2,1)S(1)}, bf16[224,96]{1,0:T(8,128)(2,1)S(1)}, u32[]{:S(2)}, u32[]{:S(2)}) %collective-permute-start.9) | collective-permute-done | bytes 43040 | tf_op jit(solution)/shard_map/ppermute | solution.py:638
  48.6 0.9 %collective-permute-done.8 = bf16[224,96]{1,0:T(8,128)(2,1)S(1)} collective-permute-done((bf16[224,96]{1,0:T(8,128)(2,1)S(1)}, bf16[224,96]{1,0:T(8,128)(2,1)S(1)}, u32[]{:S(2)}, u32[]{:S(2)}) %collective-permute-start.8) | collective-permute-done | bytes 43040 | tf_op jit(solution)/shard_map/ppermute | solution.py:638
  49.5 0.0 collective-permute-done.7
  49.5 1.6 %collective-permute-start.12 = (bf16[224,96]{1,0:T(8,128)(2,1)S(1)}, bf16[224,96]{1,0:T(8,128)(2,1)S(1)}, u32[]{:S(2)}, u32[]{:S(2)}) collective-permute-start(bf16[224,96]{1,0:T(8,128)(2,1)S(1)} %add_convert_fusion), channel_id=1, source_target_pairs={{0,5},{1,4},{2,7},{3,6},{4,1},{5,0},{6,3},{7,2},{8,13},{9,12},{10,... | collective-permute-start | bytes 129032 | tf_op jit(solution)/shard_map/ppermute | solution.py:638
  51.1 1.3 %collective-permute-start.11 = (bf16[224,96]{1,0:T(8,128)(2,1)S(1)}, bf16[224,96]{1,0:T(8,128)(2,1)S(1)}, u32[]{:S(2)}, u32[]{:S(2)}) collective-permute-start(bf16[224,96]{1,0:T(8,128)(2,1)S(1)} %add_convert_fusion), channel_id=1, source_target_pairs={{0,4},{1,5},{2,6},{3,7},{4,0},{5,1},{6,2},{7,3},{8,12},{9,13},{10,... | collective-permute-start | bytes 129032 | tf_op jit(solution)/shard_map/ppermute | solution.py:638
  52.4 0.7 %collective-permute-start.10 = (bf16[224,96]{1,0:T(8,128)(2,1)S(1)}, bf16[224,96]{1,0:T(8,128)(2,1)S(1)}, u32[]{:S(2)}, u32[]{:S(2)}) collective-permute-start(bf16[224,96]{1,0:T(8,128)(2,1)S(1)} %add_convert_fusion), channel_id=1, source_target_pairs={{0,1},{1,0},{2,3},{3,2},{4,5},{5,4},{6,7},{7,6},{8,9},{9,8},{10,11... | collective-permute-start | bytes 129032 | tf_op jit(solution)/shard_map/ppermute | solution.py:638
  53.1 2.1 %collective-permute-done.12 = bf16[224,96]{1,0:T(8,128)(2,1)S(1)} collective-permute-done((bf16[224,96]{1,0:T(8,128)(2,1)S(1)}, bf16[224,96]{1,0:T(8,128)(2,1)S(1)}, u32[]{:S(2)}, u32[]{:S(2)}) %collective-permute-start.12) | collective-permute-done | bytes 43040 | tf_op jit(solution)/shard_map/ppermute | solution.py:638
  55.1 0.4 collective-permute-done.11
  55.5 1.1 %collective-permute-done.10 = bf16[224,96]{1,0:T(8,128)(2,1)S(1)} collective-permute-done((bf16[224,96]{1,0:T(8,128)(2,1)S(1)}, bf16[224,96]{1,0:T(8,128)(2,1)S(1)}, u32[]{:S(2)}, u32[]{:S(2)}) %collective-permute-start.10) | collective-permute-done | bytes 43040 | tf_op jit(solution)/shard_map/ppermute | solution.py:638
  56.6 0.1 pad_maximum_fusion.mine_ref
  56.6 0.1 collective-permute-start.13
  56.7 1.5 %collective-permute-done.13.theirs_ref = bf16[4,224,96]{2,1,0:T(8,128)(2,1)S(1)} collective-permute-done((bf16[4,224,96]{2,1,0:T(8,128)(2,1)S(1)}, bf16[4,224,96]{2,1,0:T(8,128)(2,1)S(1)}, u32[]{:S(2)}, u32[]{:S(2)}) %collective-permute-start.13) | collective-permute-done | bytes 172064 | tf_op jit(solution)/shard_map/ppermute | solution.py:638
  58.2 1.6 %shard_map.132 = (f32[864,96]{1,0:T(8,128)}, f32[864,96]{1,0:T(8,128)}) custom-call(s32[5]{0:T(128)S(1)} %stack.44.ids_ref, bf16[4,224,96]{2,1,0:T(8,128)(2,1)S(1)} %pad_maximum_fusion.mine_ref, bf16[4,224,96]{2,1,0:T(8,128)(2,1)S(1)} %collective-permute-done.13.theirs_ref), custom_call_target="tpu_custom_call" | custom-call | tf_op jit(solution)/shard_map/pallas_call | solution.py:590
  (8 shorter events, 0.3 us)
Async XLA Ops:
  0.6 6.2 %copy-start = (bf16[2,512,512]{2,1,0:T(8,128)(2,1)S(1)}, bf16[2,512,512]{2,1,0:T(8,128)(2,1)}, u32[]{:S(2)}) copy-start(bf16[2,512,512]{2,1,0:T(8,128)(2,1)} %constant.40.clone.table_ref) | copy-start | bytes 3145732
  1.8 11.4 %collective-permute-start = (bf16[2,2,96,128]{3,2,1,0:T(8,128)(2,1)S(1)}, bf16[2,2,96,128]{3,2,1,0:T(8,128)(2,1)S(1)}, u32[]{:S(2)}, u32[]{:S(2)}) collective-permute-start(bf16[2,2,96,128]{3,2,1,0:T(8,128)(2,1)S(1)} %fusion.3), channel_id=1, source_target_pairs={{30,31},{31,30},{1,0},{0,1}} | collective-permute-start | bytes 294920 | tf_op jit(solution)/shard_map/ppermute | solution.py:606
  6.7 0.7 %copy-start.6 = (bf16[2,8,512]{2,1,0:T(8,128)(2,1)S(1)}, bf16[2,8,512]{2,1,0:T(8,128)(2,1)}, u32[]{:S(2)}) copy-start(bf16[2,8,512]{2,1,0:T(8,128)(2,1)} %constant.41.clone.poles_ref) | copy-start | bytes 49156
  9.1 18.3 %copy-start.5 = (bf16[768,128]{1,0:T(8,128)(2,1)S(1)}, bf16[768,128]{1,0:T(8,128)(2,1)}, u32[]{:S(2)}) copy-start(bf16[768,128]{1,0:T(8,128)(2,1)} %constant.44.clone.refs_6_) | copy-start | bytes 589828
  9.1 18.3 %all-to-all-start = ((bf16[32,48,96]{2,1,0:T(8,128)(2,1)}), bf16[32,48,96]{2,1,0:T(8,128)(2,1)S(1)}, u32[]{:S(2)}, u32[]{:S(2)}) async-start(bf16[32,48,96]{2,1,0:T(8,128)(2,1)} %bitcast.9), calls=%async_computation | async-start | bytes 786432 | tf_op jit(solution)/shard_map/all_to_all | solution.py:628
  13.3 14.2 %copy-start.3 = (bf16[256,512]{1,0:T(8,128)(2,1)S(1)}, bf16[256,512]{1,0:T(8,128)(2,1)}, u32[]{:S(2)}) copy-start(bf16[256,512]{1,0:T(8,128)(2,1)} %constant.43.clone.refs_5_) | copy-start | bytes 786436
  13.3 14.2 %copy-start.4 = (bf16[256,512]{1,0:T(8,128)(2,1)S(1)}, bf16[256,512]{1,0:T(8,128)(2,1)}, u32[]{:S(2)}) copy-start(bf16[256,512]{1,0:T(8,128)(2,1)} %constant.42.clone.refs_4_) | copy-start | bytes 786436
  13.3 14.2 %copy-start.1 = (bf16[3,3,96,96]{3,2,1,0:T(8,128)(2,1)S(1)}, bf16[3,3,96,96]{3,2,1,0:T(8,128)(2,1)}, u32[]{:S(2)}) copy-start(bf16[3,3,96,96]{3,2,1,0:T(8,128)(2,1)} %param.12) | copy-start | bytes 497668
  13.3 14.2 %copy-start.2 = (bf16[3,3,96,96]{3,2,1,0:T(8,128)(2,1)S(1)}, bf16[3,3,96,96]{3,2,1,0:T(8,128)(2,1)}, u32[]{:S(2)}) copy-start(bf16[3,3,96,96]{3,2,1,0:T(8,128)(2,1)} %param.13) | copy-start | bytes 497668
  13.3 14.2 %copy-start.7 = (bf16[32,128]{1,0:T(8,128)(2,1)S(1)}, bf16[32,128]{1,0:T(8,128)(2,1)}, u32[]{:S(2)}) copy-start(bf16[32,128]{1,0:T(8,128)(2,1)} %constant.45.clone.refs_7_) | copy-start | bytes 24580
  13.4 14.1 %collective-permute-start.2 = (bf16[2,2,2,96,128]{4,3,2,1,0:T(8,128)(2,1)S(1)}, bf16[2,2,2,96,128]{4,3,2,1,0:T(8,128)(2,1)S(1)}, u32[]{:S(2)}, u32[]{:S(2)}) collective-permute-start(bf16[2,2,2,96,128]{4,3,2,1,0:T(8,128)(2,1)S(1)} %maximum_select_fusion), channel_id=1, source_target_pairs={{0,30},{2,4},{4,2},{6,8},{8,6},{10,12},{12,10},{14,16},{16,14},{18... | collective-permute-start | bytes 589832 | tf_op jit(solution)/shard_map/ppermute | solution.py:621
  17.8 9.7 %collective-permute-start.1 = (bf16[2,2,2,96,128]{4,3,2,1,0:T(8,128)(2,1)S(1)}, bf16[2,2,2,96,128]{4,3,2,1,0:T(8,128)(2,1)S(1)}, u32[]{:S(2)}, u32[]{:S(2)}) collective-permute-start(bf16[2,2,2,96,128]{4,3,2,1,0:T(8,128)(2,1)S(1)} %pad.4.columns_ref.refs_0_), channel_id=1, source_target_pairs={{0,2},{2,0},{4,6},{6,4},{8,10},{10,8},{12,14},{14,12},{16,18},{18,... | collective-permute-start | bytes 589832 | tf_op jit(solution)/shard_map/ppermute | solution.py:620
  32.4 2.5 %collective-permute-start.3 = (bf16[4,224,96]{2,1,0:T(8,128)(2,1)S(1)}, bf16[4,224,96]{2,1,0:T(8,128)(2,1)S(1)}, u32[]{:S(2)}, u32[]{:S(2)}) collective-permute-start(bf16[4,224,96]{2,1,0:T(8,128)(2,1)S(1)} %get-tuple-element.22), channel_id=1, source_target_pairs={{0,2},{1,3},{2,0},{3,1},{4,6},{5,7},{6,4},{7,5},{8,10},{9,11},{10,... | collective-permute-start | bytes 516104 | tf_op jit(solution)/shard_map/ppermute | solution.py:638
  35.1 6.7 %collective-permute-start.6 = (bf16[224,96]{1,0:T(8,128)(2,1)S(1)}, bf16[224,96]{1,0:T(8,128)(2,1)S(1)}, u32[]{:S(2)}, u32[]{:S(2)}) collective-permute-start(bf16[224,96]{1,0:T(8,128)(2,1)S(1)} %get-tuple-element.36), channel_id=1, source_target_pairs={{0,5},{1,4},{2,7},{3,6},{4,1},{5,0},{6,3},{7,2},{8,13},{9,12},{10,... | collective-permute-start | bytes 129032 | tf_op jit(solution)/shard_map/ppermute | solution.py:638
  36.6 5.2 %collective-permute-start.5 = (bf16[224,96]{1,0:T(8,128)(2,1)S(1)}, bf16[224,96]{1,0:T(8,128)(2,1)S(1)}, u32[]{:S(2)}, u32[]{:S(2)}) collective-permute-start(bf16[224,96]{1,0:T(8,128)(2,1)S(1)} %get-tuple-element.37), channel_id=1, source_target_pairs={{0,4},{1,5},{2,6},{3,7},{4,0},{5,1},{6,2},{7,3},{8,12},{9,13},{10,... | collective-permute-start | bytes 129032 | tf_op jit(solution)/shard_map/ppermute | solution.py:638
  37.7 4.2 %collective-permute-start.4 = (bf16[224,96]{1,0:T(8,128)(2,1)S(1)}, bf16[224,96]{1,0:T(8,128)(2,1)S(1)}, u32[]{:S(2)}, u32[]{:S(2)}) collective-permute-start(bf16[224,96]{1,0:T(8,128)(2,1)S(1)} %get-tuple-element.38), channel_id=1, source_target_pairs={{0,1},{1,0},{2,3},{3,2},{4,5},{5,4},{6,7},{7,6},{8,9},{9,8},{10,11... | collective-permute-start | bytes 129032 | tf_op jit(solution)/shard_map/ppermute | solution.py:638
  41.9 6.7 %collective-permute-start.9 = (bf16[224,96]{1,0:T(8,128)(2,1)S(1)}, bf16[224,96]{1,0:T(8,128)(2,1)S(1)}, u32[]{:S(2)}, u32[]{:S(2)}) collective-permute-start(bf16[224,96]{1,0:T(8,128)(2,1)S(1)} %fusion.2), channel_id=1, source_target_pairs={{0,24},{1,25},{2,26},{3,27},{4,28},{5,29},{6,30},{7,31},{8,16},{9,... | collective-permute-start | bytes 129032 | tf_op jit(solution)/shard_map/ppermute | solution.py:638
  42.9 6.6 %collective-permute-start.8 = (bf16[224,96]{1,0:T(8,128)(2,1)S(1)}, bf16[224,96]{1,0:T(8,128)(2,1)S(1)}, u32[]{:S(2)}, u32[]{:S(2)}) collective-permute-start(bf16[224,96]{1,0:T(8,128)(2,1)S(1)} %fusion.2), channel_id=1, source_target_pairs={{0,16},{1,17},{2,18},{3,19},{4,20},{5,21},{6,22},{7,23},{8,24},{9,... | collective-permute-start | bytes 129032 | tf_op jit(solution)/shard_map/ppermute | solution.py:638
  44.3 5.2 %collective-permute-start.7 = (bf16[224,96]{1,0:T(8,128)(2,1)S(1)}, bf16[224,96]{1,0:T(8,128)(2,1)S(1)}, u32[]{:S(2)}, u32[]{:S(2)}) collective-permute-start(bf16[224,96]{1,0:T(8,128)(2,1)S(1)} %fusion.2), channel_id=1, source_target_pairs={{0,8},{1,9},{2,10},{3,11},{4,12},{5,13},{6,14},{7,15},{8,0},{9,1},... | collective-permute-start | bytes 129032 | tf_op jit(solution)/shard_map/ppermute | solution.py:638
  49.5 5.6 %collective-permute-start.12 = (bf16[224,96]{1,0:T(8,128)(2,1)S(1)}, bf16[224,96]{1,0:T(8,128)(2,1)S(1)}, u32[]{:S(2)}, u32[]{:S(2)}) collective-permute-start(bf16[224,96]{1,0:T(8,128)(2,1)S(1)} %add_convert_fusion), channel_id=1, source_target_pairs={{0,5},{1,4},{2,7},{3,6},{4,1},{5,0},{6,3},{7,2},{8,13},{9,12},{10,... | collective-permute-start | bytes 129032 | tf_op jit(solution)/shard_map/ppermute | solution.py:638
  51.1 4.4 %collective-permute-start.11 = (bf16[224,96]{1,0:T(8,128)(2,1)S(1)}, bf16[224,96]{1,0:T(8,128)(2,1)S(1)}, u32[]{:S(2)}, u32[]{:S(2)}) collective-permute-start(bf16[224,96]{1,0:T(8,128)(2,1)S(1)} %add_convert_fusion), channel_id=1, source_target_pairs={{0,4},{1,5},{2,6},{3,7},{4,0},{5,1},{6,2},{7,3},{8,12},{9,13},{10,... | collective-permute-start | bytes 129032 | tf_op jit(solution)/shard_map/ppermute | solution.py:638
  52.4 4.2 %collective-permute-start.10 = (bf16[224,96]{1,0:T(8,128)(2,1)S(1)}, bf16[224,96]{1,0:T(8,128)(2,1)S(1)}, u32[]{:S(2)}, u32[]{:S(2)}) collective-permute-start(bf16[224,96]{1,0:T(8,128)(2,1)S(1)} %add_convert_fusion), channel_id=1, source_target_pairs={{0,1},{1,0},{2,3},{3,2},{4,5},{5,4},{6,7},{7,6},{8,9},{9,8},{10,11... | collective-permute-start | bytes 129032 | tf_op jit(solution)/shard_map/ppermute | solution.py:638
  56.6 1.6 %collective-permute-start.13 = (bf16[4,224,96]{2,1,0:T(8,128)(2,1)S(1)}, bf16[4,224,96]{2,1,0:T(8,128)(2,1)S(1)}, u32[]{:S(2)}, u32[]{:S(2)}) collective-permute-start(bf16[4,224,96]{2,1,0:T(8,128)(2,1)S(1)} %pad_maximum_fusion.mine_ref), channel_id=1, source_target_pairs={{0,2},{1,3},{2,0},{3,1},{4,6},{5,7},{6,4},{7,5},{8,10},{9,11},{10,... | collective-permute-start | bytes 516104 | tf_op jit(solution)/shard_map/ppermute | solution.py:638

commit v3 on v2

--- a/solution.py
+++ b/solution.py
@@ -29,107 +29,113 @@
         self.channels = block[0] * mesh_shape["sub"]
         self.own = block[0]
         w = self.cols
+        assert w == 2
         self.reach = w + 4
-        self.line = (0, self.reach)
-        self.row = (2 * self.reach, 2 * self.reach + w)
-        self.cells = up_to(2 * self.reach + 2 * w, 16)
-        self.poles = up_to(2 * 3 * self.stacks, 16)
-        self.block = 2 * self.cells + self.poles
+        self.cells = 2 * self.reach
+        self.block = 2 * self.cells
         self.kinds = 2 if self.stacks > 1 else 1
         self.segments = self.stacks * (w + 2) + 1
-        self.rim = up_to(2 * self.stacks * 8, 1)
         self.near = 2
         self.mid = 2 * self.faces
         self.far = self.tiles // 4
         self.terms = 2 * 9 * self.channels
-        self.piece = up_to(-(-self.terms // (self.near * self.mid)), 16)
+        self.wide = self.channels
+        rest = -self.channels % 128
+        self.folds = 1
+        if rest and self.channels % rest == 0 and self.terms % (8 * (self.channels // rest + 1)) == 0:
+            self.folds = self.channels // rest + 1
+            self.wide = self.channels + rest
+        self.fold_rows = self.terms // self.folds
+        packed = self.fold_rows * max(self.folds - 1, 1)
+        self.piece = up_to(-(-packed // (self.near * self.mid)), 16)
 
     def segment(self, stack, slot):
         if 1 <= slot <= self.cols:
             return stack * self.cols + slot - 1
         return self.stacks * self.cols + 2 * stack + (1 if slot else 0)
 
-    def send_tables(self):
-        t, k, c = self.tiles, self.kinds, self.cells
+    def spot(self, depth, e):
+        return depth * self.reach + e
+
+    def send_table(self):
+        t, k, c = self.tiles, self.kinds, self.block
         g, w, n = self.stacks, self.cols, self.lanes
         high = self.height - 1
-        table = np.zeros((2, t, k, c, g, w, n), np.float32)
-        poles = np.zeros((2, self.poles // 2, g, w, n), np.float32)
+        table = np.full((3, t, k, c), -1, np.int32)
         for dest in range(t):
             for kind in range(k):
                 same = kind == 0 and k == 2
                 from_a = 1 if same else 0
                 from_b = 0 if same else g - 1
-                for e in range(self.reach):
-                    for depth in range(2):
-                        spot = self.line[depth] + e
+
+                def cell(stack, col, row):
+                    return (stack * w + col) * n + row
+
+                for depth in range(2):
+                    for e in range(self.reach):
+                        at = self.spot(depth, e)
                         row = w * dest - 2 + e
                         if 0 <= row:
-                            table[0, dest, kind, spot, from_a, depth, row] = 1
+                            table[0, dest, kind, at] = cell(from_a, depth, row)
                         row = 2 * self.side + w * dest - 2 + e
                         if row <= high:
-                            table[1, dest, kind, spot, from_b, w - 1 - depth, row] = 1
-                for e in range(w):
-                    for depth in range(2):
-                        spot = self.row[depth] + e
+                            table[2, dest, kind, at] = cell(from_b, w - 1 - depth, row)
+                    for e in range(w):
                         if dest == 0:
-                            table[:, dest, kind, spot, from_b, e, depth] = 1
+                            table[:2, dest, kind, self.spot(depth, e)] = cell(from_b, e, depth)
                         if dest == t - 1:
-                            table[:, dest, kind, spot, from_a, e, high - depth] = 1
-        for stack in range(g):
-            for i, (col, row) in enumerate(((0, 0), (1, 0), (0, 1))):
-                poles[0, 3 * stack + i, stack, col, row] = 1
-                poles[1, 3 * stack + i, stack, w - 1 - col, high - row] = 1
-        return (
-            jnp.asarray(table.reshape(2, t * k * c, g * w * n), BF16),
-            jnp.asarray(poles.reshape(2, -1, g * w * n), BF16),
-        )
+                            at = self.spot(depth, w + 2 + e)
+                            table[1:, dest, kind, at] = cell(from_a, e, high - depth)
+        return jnp.asarray(table.reshape(3, 1, -1))
 
     def take_tables(self):
-        t, c, w, n = self.tiles, self.cells, self.cols, self.lanes
-        from_a = np.zeros((t, c, 4, n), np.float32)
-        from_b = np.zeros((t, c, 4, n), np.float32)
+        t, c, w, n = self.tiles, self.block, self.cols, self.lanes
+        from_a = np.zeros((t, 2, self.cells, 2, 4, n), np.float32)
+        from_b = np.zeros((t, 2, self.cells, 2, 4, n), np.float32)
         for depth in range(2):
-            for src in range(t):
-                for e in range(w):
-                    spot = self.row[depth] + e
-                    from_a[src, spot, depth, 2 * self.side + src * w + e] = 1
-                    from_b[src, spot, depth, src * w + e] = 1
-            for e in range(self.reach):
-                from_a[0, self.line[depth] + e, 2 + depth, e] = 1
-                from_b[t - 1, self.line[depth] + e, 2 + depth, 8 + e] = 1
+            for k in range(2):
+                for src in range(t):
+                    for e in range(w):
+                        if src > 0:
+                            at = self.spot(depth, w + 2 + e)
+                            from_a[src, k, at, k, depth, 2 * self.side + src * w + e] = 1
+                        if src < t - 1:
+                            from_b[src, k, self.spot(depth, e), k, depth, src * w + e] = 1
+                for e in range(self.reach):
+                    at = self.spot(depth, e)
+                    from_a[0, k, at, k, 2 + depth, e] = 1
+                    from_b[t - 1, k, at, k, 2 + depth, 8 + e] = 1
         ends = np.zeros((self.reach, n, n), np.float32)
         for e in range(self.reach):
             ends[e, 0, e] = 1
             ends[e, self.height - 1, 8 + e] = 1
-        shape = (t * c, 4 * n)
+        shape = (t * c, 8 * n)
         return (
             jnp.asarray(from_a.reshape(shape), BF16),
             jnp.asarray(from_b.reshape(shape), BF16),
             jnp.asarray(ends.reshape(-1, n), BF16),
-            jnp.asarray(np.eye(2 * self.poles, n), BF16),
         )
 
 
-def first_kernel(plan, ids_ref, table_ref, poles_ref, columns_ref, blocks_ref):
-    t, c, g, w = plan.tiles, plan.cells, plan.stacks, plan.cols
+def first_kernel(plan, ids_ref, table_ref, columns_ref, blocks_ref):
+    t, c, g, w = plan.tiles, plan.block, plan.stacks, plan.cols
     face = ids_ref[1]
-    end = jnp.where(ids_ref[0] == plan.tiles - 1, 1, 0)
-    poles = []
-    for k in range(2):
-        flat = jnp.concatenate([columns_ref[i, k, j] for j in range(g) for i in range(w)], axis=1)
-        picked = product(table_ref[end], flat, 1, 1).astype(BF16)
-        picked = picked.reshape(t, plan.kinds, c, flat.shape[0])
-        for dest in range(plan.faces):
-            if plan.kinds == 2:
-                block = jnp.where(face == dest, picked[:, 0], picked[:, 1])
-            else:
-                block = picked[:, 0]
-            blocks_ref[:, dest, k * c : (k + 1) * c, :] = block
-        poles.append(product(poles_ref[end], flat, 1, 1))
-    poles = jnp.concatenate(poles, axis=0).astype(BF16)
+    flat = [
+        jnp.concatenate([columns_ref[i, k, j] for j in range(g) for i in range(w)], axis=1)
+        for k in range(2)
+    ]
+    wanted = table_ref[ids_ref[5]]
+    cell = lax.broadcasted_iota(jnp.int32, (flat[0].shape[1], wanted.shape[1]), 0)
+    pick = jnp.where(cell == wanted, 1.0, 0.0).astype(BF16)
+    picked = [jnp.transpose(product(x, pick, 1, 0)) for x in flat]
+    both = picked[0] + pltpu.roll(picked[1], plan.cells, 0)
+    both = both.reshape(t, plan.kinds, c, both.shape[-1])
     for dest in range(plan.faces):
-        blocks_ref[:, dest, 2 * c :, :] = jnp.broadcast_to(poles[None], (t,) + poles.shape)
+        if plan.kinds == 2:
+            block = jnp.where(face == dest, both[:, 0], both[:, 1])
+        else:
+            block = both[:, 0]
+        blocks_ref[:, dest] = block.astype(BF16)
 
 
 def product(x, y, x_dim, y_dim):
@@ -140,43 +146,56 @@
     return pltpu.roll(x, by % x.shape[1], 1)
 
 
-def surroundings(plan, ids_ref, k, columns_ref, inner_ref, outer_ref, got_ref, tables):
-    w, n, c = plan.cols, plan.lanes, plan.cells
+def seam_cells(plan, ids_ref, got_ref, tab_a, tab_b):
+    face = ids_ref[1]
+    after = lax.rem(face + 1, plan.faces)
+    before = lax.rem(face + plan.faces - 1, plan.faces)
+    result = []
+    for g in range(plan.stacks):
+        face_a = face if g < plan.stacks - 1 else after
+        face_b = face if g > 0 else before
+        pair = []
+        for at, table in ((face_a, tab_a), (face_b, tab_b)):
+            rows = got_ref[:, at].astype(F32)
+            rows = rows.reshape(plan.tiles * plan.block, rows.shape[-1])
+            pair.append(product(rows.astype(BF16), table[...], 0, 0))
+        result.append(pair)
+    return result
+
+
+def surroundings(plan, ids_ref, k, columns_ref, inner_ref, outer_ref, across_ref, seams_of, tab_ends):
+    w, n, side = plan.cols, plan.lanes, plan.side
     high, g_count = plan.height, plan.stacks
     first = ids_ref[0] == 0
     last = ids_ref[0] == plan.tiles - 1
     even = lax.rem(ids_ref[0], 2) == 0
-    face = ids_ref[1]
-    after = lax.rem(face + 1, plan.faces)
-    before = lax.rem(face + plan.faces - 1, plan.faces)
-    across = lax.rem(face + 2 // g_count, plan.faces)
-    tab_a, tab_b, tab_ends, tab_eye = tables
-    pole_rows = [got_ref[at, across, 2 * c :, :] for at in (0, plan.tiles - 1)]
-    poles = product(jnp.concatenate(pole_rows, axis=0), tab_eye, 0, 0)
     shape = (plan.channels, n)
     lane = lax.broadcasted_iota(jnp.int32, shape, 1)
     stacks = []
     line, deep, ends = [jnp.zeros(shape, F32) for _ in range(3)]
     for g in range(g_count):
-        face_a = face if g < g_count - 1 else after
-        face_b = face if g > 0 else before
-        seams = []
-        for at, table in ((face_a, tab_a), (face_b, tab_b)):
-            rows = got_ref[:, at, k * c : (k + 1) * c, :]
-            rows = rows.reshape(plan.tiles * c, rows.shape[-1])
-            out = product(rows, table, 0, 0)
-            seams.append([out[:, i * n : (i + 1) * n] for i in range(4)])
+        start = 4 * k * n
+        seams = [
+            [x[:, start + i * n : start + (i + 1) * n] for i in range(4)] for x in seams_of[g]
+        ]
         line += shift(seams[0][2] + seams[1][2], 16 * g)
         deep += shift(seams[0][3] + seams[1][3], 16 * g)
         raw = [jnp.where(even, outer_ref[i, k, g], inner_ref[i, k, g]) for i in range(2)]
         raw += [columns_ref[i, k, g] for i in range(w)]
         raw += [jnp.where(even, inner_ref[i, k, g], outer_ref[i, k, g]) for i in range(2)]
-        ends += shift(product(jnp.concatenate(raw, axis=1), tab_ends, 1, 0), 16 * g)
+        ends += shift(product(jnp.concatenate(raw, axis=1), tab_ends[...], 1, 0), 16 * g)
         raw = [x.astype(F32) for x in raw]
-        pole = []
-        for at in range(2):
-            base = at * plan.poles + k * (plan.poles // 2) + 3 * g
-            pole.append([poles[:, base + i : base + i + 1] for i in range(3)])
+        for d in range(2):
+            for i in range(2):
+                here = lane == side - 2 + i
+                seams[1][d] = jnp.where(here, shift(raw[i], side - 2 + i - d), seams[1][d])
+                here = lane == 2 * side + i
+                by = 2 * side + i - (high - 1 - d)
+                seams[0][d] = jnp.where(here, shift(raw[w + 2 + i], by), seams[0][d])
+        pole = [across_ref[i, k, g].astype(F32) for i in range(2)]
+        north = [pole[0][:, :1], pole[1][:, :1], pole[0][:, 1:2]]
+        south = [pole[1][:, high - 1 : high], pole[0][:, high - 1 : high]]
+        south.append(pole[1][:, high - 2 : high - 1])
         stacks.append(
             dict(
                 raw=raw,
@@ -184,14 +203,18 @@
                 row_r=seams[0][:2],
                 col_l=[shift(x, plan.side) for x in raw[:2]],
                 col_r=[shift(x, -plan.side) for x in raw[w + 2 :]],
-                north=pole[0],
-                south=pole[1],
+                north=north,
+                south=south,
             )
         )
     spot = lane % 8
+    is_top = (lane % 16) < 8
+    unsent = (first & is_top & (spot < 2)) | (last & jnp.logical_not(is_top) & (spot >= w + 2))
+    line = jnp.where(unsent, 0.0, line)
+    deep = jnp.where(unsent, 0.0, deep)
     ends = jnp.where(first & (spot < 2), 0.0, ends)
     ends = jnp.where(last & (spot >= w + 2), 0.0, ends)
-    rim = dict(line=line, deep=deep, ends=ends, spot=spot, is_top=(lane % 16) < 8)
+    rim = dict(line=line, deep=deep, ends=ends, spot=spot, is_top=is_top)
     return stacks, rim, lane, first, last
 
 
@@ -503,11 +526,15 @@
 
 def middle_kernel(plan, ids_ref, *refs):
     w, n, g_count, c = plan.cols, plan.lanes, plan.stacks, plan.channels
-    around, tables, (w_one, w_two), refs = refs[:4], refs[4:8], refs[8:10], refs[10:]
-    hidden_ref, pre_grad_ref, mine_ref, theirs_ref, fwd_ref, bwd_ref, sums_ref = refs
-    tables = [x[...] for x in tables]
-    wide_forward(plan, surroundings(plan, ids_ref, 0, *around, tables), fwd_ref)
-    wide_backward(plan, surroundings(plan, ids_ref, 1, *around, tables), bwd_ref)
+    around, tables, (w_one, w_two), refs = refs[:5], refs[5:8], refs[8:10], refs[10:]
+    hidden_ref, pre_grad_ref, mine_ref, theirs_ref, fwd_ref, bwd_ref, sums_ref, packed_ref = refs
+    *around, got = around
+    seams = seam_cells(plan, ids_ref, got, *tables[:2])
+    found = [
+        surroundings(plan, ids_ref, k, *around, seams, tables[2]) for k in range(2)
+    ]
+    wide_forward(plan, found[0], fwd_ref)
+    wide_backward(plan, found[1], bwd_ref)
     pre = product(w_one[...], fwd_ref[...], 0, 0)
     grad = product(seam_weights(w_two), bwd_ref[...], 1, 0)
     bend = jnp.tanh(GELU_A * (pre + GELU_B * (pre * pre * pre)))
@@ -542,15 +569,25 @@
     sums_ref[0 : 9 * c, :] = terms
     for i in range(9):
         sums_ref[(9 + i) * c : (10 + i) * c, :] = jnp.transpose(tap[i])
-    rest = sums_ref.shape[0] - 18 * c
-    if rest:
-        sums_ref[18 * c :, :] = jnp.zeros((rest, c), F32)
+    packed_rows = max(plan.folds - 1, 1) * plan.fold_rows
+    shared = (plan.folds - 1) * plan.fold_rows
+    for i in range(max(plan.folds - 1, 1)):
+        at = i * plan.fold_rows
+        block = sums_ref[at : at + plan.fold_rows, :]
+        if plan.folds > 1:
+            rest = plan.wide - c
+            more = sums_ref[shared : shared + plan.fold_rows, i * rest : (i + 1) * rest]
+            block = jnp.concatenate([block, more], axis=1)
+        packed_ref[at : at + plan.fold_rows, :] = block
+    spare = packed_ref.shape[0] - packed_rows
+    if spare:
+        packed_ref[packed_rows:, :] = jnp.zeros((spare, plan.wide), F32)
     near, mid = ids_ref[3], ids_ref[4]
     for d in range(plan.mid):
         spot = jnp.bitwise_xor(mid, d)
         for other, ref in ((0, mine_ref), (1, theirs_ref)):
             at = (jnp.bitwise_xor(near, other) * plan.mid + spot) * plan.piece
-            rows = sums_ref[pl.ds(pl.multiple_of(at, 16), plan.piece), :]
+            rows = packed_ref[pl.ds(pl.multiple_of(at, 16), plan.piece), :]
             ref[d] = rows.astype(ref.dtype)
 
 
@@ -570,13 +607,22 @@
             back_ref[:, g, i, :] = back[:, at : at + plan.height]
 
 
-def sum_kernel(plan, scale, ids_ref, mine_ref, theirs_ref, one_ref, two_ref, sums_ref):
+def sum_kernel(plan, scale, ids_ref, mine_ref, theirs_ref, one_ref, two_ref, packed_ref, sums_ref):
     near, mid = ids_ref[3], ids_ref[4]
     for d in range(plan.mid):
         spot = jnp.bitwise_xor(mid, d)
         for other, ref in ((0, mine_ref), (1, theirs_ref)):
             at = (jnp.bitwise_xor(near, other) * plan.mid + spot) * plan.piece
-            sums_ref[pl.ds(pl.multiple_of(at, 16), plan.piece), :] = ref[d].astype(F32) * scale
+            packed_ref[pl.ds(pl.multiple_of(at, 16), plan.piece), :] = ref[d].astype(F32) * scale
+    c, shared = plan.channels, (plan.folds - 1) * plan.fold_rows
+    more = []
+    for i in range(max(plan.folds - 1, 1)):
+        at = i * plan.fold_rows
+        block = packed_ref[at : at + plan.fold_rows, :]
+        sums_ref[at : at + plan.fold_rows, :] = block[:, :c]
+        more.append(block[:, c:])
+    if plan.folds > 1:
+        sums_ref[shared : shared + plan.fold_rows, :] = jnp.concatenate(more, axis=1)
     rows = one_ref.shape[0]
     one_ref[...] = sums_ref[:rows]
     two_ref[...] = sums_ref[rows : 2 * rows]
@@ -597,12 +643,12 @@
     )(ids, *inputs)
 
 
-def end_stacks(plan, columns):
+def across_faces(plan, columns, step):
     t, f = plan.tiles, plan.faces
     first = lax.axis_index("tile") == 0
-    sent = jnp.where(first, columns[:2, :, 0], columns[plan.cols - 2 :, :, plan.stacks - 1])
-    pairs = [((t - 1) * f + i, (t - 1) * f + (i + 1) % f) for i in range(f)]
-    pairs += [((i + 1) % f, i) for i in range(f)]
+    sent = jnp.where(first, columns[:2], columns[plan.cols - 2 :])
+    pairs = [((t - 1) * f + i, (t - 1) * f + (i + step) % f) for i in range(f)]
+    pairs += [((i + step) % f, i) for i in range(f)]
     return lax.ppermute(sent, BOTH, pairs)
 
 
@@ -613,7 +659,7 @@
     head, tail = columns[:2], columns[plan.cols - 2 :]
     inner = jnp.where(even, tail, head)
     outer = jnp.where(even, head, tail)
-    passed = passed[:, :, None]
+    passed = jnp.where(tile == 0, passed[:, :, :1], passed[:, :, g - 1 :])
     to_last = jnp.concatenate([head[:, :, 1:], passed], axis=2)
     to_first = jnp.concatenate([passed, tail[:, :, : g - 1]], axis=2)
     outer = jnp.where(tile == 0, to_last, jnp.where(tile == t - 1, to_first, outer))
@@ -664,7 +710,8 @@
     tile, face = lax.axis_index("tile"), lax.axis_index("face")
     sub = lax.axis_index("sub")
     mid = ((tile >> 1) & 1) * plan.faces + face
-    ids = jnp.stack([tile, face, sub, tile & 1, mid]).astype(jnp.int32)
+    kind = jnp.where(tile == 0, 0, jnp.where(tile == plan.tiles - 1, 2, 1))
+    ids = jnp.stack([tile, face, sub, tile & 1, mid, kind]).astype(jnp.int32)
     if mesh_shape["sub"] > 1:
         fields = lax.all_gather(fields, "sub", axis=0, tiled=True)
         upstream = lax.all_gather(upstream, "sub", axis=0, tiled=True)
@@ -673,15 +720,13 @@
     columns = jnp.pad(both, ((0, 0),) * 4 + ((0, n - h),))
     blocks_shape = jax.ShapeDtypeStruct((plan.tiles, plan.faces, plan.block, c), BF16)
     (blocks,) = call(
-        functools.partial(first_kernel, plan),
-        ids,
-        [*plan.send_tables(), columns],
-        [blocks_shape],
+        functools.partial(first_kernel, plan), ids, [plan.send_table(), columns], [blocks_shape]
     )
-    passed = end_stacks(plan, columns)
+    passed = across_faces(plan, columns, 1)
+    across = passed if g == 2 else across_faces(plan, columns, 2)
     got = spread_blocks(plan, blocks)
     sent, passed, _ = lax.optimization_barrier((columns, passed, blocks))
-    halo = (*pair_up(plan, sent, passed), got)
+    halo = (*pair_up(plan, sent, passed), across, got)
 
     fwd_one = kernel_one.reshape(9 * c, c)
     bwd_two = kernel_two.reshape(9, c, c)
@@ -691,7 +736,7 @@
     def taps(width):
         return [pltpu.VMEM((9 * c, width), BF16), pltpu.VMEM((21 * c, width), BF16)]
 
-    piece = (plan.mid, plan.piece, c)
+    piece = (plan.mid, plan.piece, plan.wide)
     rows = plan.near * plan.mid * plan.piece
     wide = plan.segments * n
     hidden, pre_grad, mine, theirs = call(
@@ -700,7 +745,7 @@
         [columns, *halo, *plan.take_tables(), fwd_one, bwd_two],
         [jax.ShapeDtypeStruct((c, wide), BF16)] * 2
         + [jax.ShapeDtypeStruct(piece, F32), jax.ShapeDtypeStruct(piece, BF16)],
-        taps(wide) + [pltpu.VMEM((rows, c), F32)],
+        taps(wide) + [pltpu.VMEM((plan.terms, c), F32), pltpu.VMEM((rows, plan.wide), F32)],
     )
     out_shape = jax.ShapeDtypeStruct((own, g, w, h), BF16)
     beside = call(
@@ -717,7 +762,7 @@
         ids,
         [mine, theirs],
         [jax.ShapeDtypeStruct((9 * c, c), F32)] * 2,
-        [pltpu.VMEM((rows, c), F32)],
+        [pltpu.VMEM((rows, plan.wide), F32), pltpu.VMEM((plan.terms, c), F32)],
     )
     grads = []
     for i in range(2):

time: 60.1 us -> 54.9 us (0.913)
  waiting for transfers between devices: 19 us -> 15.3 us
  starting transfers between devices: 26.3 us -> 25 us
  Pallas kernels: 11.4 us -> 12.1 us
  local copies, waits for them, and re-layouts: 1.82 us -> 1.16 us
    ppermute x1, waiting for transfers between devices: 9.69 us -> 0.86 us  [pair_up(): lax.ppermute(outer, 'tile', [(i, (i + 1 ^ 1) - 1 if i else t - 1) for i i...]
    all_to_all x1, waiting for transfers between devices: 0.01 us -> 5.67 us  [spread_blocks(): return lax.all_to_all(flat, BOTH, 0, 0, tiled=True).reshape(blocks.shape)]
    ppermute x11, starting transfers between devices: 13 us -> 11.7 us  [swapped(): return lax.ppermute(x, BOTH, pairs)]
    pallas_call x4, Pallas kernels: 11.4 us -> 12.1 us  [call(): pl.pallas_call(body, out_shape=outs, in_specs=[SMEM] + [VMEM] * len(input...]
  transfers between devices with their start and end apart: 15 -> 15, of which waited for: 9 -> 10; matrix products, arithmetic and copies ran while one was open for 0% -> 0% of each run, Pallas kernels for 8% -> 9%
where the time goes in v3:
time: 54.9 us; the launch traced here: 54.6 us
  starting transfers between devices  25 us (46%)
  waiting for transfers between devices  15.3 us (28%)
  Pallas kernels  12.1 us (22%)
  local copies, waits for them, and re-layouts  1.16 us (2%)
  between operations  0.84 us (2%)
    pallas_call x4, Pallas kernels, call(): pl.pallas_call(body, out_shape=outs, in_specs=[SMEM] + [VMEM] * len(input...  12.1 us
    ppermute x11, starting transfers between devices, swapped(): return lax.ppermute(x, BOTH, pairs)  11.7 us
    ppermute x11, waiting for transfers between devices, swapped(): return lax.ppermute(x, BOTH, pairs)  8.77 us
    all_to_all x1, waiting for transfers between devices, spread_blocks(): return lax.all_to_all(flat, BOTH, 0, 0, tiled=True).reshape(blocks.shape)  5.67 us
    ppermute x1, starting transfers between devices, across_faces(): return lax.ppermute(sent, BOTH, pairs)  4.85 us
    ppermute x1, starting transfers between devices, pair_up(): lax.ppermute(outer, 'tile', [(i, (i + 1 ^ 1) - 1 if i else t - 1) for i i...  4.37 us
    all_to_all x1, starting transfers between devices, spread_blocks(): return lax.all_to_all(flat, BOTH, 0, 0, tiled=True).reshape(blocks.shape)  4.08 us
  transfers between devices with their start and end apart: 15, of which 10 were waited for; matrix products, arithmetic and copies ran while one was open for 0% of the time, Pallas kernels for 9%

profile of v3, /device:TPU:0, one launch (start us, length us, event | category | flops | bytes accessed | tf_op | source)
XLA Modules:
  0.0 54.6 jit_solution(8611271640581356637)
XLA Ops:
  0.6 1.0 %copy_bitcast_fusion = (bf16[1,96,2,2,96]{4,1,2,0,3:T(8,128)(2,1)S(1)}, bf16[1,96,2,2,96]{4,1,2,0,3:T(8,128)(2,1)S(1)}) fusion(bf16[96,2,2,96]{3,2,1,0:T(2,128)(2,1)} %param.9, bf16[96,2,2,96]{3,2,1,0:T(2,128)(2,1)} %param.8), kind=kLoop, calls=%fused_computation.5 | loop fusion | bytes 294912 | tf_op jit(solution)/shard_map/stack | solution.py:719
  1.7 0.0 copy-start.5
  1.7 4.8 %collective-permute-start = (bf16[2,2,2,96,128]{4,3,2,1,0:T(8,128)(2,1)S(1)}, bf16[2,2,2,96,128]{4,3,2,1,0:T(8,128)(2,1)S(1)}, u32[]{:S(2)}, u32[]{:S(2)}) collective-permute-start(bf16[2,2,2,96,128]{4,3,2,1,0:T(8,128)(2,1)S(1)} %pad.4.columns_ref.refs_0_), channel_id=1, source_target_pairs={{30,31},{31,30},{1,0},{0,1}} | collective-permute-start | bytes 589832 | tf_op jit(solution)/shard_map/ppermute | solution.py:652
  6.6 0.0 copy-start.4
  6.6 0.1 stack.48.ids_ref
  6.7 0.0 copy-done.5
  6.7 0.0 copy-start.3
  6.7 1.8 %shard_map.111 = bf16[16,2,24,96]{3,2,1,0:T(8,128)(2,1)} custom-call(s32[6]{0:T(128)S(1)} %stack.48.ids_ref, s32[3,1,768]{2,1,0:T(1,128)S(1)} %copy-done.5, bf16[2,2,2,96,128]{4,3,2,1,0:T(8,128)(2,1)S(1)} %pad.4.columns_ref.refs_0_), custom_call_target="tpu_custom_call" | custom-call | tf_op jit(solution)/shard_map/pallas_call | solution.py:636
  8.5 4.1 %all-to-all-start = ((bf16[32,24,96]{2,1,0:T(8,128)(2,1)}), bf16[32,24,96]{2,1,0:T(8,128)(2,1)S(1)}, u32[]{:S(2)}, u32[]{:S(2)}) async-start(bf16[32,24,96]{2,1,0:T(8,128)(2,1)} %bitcast.8), calls=%async_computation | async-start | bytes 393216 | tf_op jit(solution)/shard_map/all_to_all | solution.py:674
  12.6 0.0 copy-start.2
  12.6 0.0 collective-permute-done.refs_3_
  12.7 0.0 copy-start
  12.7 0.0 copy-start.1
  12.8 4.4 %collective-permute-start.2 = (bf16[2,2,2,96,128]{4,3,2,1,0:T(8,128)(2,1)S(1)}, bf16[2,2,2,96,128]{4,3,2,1,0:T(8,128)(2,1)S(1)}, u32[]{:S(2)}, u32[]{:S(2)}) collective-permute-start(bf16[2,2,2,96,128]{4,3,2,1,0:T(8,128)(2,1)S(1)} %maximum_select_fusion), channel_id=1, source_target_pairs={{0,30},{2,4},{4,2},{6,8},{8,6},{10,12},{12,10},{14,16},{16,14},{18... | collective-permute-start | bytes 589832 | tf_op jit(solution)/shard_map/ppermute | solution.py:667
  17.1 0.0 collective-permute-start.1
  17.1 5.7 %all-to-all-done = bf16[32,24,96]{2,1,0:T(8,128)(2,1)S(1)} async-done(((bf16[32,24,96]{2,1,0:T(8,128)(2,1)}), bf16[32,24,96]{2,1,0:T(8,128)(2,1)S(1)}, u32[]{:S(2)}, u32[]{:S(2)}) %all-to-all-start) | async-done | bytes 147488 | tf_op jit(solution)/shard_map/all_to_all | solution.py:674
  22.8 0.9 %collective-permute-done.2.refs_2_ = bf16[2,2,2,96,128]{4,3,2,1,0:T(8,128)(2,1)S(1)} collective-permute-done((bf16[2,2,2,96,128]{4,3,2,1,0:T(8,128)(2,1)S(1)}, bf16[2,2,2,96,128]{4,3,2,1,0:T(8,128)(2,1)S(1)}, u32[]{:S(2)}, u32[]{:S(2)}) %collective-permute-start.2) | collective-permute-done | bytes 196640 | tf_op jit(solution)/shard_map/ppermute | solution.py:667
  23.7 0.0 collective-permute-done.1.refs_1_
  23.7 0.0 copy-done.4
  23.7 0.0 copy-done.3
  23.7 0.0 copy-done.2
  23.7 0.0 copy-done
  23.7 0.0 copy-done.1
  23.7 5.4 %shard_map.112 = (bf16[96,1152]{1,0:T(8,128)(2,1)S(1)}, bf16[96,1152]{1,0:T(8,128)(2,1)S(1)}, f32[4,176,128]{2,1,0:T(8,128)S(1)}, bf16[4,176,128]{2,1,0:T(8,128)(2,1)S(1)}) custom-call(s32[6]{0:T(128)S(1)} %stack.48.ids_ref, bf16[2,2,2,96,128]{4,3,2,1,0:T(8,128)(2,1)S(1)} %pad.4.columns_ref.refs_0_, ...), custom_call_target="tpu_custom_call" | custom-call | tf_op jit(solution)/shard_map/pallas_call | solution.py:636
  29.1 0.1 collective-permute-start.3
  29.2 1.4 %collective-permute-done.3 = bf16[4,176,128]{2,1,0:T(8,128)(2,1)S(1)} collective-permute-done((bf16[4,176,128]{2,1,0:T(8,128)(2,1)S(1)}, bf16[4,176,128]{2,1,0:T(8,128)(2,1)S(1)}, u32[]{:S(2)}, u32[]{:S(2)}) %collective-permute-start.3) | collective-permute-done | bytes 180256 | tf_op jit(solution)/shard_map/ppermute | solution.py:684
  30.6 0.1 fusion.3
  30.7 1.5 %collective-permute-start.6 = (bf16[176,128]{1,0:T(8,128)(2,1)S(1)}, bf16[176,128]{1,0:T(8,128)(2,1)S(1)}, u32[]{:S(2)}, u32[]{:S(2)}) collective-permute-start(bf16[176,128]{1,0:T(8,128)(2,1)S(1)} %get-tuple-element.38), channel_id=1, source_target_pairs={{0,5},{1,4},{2,7},{3,6},{4,1},{5,0},{6,3},{7,2},{8,13},{9,12},{10,... | collective-permute-start | bytes 135176 | tf_op jit(solution)/shard_map/ppermute | solution.py:684
  32.2 1.4 %collective-permute-start.5 = (bf16[176,128]{1,0:T(8,128)(2,1)S(1)}, bf16[176,128]{1,0:T(8,128)(2,1)S(1)}, u32[]{:S(2)}, u32[]{:S(2)}) collective-permute-start(bf16[176,128]{1,0:T(8,128)(2,1)S(1)} %get-tuple-element.39), channel_id=1, source_target_pairs={{0,4},{1,5},{2,6},{3,7},{4,0},{5,1},{6,2},{7,3},{8,12},{9,13},{10,... | collective-permute-start | bytes 135176 | tf_op jit(solution)/shard_map/ppermute | solution.py:684
  33.6 0.7 %collective-permute-start.4 = (bf16[176,128]{1,0:T(8,128)(2,1)S(1)}, bf16[176,128]{1,0:T(8,128)(2,1)S(1)}, u32[]{:S(2)}, u32[]{:S(2)}) collective-permute-start(bf16[176,128]{1,0:T(8,128)(2,1)S(1)} %get-tuple-element.40), channel_id=1, source_target_pairs={{0,1},{1,0},{2,3},{3,2},{4,5},{5,4},{6,7},{7,6},{8,9},{9,8},{10,11... | collective-permute-start | bytes 135176 | tf_op jit(solution)/shard_map/ppermute | solution.py:684
  34.3 3.1 %shard_map.113 = (bf16[96,2,2,96]{3,2,1,0:T(2,128)(2,1)}, bf16[96,2,2,96]{3,2,1,0:T(2,128)(2,1)}) custom-call(s32[6]{0:T(128)S(1)} %stack.48.ids_ref, bf16[96,1152]{1,0:T(8,128)(2,1)S(1)} %get-tuple-element.23.hidden_ref, bf16[96,1152]{1,0:T(8,128)(2,1)S(1)} %get-tuple-element.24.pre_grad_ref, bf16[864,96]{1,0:T(8,128)(2,1)S(1)} %bitcast.40, ...), custom_call_target="tpu_custom_call" | custom-call | tf_op jit(solution)/shard_map/pallas_call | solution.py:636
  37.4 0.0 collective-permute-done.6
  37.4 0.0 collective-permute-done.5
  37.4 0.2 collective-permute-done.4
  37.7 1.3 %collective-permute-start.9 = (bf16[176,128]{1,0:T(8,128)(2,1)S(1)}, bf16[176,128]{1,0:T(8,128)(2,1)S(1)}, u32[]{:S(2)}, u32[]{:S(2)}) collective-permute-start(bf16[176,128]{1,0:T(8,128)(2,1)S(1)} %fusion.2), channel_id=1, source_target_pairs={{0,24},{1,25},{2,26},{3,27},{4,28},{5,29},{6,30},{7,31},{8,16},{9,... | collective-permute-start | bytes 135176 | tf_op jit(solution)/shard_map/ppermute | solution.py:684
  38.9 0.9 %collective-permute-start.8 = (bf16[176,128]{1,0:T(8,128)(2,1)S(1)}, bf16[176,128]{1,0:T(8,128)(2,1)S(1)}, u32[]{:S(2)}, u32[]{:S(2)}) collective-permute-start(bf16[176,128]{1,0:T(8,128)(2,1)S(1)} %fusion.2), channel_id=1, source_target_pairs={{0,16},{1,17},{2,18},{3,19},{4,20},{5,21},{6,22},{7,23},{8,24},{9,... | collective-permute-start | bytes 135176 | tf_op jit(solution)/shard_map/ppermute | solution.py:684
  39.8 2.3 %collective-permute-start.7 = (bf16[176,128]{1,0:T(8,128)(2,1)S(1)}, bf16[176,128]{1,0:T(8,128)(2,1)S(1)}, u32[]{:S(2)}, u32[]{:S(2)}) collective-permute-start(bf16[176,128]{1,0:T(8,128)(2,1)S(1)} %fusion.2), channel_id=1, source_target_pairs={{0,8},{1,9},{2,10},{3,11},{4,12},{5,13},{6,14},{7,15},{8,0},{9,1},... | collective-permute-start | bytes 135176 | tf_op jit(solution)/shard_map/ppermute | solution.py:684
  42.1 1.8 %collective-permute-done.9 = bf16[176,128]{1,0:T(8,128)(2,1)S(1)} collective-permute-done((bf16[176,128]{1,0:T(8,128)(2,1)S(1)}, bf16[176,128]{1,0:T(8,128)(2,1)S(1)}, u32[]{:S(2)}, u32[]{:S(2)}) %collective-permute-start.9) | collective-permute-done | bytes 45088 | tf_op jit(solution)/shard_map/ppermute | solution.py:684
  43.9 0.8 %collective-permute-done.8 = bf16[176,128]{1,0:T(8,128)(2,1)S(1)} collective-permute-done((bf16[176,128]{1,0:T(8,128)(2,1)S(1)}, bf16[176,128]{1,0:T(8,128)(2,1)S(1)}, u32[]{:S(2)}, u32[]{:S(2)}) %collective-permute-start.8) | collective-permute-done | bytes 45088 | tf_op jit(solution)/shard_map/ppermute | solution.py:684
  44.7 0.0 collective-permute-done.7
  44.7 1.4 %collective-permute-start.12 = (bf16[176,128]{1,0:T(8,128)(2,1)S(1)}, bf16[176,128]{1,0:T(8,128)(2,1)S(1)}, u32[]{:S(2)}, u32[]{:S(2)}) collective-permute-start(bf16[176,128]{1,0:T(8,128)(2,1)S(1)} %add_convert_fusion), channel_id=1, source_target_pairs={{0,5},{1,4},{2,7},{3,6},{4,1},{5,0},{6,3},{7,2},{8,13},{9,12},{10,... | collective-permute-start | bytes 135176 | tf_op jit(solution)/shard_map/ppermute | solution.py:684
  46.1 1.3 %collective-permute-start.11 = (bf16[176,128]{1,0:T(8,128)(2,1)S(1)}, bf16[176,128]{1,0:T(8,128)(2,1)S(1)}, u32[]{:S(2)}, u32[]{:S(2)}) collective-permute-start(bf16[176,128]{1,0:T(8,128)(2,1)S(1)} %add_convert_fusion), channel_id=1, source_target_pairs={{0,4},{1,5},{2,6},{3,7},{4,0},{5,1},{6,2},{7,3},{8,12},{9,13},{10,... | collective-permute-start | bytes 135176 | tf_op jit(solution)/shard_map/ppermute | solution.py:684
  47.4 0.9 %collective-permute-start.10 = (bf16[176,128]{1,0:T(8,128)(2,1)S(1)}, bf16[176,128]{1,0:T(8,128)(2,1)S(1)}, u32[]{:S(2)}, u32[]{:S(2)}) collective-permute-start(bf16[176,128]{1,0:T(8,128)(2,1)S(1)} %add_convert_fusion), channel_id=1, source_target_pairs={{0,1},{1,0},{2,3},{3,2},{4,5},{5,4},{6,7},{7,6},{8,9},{9,8},{10,11... | collective-permute-start | bytes 135176 | tf_op jit(solution)/shard_map/ppermute | solution.py:684
  48.3 1.5 %collective-permute-done.12 = bf16[176,128]{1,0:T(8,128)(2,1)S(1)} collective-permute-done((bf16[176,128]{1,0:T(8,128)(2,1)S(1)}, bf16[176,128]{1,0:T(8,128)(2,1)S(1)}, u32[]{:S(2)}, u32[]{:S(2)}) %collective-permute-start.12) | collective-permute-done | bytes 45088 | tf_op jit(solution)/shard_map/ppermute | solution.py:684
  49.8 0.5 collective-permute-done.11
  50.2 1.2 %collective-permute-done.10 = bf16[176,128]{1,0:T(8,128)(2,1)S(1)} collective-permute-done((bf16[176,128]{1,0:T(8,128)(2,1)S(1)}, bf16[176,128]{1,0:T(8,128)(2,1)S(1)}, u32[]{:S(2)}, u32[]{:S(2)}) %collective-permute-start.10) | collective-permute-done | bytes 45088 | tf_op jit(solution)/shard_map/ppermute | solution.py:684
  51.5 0.1 collective-permute-start.13
  51.6 1.4 %collective-permute-done.13.theirs_ref = bf16[4,176,128]{2,1,0:T(8,128)(2,1)S(1)} collective-permute-done((bf16[4,176,128]{2,1,0:T(8,128)(2,1)S(1)}, bf16[4,176,128]{2,1,0:T(8,128)(2,1)S(1)}, u32[]{:S(2)}, u32[]{:S(2)}) %collective-permute-start.13) | collective-permute-done | bytes 180256 | tf_op jit(solution)/shard_map/ppermute | solution.py:684
  53.0 1.7 %shard_map.114 = (f32[864,96]{1,0:T(8,128)}, f32[864,96]{1,0:T(8,128)}) custom-call(s32[6]{0:T(128)S(1)} %stack.48.ids_ref, bf16[4,176,128]{2,1,0:T(8,128)(2,1)S(1)} %pad_maximum_fusion.mine_ref, bf16[4,176,128]{2,1,0:T(8,128)(2,1)S(1)} %collective-permute-done.13.theirs_ref), custom_call_target="tpu_custom_call" | custom-call | tf_op jit(solution)/shard_map/pallas_call | solution.py:636
  (9 shorter events, 0.2 us)
Async XLA Ops:
  1.7 5.0 %copy-start.5 = (s32[3,1,768]{2,1,0:T(1,128)S(1)}, s32[3,1,768]{2,1,0:T(1,128)}, u32[]{:S(2)}) copy-start(s32[3,1,768]{2,1,0:T(1,128)} %constant.36.clone.table_ref) | copy-start | bytes 27652
  1.7 10.9 %collective-permute-start = (bf16[2,2,2,96,128]{4,3,2,1,0:T(8,128)(2,1)S(1)}, bf16[2,2,2,96,128]{4,3,2,1,0:T(8,128)(2,1)S(1)}, u32[]{:S(2)}, u32[]{:S(2)}) collective-permute-start(bf16[2,2,2,96,128]{4,3,2,1,0:T(8,128)(2,1)S(1)} %pad.4.columns_ref.refs_0_), channel_id=1, source_target_pairs={{30,31},{31,30},{1,0},{0,1}} | collective-permute-start | bytes 589832 | tf_op jit(solution)/shard_map/ppermute | solution.py:652
  6.6 17.1 %copy-start.4 = (bf16[768,128]{1,0:T(8,128)(2,1)S(1)}, bf16[768,128]{1,0:T(8,128)(2,1)}, u32[]{:S(2)}) copy-start(bf16[768,128]{1,0:T(8,128)(2,1)} %constant.39.clone.refs_7_) | copy-start | bytes 589828
  6.7 17.0 %copy-start.3 = (bf16[384,1024]{1,0:T(8,128)(2,1)S(1)}, bf16[384,1024]{1,0:T(8,128)(2,1)}, u32[]{:S(2)}) copy-start(bf16[384,1024]{1,0:T(8,128)(2,1)} %constant.37.clone.refs_5_) | copy-start | bytes 2359300
  8.5 14.3 %all-to-all-start = ((bf16[32,24,96]{2,1,0:T(8,128)(2,1)}), bf16[32,24,96]{2,1,0:T(8,128)(2,1)S(1)}, u32[]{:S(2)}, u32[]{:S(2)}) async-start(bf16[32,24,96]{2,1,0:T(8,128)(2,1)} %bitcast.8), calls=%async_computation | async-start | bytes 393216 | tf_op jit(solution)/shard_map/all_to_all | solution.py:674
  12.6 11.1 %copy-start.2 = (bf16[384,1024]{1,0:T(8,128)(2,1)S(1)}, bf16[384,1024]{1,0:T(8,128)(2,1)}, u32[]{:S(2)}) copy-start(bf16[384,1024]{1,0:T(8,128)(2,1)} %constant.38.clone.refs_6_) | copy-start | bytes 2359300
  12.7 11.0 %copy-start = (bf16[3,3,96,96]{3,2,1,0:T(8,128)(2,1)S(1)}, bf16[3,3,96,96]{3,2,1,0:T(8,128)(2,1)}, u32[]{:S(2)}) copy-start(bf16[3,3,96,96]{3,2,1,0:T(8,128)(2,1)} %param.10) | copy-start | bytes 497668
  12.7 11.0 %copy-start.1 = (bf16[3,3,96,96]{3,2,1,0:T(8,128)(2,1)S(1)}, bf16[3,3,96,96]{3,2,1,0:T(8,128)(2,1)}, u32[]{:S(2)}) copy-start(bf16[3,3,96,96]{3,2,1,0:T(8,128)(2,1)} %param.11) | copy-start | bytes 497668
  12.8 10.9 %collective-permute-start.2 = (bf16[2,2,2,96,128]{4,3,2,1,0:T(8,128)(2,1)S(1)}, bf16[2,2,2,96,128]{4,3,2,1,0:T(8,128)(2,1)S(1)}, u32[]{:S(2)}, u32[]{:S(2)}) collective-permute-start(bf16[2,2,2,96,128]{4,3,2,1,0:T(8,128)(2,1)S(1)} %maximum_select_fusion), channel_id=1, source_target_pairs={{0,30},{2,4},{4,2},{6,8},{8,6},{10,12},{12,10},{14,16},{16,14},{18... | collective-permute-start | bytes 589832 | tf_op jit(solution)/shard_map/ppermute | solution.py:667
  17.1 6.5 %collective-permute-start.1 = (bf16[2,2,2,96,128]{4,3,2,1,0:T(8,128)(2,1)S(1)}, bf16[2,2,2,96,128]{4,3,2,1,0:T(8,128)(2,1)S(1)}, u32[]{:S(2)}, u32[]{:S(2)}) collective-permute-start(bf16[2,2,2,96,128]{4,3,2,1,0:T(8,128)(2,1)S(1)} %pad.4.columns_ref.refs_0_), channel_id=1, source_target_pairs={{0,2},{2,0},{4,6},{6,4},{8,10},{10,8},{12,14},{14,12},{16,18},{18,... | collective-permute-start | bytes 589832 | tf_op jit(solution)/shard_map/ppermute | solution.py:666
  29.1 1.5 %collective-permute-start.3 = (bf16[4,176,128]{2,1,0:T(8,128)(2,1)S(1)}, bf16[4,176,128]{2,1,0:T(8,128)(2,1)S(1)}, u32[]{:S(2)}, u32[]{:S(2)}) collective-permute-start(bf16[4,176,128]{2,1,0:T(8,128)(2,1)S(1)} %get-tuple-element.22), channel_id=1, source_target_pairs={{0,2},{1,3},{2,0},{3,1},{4,6},{5,7},{6,4},{7,5},{8,10},{9,11},{10,... | collective-permute-start | bytes 540680 | tf_op jit(solution)/shard_map/ppermute | solution.py:684
  30.7 6.7 %collective-permute-start.6 = (bf16[176,128]{1,0:T(8,128)(2,1)S(1)}, bf16[176,128]{1,0:T(8,128)(2,1)S(1)}, u32[]{:S(2)}, u32[]{:S(2)}) collective-permute-start(bf16[176,128]{1,0:T(8,128)(2,1)S(1)} %get-tuple-element.38), channel_id=1, source_target_pairs={{0,5},{1,4},{2,7},{3,6},{4,1},{5,0},{6,3},{7,2},{8,13},{9,12},{10,... | collective-permute-start | bytes 135176 | tf_op jit(solution)/shard_map/ppermute | solution.py:684
  32.2 5.2 %collective-permute-start.5 = (bf16[176,128]{1,0:T(8,128)(2,1)S(1)}, bf16[176,128]{1,0:T(8,128)(2,1)S(1)}, u32[]{:S(2)}, u32[]{:S(2)}) collective-permute-start(bf16[176,128]{1,0:T(8,128)(2,1)S(1)} %get-tuple-element.39), channel_id=1, source_target_pairs={{0,4},{1,5},{2,6},{3,7},{4,0},{5,1},{6,2},{7,3},{8,12},{9,13},{10,... | collective-permute-start | bytes 135176 | tf_op jit(solution)/shard_map/ppermute | solution.py:684
  33.6 4.0 %collective-permute-start.4 = (bf16[176,128]{1,0:T(8,128)(2,1)S(1)}, bf16[176,128]{1,0:T(8,128)(2,1)S(1)}, u32[]{:S(2)}, u32[]{:S(2)}) collective-permute-start(bf16[176,128]{1,0:T(8,128)(2,1)S(1)} %get-tuple-element.40), channel_id=1, source_target_pairs={{0,1},{1,0},{2,3},{3,2},{4,5},{5,4},{6,7},{7,6},{8,9},{9,8},{10,11... | collective-permute-start | bytes 135176 | tf_op jit(solution)/shard_map/ppermute | solution.py:684
  37.7 6.3 %collective-permute-start.9 = (bf16[176,128]{1,0:T(8,128)(2,1)S(1)}, bf16[176,128]{1,0:T(8,128)(2,1)S(1)}, u32[]{:S(2)}, u32[]{:S(2)}) collective-permute-start(bf16[176,128]{1,0:T(8,128)(2,1)S(1)} %fusion.2), channel_id=1, source_target_pairs={{0,24},{1,25},{2,26},{3,27},{4,28},{5,29},{6,30},{7,31},{8,16},{9,... | collective-permute-start | bytes 135176 | tf_op jit(solution)/shard_map/ppermute | solution.py:684
  38.9 5.8 %collective-permute-start.8 = (bf16[176,128]{1,0:T(8,128)(2,1)S(1)}, bf16[176,128]{1,0:T(8,128)(2,1)S(1)}, u32[]{:S(2)}, u32[]{:S(2)}) collective-permute-start(bf16[176,128]{1,0:T(8,128)(2,1)S(1)} %fusion.2), channel_id=1, source_target_pairs={{0,16},{1,17},{2,18},{3,19},{4,20},{5,21},{6,22},{7,23},{8,24},{9,... | collective-permute-start | bytes 135176 | tf_op jit(solution)/shard_map/ppermute | solution.py:684
  39.8 4.9 %collective-permute-start.7 = (bf16[176,128]{1,0:T(8,128)(2,1)S(1)}, bf16[176,128]{1,0:T(8,128)(2,1)S(1)}, u32[]{:S(2)}, u32[]{:S(2)}) collective-permute-start(bf16[176,128]{1,0:T(8,128)(2,1)S(1)} %fusion.2), channel_id=1, source_target_pairs={{0,8},{1,9},{2,10},{3,11},{4,12},{5,13},{6,14},{7,15},{8,0},{9,1},... | collective-permute-start | bytes 135176 | tf_op jit(solution)/shard_map/ppermute | solution.py:684
  44.7 5.0 %collective-permute-start.12 = (bf16[176,128]{1,0:T(8,128)(2,1)S(1)}, bf16[176,128]{1,0:T(8,128)(2,1)S(1)}, u32[]{:S(2)}, u32[]{:S(2)}) collective-permute-start(bf16[176,128]{1,0:T(8,128)(2,1)S(1)} %add_convert_fusion), channel_id=1, source_target_pairs={{0,5},{1,4},{2,7},{3,6},{4,1},{5,0},{6,3},{7,2},{8,13},{9,12},{10,... | collective-permute-start | bytes 135176 | tf_op jit(solution)/shard_map/ppermute | solution.py:684
  46.1 4.1 %collective-permute-start.11 = (bf16[176,128]{1,0:T(8,128)(2,1)S(1)}, bf16[176,128]{1,0:T(8,128)(2,1)S(1)}, u32[]{:S(2)}, u32[]{:S(2)}) collective-permute-start(bf16[176,128]{1,0:T(8,128)(2,1)S(1)} %add_convert_fusion), channel_id=1, source_target_pairs={{0,4},{1,5},{2,6},{3,7},{4,0},{5,1},{6,2},{7,3},{8,12},{9,13},{10,... | collective-permute-start | bytes 135176 | tf_op jit(solution)/shard_map/ppermute | solution.py:684
  47.4 4.0 %collective-permute-start.10 = (bf16[176,128]{1,0:T(8,128)(2,1)S(1)}, bf16[176,128]{1,0:T(8,128)(2,1)S(1)}, u32[]{:S(2)}, u32[]{:S(2)}) collective-permute-start(bf16[176,128]{1,0:T(8,128)(2,1)S(1)} %add_convert_fusion), channel_id=1, source_target_pairs={{0,1},{1,0},{2,3},{3,2},{4,5},{5,4},{6,7},{7,6},{8,9},{9,8},{10,11... | collective-permute-start | bytes 135176 | tf_op jit(solution)/shard_map/ppermute | solution.py:684
  51.5 1.5 %collective-permute-start.13 = (bf16[4,176,128]{2,1,0:T(8,128)(2,1)S(1)}, bf16[4,176,128]{2,1,0:T(8,128)(2,1)S(1)}, u32[]{:S(2)}, u32[]{:S(2)}) collective-permute-start(bf16[4,176,128]{2,1,0:T(8,128)(2,1)S(1)} %pad_maximum_fusion.mine_ref), channel_id=1, source_target_pairs={{0,2},{1,3},{2,0},{3,1},{4,6},{5,7},{6,4},{7,5},{8,10},{9,11},{10,... | collective-permute-start | bytes 540680 | tf_op jit(solution)/shard_map/ppermute | solution.py:684

commit v4 on v3

--- a/solution.py
+++ b/solution.py
@@ -34,7 +34,8 @@
         self.cells = 2 * self.reach
         self.block = 2 * self.cells
         self.kinds = 2 if self.stacks > 1 else 1
-        self.segments = self.stacks * (w + 2) + 1
+        self.inner = self.stacks * w
+        self.outer = self.stacks * 2 + 1
         self.near = 2
         self.mid = 2 * self.faces
         self.far = self.tiles // 4
@@ -52,7 +53,7 @@
     def segment(self, stack, slot):
         if 1 <= slot <= self.cols:
             return stack * self.cols + slot - 1
-        return self.stacks * self.cols + 2 * stack + (1 if slot else 0)
+        return self.inner + 2 * stack + (1 if slot else 0)
 
     def spot(self, depth, e):
         return depth * self.reach + e
@@ -222,11 +223,14 @@
     return lane == 16 * g + 8 * bottom + e
 
 
-def wide_forward(plan, found, taps_ref):
+def wide_forward(plan, found, taps_ref, inner):
     stacks, rim, lane, first, last = found
     w, n, side, high, c = plan.cols, plan.lanes, plan.side, plan.height, plan.channels
 
     def put(a, b, segment, value):
+        if (segment < plan.inner) != inner:
+            return
+        segment -= 0 if inner else plan.inner
         row = (a * 3 + b) * c
         taps_ref[row : row + c, segment * n : (segment + 1) * n] = value.astype(BF16)
 
@@ -296,14 +300,17 @@
     by_a = (jnp.where(is_top, ends, deep), line, jnp.where(is_top, deep, ends))
     for a in range(3):
         for b in range(3):
-            put(a, b, plan.segments - 1, shift(by_a[a], -b) if b else by_a[a])
-
-
-def wide_backward(plan, found, taps_ref):
+            put(a, b, plan.inner + plan.outer - 1, shift(by_a[a], -b) if b else by_a[a])
+
+
+def wide_backward(plan, found, taps_ref, inner):
     stacks, rim, lane, first, last = found
     w, n, side, high, c = plan.cols, plan.lanes, plan.side, plan.height, plan.channels
 
     def put(row, segment, value):
+        if (segment < plan.inner) != inner:
+            return
+        segment -= 0 if inner else plan.inner
         taps_ref[row * c : (row + 1) * c, segment * n : (segment + 1) * n] = value.astype(BF16)
 
     zero = jnp.zeros(lane.shape, F32)
@@ -382,7 +389,7 @@
     tops = [jnp.where(is_top, y, 0.0) for y in (deep, ends)]
     bottoms = [jnp.where(is_top, 0.0, y) for y in (deep, ends)]
     by_a = (tops[0], line, bottoms[0])
-    segment = plan.segments - 1
+    segment = plan.inner + plan.outer - 1
     for b in range(3):
         for a in range(3):
             put(a * 3 + b, segment, shift(by_a[a], b - 2))
@@ -404,14 +411,13 @@
     w, n, high, side = plan.cols, plan.lanes, plan.height, plan.side
     first = ids_ref[0] == 0
     last = ids_ref[0] == plan.tiles - 1
-    start = (plan.segments - 1) * n
+    start = (plan.outer - 1) * n
     rim = ref[:, start : start + n].astype(F32)
     lane = lax.broadcasted_iota(jnp.int32, rim.shape, 1)
     result = []
     for g in range(plan.stacks):
         left, right = [
-            ref[:, plan.segment(g, j) * n : (plan.segment(g, j) + 1) * n].astype(F32)
-            for j in (0, w + 1)
+            ref[:, j * n : (j + 1) * n].astype(F32) for j in (2 * g, 2 * g + 1)
         ]
         top = [rim[:, 16 * g + e : 16 * g + e + 1] for e in range(w + 2)]
         bottom = [rim[:, 16 * g + 8 + e : 16 * g + 9 + e] for e in range(w + 2)]
@@ -524,41 +530,67 @@
     ]
 
 
-def middle_kernel(plan, ids_ref, *refs):
-    w, n, g_count, c = plan.cols, plan.lanes, plan.stacks, plan.channels
-    around, tables, (w_one, w_two), refs = refs[:5], refs[5:8], refs[8:10], refs[10:]
-    hidden_ref, pre_grad_ref, mine_ref, theirs_ref, fwd_ref, bwd_ref, sums_ref, packed_ref = refs
+def kept_lanes(plan, ids_ref, shape, inner):
+    flat = lax.broadcasted_iota(jnp.int32, shape, 1)
+    segment, lane = flat // plan.lanes, flat % plan.lanes
+    inside = lane < plan.height
+    if not inner:
+        first = ids_ref[0] == 0
+        last = ids_ref[0] == plan.tiles - 1
+        inside = inside | (segment == plan.outer - 1)
+        inside = inside | ((segment % 2 == 0) & first & (lane == plan.height))
+        inside = inside | ((segment % 2 == 1) & last & (lane == plan.lanes - 1))
+    return inside
+
+
+def with_seams(plan, ids_ref, around, tables):
     *around, got = around
     seams = seam_cells(plan, ids_ref, got, *tables[:2])
-    found = [
-        surroundings(plan, ids_ref, k, *around, seams, tables[2]) for k in range(2)
-    ]
-    wide_forward(plan, found[0], fwd_ref)
-    wide_backward(plan, found[1], bwd_ref)
-    pre = product(w_one[...], fwd_ref[...], 0, 0)
-    grad = product(seam_weights(w_two), bwd_ref[...], 1, 0)
+    return (*around, seams, tables[2])
+
+
+def go_forward(plan, ids_ref, around, weight, fwd_ref, inner):
+    wide_forward(plan, surroundings(plan, ids_ref, 0, *around), fwd_ref, inner)
+    pre = product(weight[...], fwd_ref[...], 0, 0)
     bend = jnp.tanh(GELU_A * (pre + GELU_B * (pre * pre * pre)))
     half = 0.5 * (1.0 + bend)
     slope = half + 0.5 * pre * (1.0 - bend * bend) * (
         GELU_A * (1.0 + (3.0 * GELU_B) * (pre * pre))
     )
-    first = ids_ref[0] == 0
-    last = ids_ref[0] == plan.tiles - 1
-    flat = lax.broadcasted_iota(jnp.int32, pre.shape, 1)
-    segment, lane = flat // n, flat % n
-    own_end = g_count * w
-    left = (segment >= own_end) & ((segment - own_end) % 2 == 0)
-    right = (segment >= own_end) & ((segment - own_end) % 2 == 1)
-    inside = (lane < plan.height) | (segment == plan.segments - 1)
-    inside = inside | (left & first & (lane == plan.height))
-    inside = inside | (right & last & (lane == n - 1))
-    hidden = jnp.where(inside, pre * half, 0.0).astype(BF16)
-    pre_grad = jnp.where(inside, grad * slope, 0.0).astype(BF16)
+    inside = kept_lanes(plan, ids_ref, pre.shape, inner)
+    return jnp.where(inside, pre * half, 0.0).astype(BF16), slope
+
+
+def go_back(plan, ids_ref, around, weight, slope, bwd_ref, inner):
+    wide_backward(plan, surroundings(plan, ids_ref, 1, *around), bwd_ref, inner)
+    grad = product(seam_weights(weight), bwd_ref[...], 1, 0)
+    inside = kept_lanes(plan, ids_ref, grad.shape, inner)
+    return jnp.where(inside, grad * slope, 0.0).astype(BF16)
+
+
+def outer_forward_kernel(plan, ids_ref, *refs):
+    around, tables, (weight, hidden_ref, slope_ref, fwd_ref) = refs[:5], refs[5:8], refs[8:]
+    around = with_seams(plan, ids_ref, around, tables)
+    hidden_ref[...], slope_ref[...] = go_forward(plan, ids_ref, around, weight, fwd_ref, False)
+
+
+def outer_back_kernel(plan, ids_ref, *refs):
+    around, tables, (weight, slope_ref, pre_grad_ref, bwd_ref) = refs[:5], refs[5:8], refs[8:]
+    around = with_seams(plan, ids_ref, around, tables)
+    pre_grad_ref[...] = go_back(plan, ids_ref, around, weight, slope_ref[...], bwd_ref, False)
+
+
+def inner_kernel(plan, ids_ref, *refs):
+    c = plan.channels
+    around, tables, weights, refs = refs[:5], refs[5:8], refs[8:10], refs[10:]
+    hidden_ref, pre_grad_ref, mine_ref, theirs_ref, fwd_ref, bwd_ref, sums_ref, packed_ref = refs
+    around = with_seams(plan, ids_ref, around, tables)
+    hidden, slope = go_forward(plan, ids_ref, around, weights[0], fwd_ref, True)
+    pre_grad = go_back(plan, ids_ref, around, weights[1], slope, bwd_ref, True)
     hidden_ref[...] = hidden
     pre_grad_ref[...] = pre_grad
-    own_end *= n
-    terms = product(fwd_ref[:, :own_end], pre_grad[:, :own_end], 1, 1)
-    turned = product(bwd_ref[:, :own_end], hidden[:, :own_end], 1, 1)
+    terms = product(fwd_ref[...], pre_grad, 1, 1)
+    turned = product(bwd_ref[...], hidden, 1, 1)
     tap = [turned[i * c : (i + 1) * c] for i in range(21)]
     for b in range(3):
         tap[b] = tap[b] + tap[9 + b]
@@ -591,12 +623,12 @@
             ref[d] = rows.astype(ref.dtype)
 
 
-def last_kernel(plan, ids_ref, hidden_ref, pre_grad_ref, w_two, w_one, *refs):
-    out_ref, back_ref, fwd_ref, bwd_ref = refs
+def last_kernel(plan, ids_ref, hidden_ref, pre_grad_ref, hidden_out, pre_grad_out, *refs):
+    w_two, w_one, out_ref, back_ref, fwd_ref, bwd_ref = refs
     w, n = plan.cols, plan.lanes
-    halo = second_halos(plan, ids_ref, hidden_ref)
+    halo = second_halos(plan, ids_ref, hidden_out)
     forward_operand(plan, own_columns(plan, hidden_ref), halo, fwd_ref)
-    halo = second_halos(plan, ids_ref, pre_grad_ref)
+    halo = second_halos(plan, ids_ref, pre_grad_out)
     backward_operand(plan, own_columns(plan, pre_grad_ref), halo, bwd_ref)
     out = product(w_two[...], fwd_ref[...], 0, 0).astype(BF16)
     back = product(seam_weights(w_one), bwd_ref[...], 1, 0).astype(BF16)
@@ -694,13 +726,15 @@
     half = mine + swapped(plan, theirs, near=1).astype(F32)
     short = half.astype(BF16)
     got = [swapped(plan, short[d], mid=d) for d in range(1, plan.mid)]
-    got, beside = lax.optimization_barrier((got, beside))
+    got, kept = lax.optimization_barrier((got, beside[0](None)))
     piece = tree_sum([half[0]] + [x.astype(F32) for x in got]).astype(BF16)
     got = [swapped(plan, piece, far=d) for d in range(1, plan.far)]
+    got, kept = lax.optimization_barrier((got, beside[1](kept)))
     piece = tree_sum([x.astype(F32) for x in [piece] + got]).astype(BF16)
     pieces = [piece] + [swapped(plan, piece, mid=d) for d in range(1, plan.mid)]
+    pieces, kept = lax.optimization_barrier((pieces, beside[2](kept)))
     half = jnp.stack(pieces)
-    return half, swapped(plan, half, near=1), beside
+    return half, swapped(plan, half, near=1), kept
 
 
 def on_device(mesh_shape, fields, upstream, kernel_one, kernel_two):
@@ -738,24 +772,51 @@
 
     piece = (plan.mid, plan.piece, plan.wide)
     rows = plan.near * plan.mid * plan.piece
-    wide = plan.segments * n
+    inner, outer = plan.inner * n, plan.outer * n
+    given = [columns, *halo, *plan.take_tables()]
     hidden, pre_grad, mine, theirs = call(
-        functools.partial(middle_kernel, plan),
+        functools.partial(inner_kernel, plan),
         ids,
-        [columns, *halo, *plan.take_tables(), fwd_one, bwd_two],
-        [jax.ShapeDtypeStruct((c, wide), BF16)] * 2
+        given + [fwd_one, bwd_two],
+        [jax.ShapeDtypeStruct((c, inner), BF16)] * 2
         + [jax.ShapeDtypeStruct(piece, F32), jax.ShapeDtypeStruct(piece, BF16)],
-        taps(wide) + [pltpu.VMEM((plan.terms, c), F32), pltpu.VMEM((rows, plan.wide), F32)],
+        taps(inner)
+        + [pltpu.VMEM((plan.terms, c), F32), pltpu.VMEM((rows, plan.wide), F32)],
     )
-    out_shape = jax.ShapeDtypeStruct((own, g, w, h), BF16)
-    beside = call(
-        functools.partial(last_kernel, plan),
-        ids,
-        [hidden, pre_grad, fwd_two, bwd_one],
-        [out_shape, out_shape],
-        taps(g * w * n),
+    theirs, given, hidden, pre_grad = lax.optimization_barrier((theirs, given, hidden, pre_grad))
+
+    def outer_forward(unused):
+        return call(
+            functools.partial(outer_forward_kernel, plan),
+            ids,
+            given + [fwd_one],
+            [jax.ShapeDtypeStruct((c, outer), BF16), jax.ShapeDtypeStruct((c, outer), F32)],
+            taps(outer)[:1],
+        )
+
+    def outer_back(kept):
+        hidden_out, slope = kept
+        (pre_grad_out,) = call(
+            functools.partial(outer_back_kernel, plan),
+            ids,
+            given + [bwd_two, slope],
+            [jax.ShapeDtypeStruct((c, outer), BF16)],
+            taps(outer)[1:],
+        )
+        return hidden_out, pre_grad_out
+
+    def finish(kept):
+        return call(
+            functools.partial(last_kernel, plan),
+            ids,
+            [hidden, pre_grad, *kept, fwd_two, bwd_one],
+            [jax.ShapeDtypeStruct((own, g, w, h), BF16)] * 2,
+            taps(inner),
+        )
+
+    mine, theirs, (result, fields_grad) = sum_all(
+        plan, mine, theirs, (outer_forward, outer_back, finish)
     )
-    mine, theirs, (result, fields_grad) = sum_all(plan, mine, theirs, list(beside))
     scale = 1.0 / (plan.side * 12.0**0.5)
     sums = call(
         functools.partial(sum_kernel, plan, scale),

time: 54.9 us -> 53.1 us (0.967)
  waiting for transfers between devices: 15.3 us -> 10.5 us
  Pallas kernels: 12.1 us -> 15.1 us
    ppermute x11, waiting for transfers between devices: 8.77 us -> 3.92 us  [swapped(): return lax.ppermute(x, BOTH, pairs)]
    pallas_call x4 -> x6, Pallas kernels: 12.1 us -> 15.1 us  [call(): pl.pallas_call(body, out_shape=outs, in_specs=[SMEM] + [VMEM] * len(input...]
  transfers between devices with their start and end apart: 15 -> 15, of which waited for: 10 -> 6; matrix products, arithmetic and copies ran while one was open for 0% -> 0% of each run, Pallas kernels for 9% -> 18%
where the time goes in v4:
time: 53.1 us; the launch traced here: 52.8 us
  starting transfers between devices  25 us (47%)
  Pallas kernels  15.1 us (28%)
  waiting for transfers between devices  10.5 us (20%)
  local copies, waits for them, and re-layouts  1.16 us (2%)
  between operations  0.87 us (2%)
    pallas_call x6, Pallas kernels, call(): pl.pallas_call(body, out_shape=outs, in_specs=[SMEM] + [VMEM] * len(input...  15.1 us
    ppermute x11, starting transfers between devices, swapped(): return lax.ppermute(x, BOTH, pairs)  11.7 us
    all_to_all x1, waiting for transfers between devices, spread_blocks(): return lax.all_to_all(flat, BOTH, 0, 0, tiled=True).reshape(blocks.shape)  5.7 us
    ppermute x1, starting transfers between devices, across_faces(): return lax.ppermute(sent, BOTH, pairs)  4.85 us
    ppermute x1, starting transfers between devices, pair_up(): lax.ppermute(outer, 'tile', [(i, (i + 1 ^ 1) - 1 if i else t - 1) for i i...  4.37 us
    all_to_all x1, starting transfers between devices, spread_blocks(): return lax.all_to_all(flat, BOTH, 0, 0, tiled=True).reshape(blocks.shape)  4.08 us
    ppermute x11, waiting for transfers between devices, swapped(): return lax.ppermute(x, BOTH, pairs)  3.92 us
  transfers between devices with their start and end apart: 15, of which 6 were waited for; matrix products, arithmetic and copies ran while one was open for 0% of the time, Pallas kernels for 18%

profile of v4, /device:TPU:0, one launch (start us, length us, event | category | flops | bytes accessed | tf_op | source)
XLA Modules:
  0.0 52.8 jit_solution(3391461039008708615)
XLA Ops:
  0.6 1.0 %copy_bitcast_fusion = (bf16[1,96,2,2,96]{4,1,2,0,3:T(8,128)(2,1)S(1)}, bf16[1,96,2,2,96]{4,1,2,0,3:T(8,128)(2,1)S(1)}) fusion(bf16[96,2,2,96]{3,2,1,0:T(2,128)(2,1)} %param.9, bf16[96,2,2,96]{3,2,1,0:T(2,128)(2,1)} %param.8), kind=kLoop, calls=%fused_computation.5 | loop fusion | bytes 294912 | tf_op jit(solution)/shard_map/stack | solution.py:753
  1.7 0.0 copy-start.5
  1.7 4.8 %collective-permute-start = (bf16[2,2,2,96,128]{4,3,2,1,0:T(8,128)(2,1)S(1)}, bf16[2,2,2,96,128]{4,3,2,1,0:T(8,128)(2,1)S(1)}, u32[]{:S(2)}, u32[]{:S(2)}) collective-permute-start(bf16[2,2,2,96,128]{4,3,2,1,0:T(8,128)(2,1)S(1)} %pad.4.columns_ref.refs_0_), channel_id=1, source_target_pairs={{30,31},{31,30},{1,0},{0,1}} | collective-permute-start | bytes 589832 | tf_op jit(solution)/shard_map/ppermute | solution.py:684
  6.6 0.0 copy-start.4
  6.6 0.1 stack.48.ids_ref
  6.7 0.0 copy-done.5
  6.7 0.0 copy-start.2
  6.7 0.0 copy-start.3
  6.7 1.8 %shard_map.111 = bf16[16,2,24,96]{3,2,1,0:T(8,128)(2,1)} custom-call(s32[6]{0:T(128)S(1)} %stack.48.ids_ref, s32[3,1,768]{2,1,0:T(1,128)S(1)} %copy-done.5, bf16[2,2,2,96,128]{4,3,2,1,0:T(8,128)(2,1)S(1)} %pad.4.columns_ref.refs_0_), custom_call_target="tpu_custom_call" | custom-call | tf_op jit(solution)/shard_map/pallas_call | solution.py:668
  8.5 0.0 copy-start.1
  8.5 4.1 %all-to-all-start = ((bf16[32,24,96]{2,1,0:T(8,128)(2,1)}), bf16[32,24,96]{2,1,0:T(8,128)(2,1)S(1)}, u32[]{:S(2)}, u32[]{:S(2)}) async-start(bf16[32,24,96]{2,1,0:T(8,128)(2,1)} %bitcast.8), calls=%async_computation | async-start | bytes 393216 | tf_op jit(solution)/shard_map/all_to_all | solution.py:706
  12.6 0.0 copy-start
  12.7 0.0 collective-permute-done.refs_3_
  12.8 4.4 %collective-permute-start.2 = (bf16[2,2,2,96,128]{4,3,2,1,0:T(8,128)(2,1)S(1)}, bf16[2,2,2,96,128]{4,3,2,1,0:T(8,128)(2,1)S(1)}, u32[]{:S(2)}, u32[]{:S(2)}) collective-permute-start(bf16[2,2,2,96,128]{4,3,2,1,0:T(8,128)(2,1)S(1)} %maximum_select_fusion), channel_id=1, source_target_pairs={{0,30},{2,4},{4,2},{6,8},{8,6},{10,12},{12,10},{14,16},{16,14},{18... | collective-permute-start | bytes 589832 | tf_op jit(solution)/shard_map/ppermute | solution.py:699
  17.1 0.0 collective-permute-start.1
  17.1 5.7 %all-to-all-done = bf16[32,24,96]{2,1,0:T(8,128)(2,1)S(1)} async-done(((bf16[32,24,96]{2,1,0:T(8,128)(2,1)}), bf16[32,24,96]{2,1,0:T(8,128)(2,1)S(1)}, u32[]{:S(2)}, u32[]{:S(2)}) %all-to-all-start) | async-done | bytes 147488 | tf_op jit(solution)/shard_map/all_to_all | solution.py:706
  22.8 0.9 %collective-permute-done.2.refs_2_ = bf16[2,2,2,96,128]{4,3,2,1,0:T(8,128)(2,1)S(1)} collective-permute-done((bf16[2,2,2,96,128]{4,3,2,1,0:T(8,128)(2,1)S(1)}, bf16[2,2,2,96,128]{4,3,2,1,0:T(8,128)(2,1)S(1)}, u32[]{:S(2)}, u32[]{:S(2)}) %collective-permute-start.2) | collective-permute-done | bytes 196640 | tf_op jit(solution)/shard_map/ppermute | solution.py:699
  23.7 0.0 collective-permute-done.1.refs_1_
  23.7 0.0 copy-done.4
  23.7 0.0 copy-done.2
  23.7 0.0 copy-done.3
  23.7 0.0 copy-done.1
  23.7 0.0 copy-done
  23.7 3.7 %shard_map.112 = (bf16[96,512]{1,0:T(8,128)(2,1)S(1)}, bf16[96,512]{1,0:T(8,128)(2,1)S(1)}, f32[4,176,128]{2,1,0:T(8,128)S(1)}, bf16[4,176,128]{2,1,0:T(8,128)(2,1)S(1)}) custom-call(s32[6]{0:T(128)S(1)} %stack.48.ids_ref, bf16[2,2,2,96,128]{4,3,2,1,0:T(8,128)(2,1)S(1)} %pad.4.columns_ref.refs_0_, ...), custom_call_target="tpu_custom_call" | custom-call | tf_op jit(solution)/shard_map/pallas_call | solution.py:668
  27.4 0.1 collective-permute-start.3
  27.5 1.4 %collective-permute-done.3 = bf16[4,176,128]{2,1,0:T(8,128)(2,1)S(1)} collective-permute-done((bf16[4,176,128]{2,1,0:T(8,128)(2,1)S(1)}, bf16[4,176,128]{2,1,0:T(8,128)(2,1)S(1)}, u32[]{:S(2)}, u32[]{:S(2)}) %collective-permute-start.3) | collective-permute-done | bytes 180256 | tf_op jit(solution)/shard_map/ppermute | solution.py:716
  28.9 0.1 fusion.3
  29.0 1.5 %collective-permute-start.6 = (bf16[176,128]{1,0:T(8,128)(2,1)S(1)}, bf16[176,128]{1,0:T(8,128)(2,1)S(1)}, u32[]{:S(2)}, u32[]{:S(2)}) collective-permute-start(bf16[176,128]{1,0:T(8,128)(2,1)S(1)} %get-tuple-element.86), channel_id=1, source_target_pairs={{0,5},{1,4},{2,7},{3,6},{4,1},{5,0},{6,3},{7,2},{8,13},{9,12},{10,... | collective-permute-start | bytes 135176 | tf_op jit(solution)/shard_map/ppermute | solution.py:716
  30.5 1.4 %collective-permute-start.5 = (bf16[176,128]{1,0:T(8,128)(2,1)S(1)}, bf16[176,128]{1,0:T(8,128)(2,1)S(1)}, u32[]{:S(2)}, u32[]{:S(2)}) collective-permute-start(bf16[176,128]{1,0:T(8,128)(2,1)S(1)} %get-tuple-element.87), channel_id=1, source_target_pairs={{0,4},{1,5},{2,6},{3,7},{4,0},{5,1},{6,2},{7,3},{8,12},{9,13},{10,... | collective-permute-start | bytes 135176 | tf_op jit(solution)/shard_map/ppermute | solution.py:716
  31.9 0.7 %collective-permute-start.4 = (bf16[176,128]{1,0:T(8,128)(2,1)S(1)}, bf16[176,128]{1,0:T(8,128)(2,1)S(1)}, u32[]{:S(2)}, u32[]{:S(2)}) collective-permute-start(bf16[176,128]{1,0:T(8,128)(2,1)S(1)} %get-tuple-element.88), channel_id=1, source_target_pairs={{0,1},{1,0},{2,3},{3,2},{4,5},{5,4},{6,7},{7,6},{8,9},{9,8},{10,11... | collective-permute-start | bytes 135176 | tf_op jit(solution)/shard_map/ppermute | solution.py:716
  32.6 2.4 %shard_map.113 = (bf16[96,640]{1,0:T(8,128)(2,1)S(1)}, f32[96,640]{1,0:T(8,128)S(1)}) custom-call(s32[6]{0:T(128)S(1)} %stack.48.ids_ref, bf16[2,2,2,96,128]{4,3,2,1,0:T(8,128)(2,1)S(1)} %pad.4.columns_ref.refs_0_, bf16[2,2,2,96,128]{4,3,2,1,0:T(8,128)(2,1)S(1)} %collective-permute-done.1.refs_1_, ...), custom_call_target="tpu_custom_call" | custom-call | tf_op jit(solution)/shard_map/pallas_call | solution.py:668
  35.0 0.0 collective-permute-done.6
  35.0 0.0 collective-permute-done.5
  35.0 0.9 %collective-permute-done.4 = bf16[176,128]{1,0:T(8,128)(2,1)S(1)} collective-permute-done((bf16[176,128]{1,0:T(8,128)(2,1)S(1)}, bf16[176,128]{1,0:T(8,128)(2,1)S(1)}, u32[]{:S(2)}, u32[]{:S(2)}) %collective-permute-start.4) | collective-permute-done | bytes 45088 | tf_op jit(solution)/shard_map/ppermute | solution.py:716
  36.0 1.2 %collective-permute-start.9 = (bf16[176,128]{1,0:T(8,128)(2,1)S(1)}, bf16[176,128]{1,0:T(8,128)(2,1)S(1)}, u32[]{:S(2)}, u32[]{:S(2)}) collective-permute-start(bf16[176,128]{1,0:T(8,128)(2,1)S(1)} %fusion.2), channel_id=1, source_target_pairs={{0,24},{1,25},{2,26},{3,27},{4,28},{5,29},{6,30},{7,31},{8,16},{9,... | collective-permute-start | bytes 135176 | tf_op jit(solution)/shard_map/ppermute | solution.py:716
  37.1 0.9 %collective-permute-start.8 = (bf16[176,128]{1,0:T(8,128)(2,1)S(1)}, bf16[176,128]{1,0:T(8,128)(2,1)S(1)}, u32[]{:S(2)}, u32[]{:S(2)}) collective-permute-start(bf16[176,128]{1,0:T(8,128)(2,1)S(1)} %fusion.2), channel_id=1, source_target_pairs={{0,16},{1,17},{2,18},{3,19},{4,20},{5,21},{6,22},{7,23},{8,24},{9,... | collective-permute-start | bytes 135176 | tf_op jit(solution)/shard_map/ppermute | solution.py:716
  38.1 2.4 %collective-permute-start.7 = (bf16[176,128]{1,0:T(8,128)(2,1)S(1)}, bf16[176,128]{1,0:T(8,128)(2,1)S(1)}, u32[]{:S(2)}, u32[]{:S(2)}) collective-permute-start(bf16[176,128]{1,0:T(8,128)(2,1)S(1)} %fusion.2), channel_id=1, source_target_pairs={{0,8},{1,9},{2,10},{3,11},{4,12},{5,13},{6,14},{7,15},{8,0},{9,1},... | collective-permute-start | bytes 135176 | tf_op jit(solution)/shard_map/ppermute | solution.py:716
  40.4 2.3 %shard_map.114.pre_grad_out = bf16[96,640]{1,0:T(8,128)(2,1)S(1)} custom-call(s32[6]{0:T(128)S(1)} %stack.48.ids_ref, bf16[2,2,2,96,128]{4,3,2,1,0:T(8,128)(2,1)S(1)} %pad.4.columns_ref.refs_0_, bf16[2,2,2,96,128]{4,3,2,1,0:T(8,128)(2,1)S(1)} %collective-permute-done.1.refs_1_, bf16[2,2,2,96,128]{4,3,2,1,0:T(8,128)(2,1)S(1)} %collective-permute-done.2.refs_2_, ...), custom_call_target="tpu_custom_call" | custom-call | tf_op jit(solution)/shard_map/pallas_call | solution.py:668
  42.7 0.0 collective-permute-done.9
  42.7 0.2 collective-permute-done.8
  42.9 0.0 collective-permute-done.7
  42.9 0.9 %collective-permute-start.12 = (bf16[176,128]{1,0:T(8,128)(2,1)S(1)}, bf16[176,128]{1,0:T(8,128)(2,1)S(1)}, u32[]{:S(2)}, u32[]{:S(2)}) collective-permute-start(bf16[176,128]{1,0:T(8,128)(2,1)S(1)} %add_convert_fusion), channel_id=1, source_target_pairs={{0,5},{1,4},{2,7},{3,6},{4,1},{5,0},{6,3},{7,2},{8,13},{9,12},{10,... | collective-permute-start | bytes 135176 | tf_op jit(solution)/shard_map/ppermute | solution.py:716
  43.9 1.3 %collective-permute-start.11 = (bf16[176,128]{1,0:T(8,128)(2,1)S(1)}, bf16[176,128]{1,0:T(8,128)(2,1)S(1)}, u32[]{:S(2)}, u32[]{:S(2)}) collective-permute-start(bf16[176,128]{1,0:T(8,128)(2,1)S(1)} %add_convert_fusion), channel_id=1, source_target_pairs={{0,4},{1,5},{2,6},{3,7},{4,0},{5,1},{6,2},{7,3},{8,12},{9,13},{10,... | collective-permute-start | bytes 135176 | tf_op jit(solution)/shard_map/ppermute | solution.py:716
  45.2 1.3 %collective-permute-start.10 = (bf16[176,128]{1,0:T(8,128)(2,1)S(1)}, bf16[176,128]{1,0:T(8,128)(2,1)S(1)}, u32[]{:S(2)}, u32[]{:S(2)}) collective-permute-start(bf16[176,128]{1,0:T(8,128)(2,1)S(1)} %add_convert_fusion), channel_id=1, source_target_pairs={{0,1},{1,0},{2,3},{3,2},{4,5},{5,4},{6,7},{7,6},{8,9},{9,8},{10,11... | collective-permute-start | bytes 135176 | tf_op jit(solution)/shard_map/ppermute | solution.py:716
  46.5 3.1 %shard_map.115 = (bf16[96,2,2,96]{3,2,1,0:T(2,128)(2,1)}, bf16[96,2,2,96]{3,2,1,0:T(2,128)(2,1)}) custom-call(s32[6]{0:T(128)S(1)} %stack.48.ids_ref, bf16[96,512]{1,0:T(8,128)(2,1)S(1)} %get-tuple-element.68.hidden_ref, bf16[96,512]{1,0:T(8,128)(2,1)S(1)} %get-tuple-element.69.pre_grad_ref, bf16[96,640]{1,0:T(8,128)(2,1)S(1)} %get-tuple-element.70.hidden_out, ...), custom_call_target="tpu_custom_call" | custom-call | tf_op jit(solution)/shard_map/pallas_call | solution.py:668
  49.6 0.0 collective-permute-done.12
  49.6 0.0 collective-permute-done.11
  49.6 0.0 collective-permute-done.10
  49.7 0.1 collective-permute-start.13
  49.8 1.4 %collective-permute-done.13.theirs_ref = bf16[4,176,128]{2,1,0:T(8,128)(2,1)S(1)} collective-permute-done((bf16[4,176,128]{2,1,0:T(8,128)(2,1)S(1)}, bf16[4,176,128]{2,1,0:T(8,128)(2,1)S(1)}, u32[]{:S(2)}, u32[]{:S(2)}) %collective-permute-start.13) | collective-permute-done | bytes 180256 | tf_op jit(solution)/shard_map/ppermute | solution.py:716
  51.2 1.7 %shard_map.116 = (f32[864,96]{1,0:T(8,128)}, f32[864,96]{1,0:T(8,128)}) custom-call(s32[6]{0:T(128)S(1)} %stack.48.ids_ref, bf16[4,176,128]{2,1,0:T(8,128)(2,1)S(1)} %pad_maximum_fusion.mine_ref, bf16[4,176,128]{2,1,0:T(8,128)(2,1)S(1)} %collective-permute-done.13.theirs_ref), custom_call_target="tpu_custom_call" | custom-call | tf_op jit(solution)/shard_map/pallas_call | solution.py:668
  (9 shorter events, 0.2 us)
Async XLA Ops:
  1.7 5.0 %copy-start.5 = (s32[3,1,768]{2,1,0:T(1,128)S(1)}, s32[3,1,768]{2,1,0:T(1,128)}, u32[]{:S(2)}) copy-start(s32[3,1,768]{2,1,0:T(1,128)} %constant.36.clone.table_ref) | copy-start | bytes 27652
  1.7 10.9 %collective-permute-start = (bf16[2,2,2,96,128]{4,3,2,1,0:T(8,128)(2,1)S(1)}, bf16[2,2,2,96,128]{4,3,2,1,0:T(8,128)(2,1)S(1)}, u32[]{:S(2)}, u32[]{:S(2)}) collective-permute-start(bf16[2,2,2,96,128]{4,3,2,1,0:T(8,128)(2,1)S(1)} %pad.4.columns_ref.refs_0_), channel_id=1, source_target_pairs={{30,31},{31,30},{1,0},{0,1}} | collective-permute-start | bytes 589832 | tf_op jit(solution)/shard_map/ppermute | solution.py:684
  6.6 17.1 %copy-start.4 = (bf16[768,128]{1,0:T(8,128)(2,1)S(1)}, bf16[768,128]{1,0:T(8,128)(2,1)}, u32[]{:S(2)}) copy-start(bf16[768,128]{1,0:T(8,128)(2,1)} %constant.39.clone.refs_7_) | copy-start | bytes 589828
  6.7 17.0 %copy-start.2 = (bf16[3,3,96,96]{3,2,1,0:T(8,128)(2,1)S(1)}, bf16[3,3,96,96]{3,2,1,0:T(8,128)(2,1)}, u32[]{:S(2)}) copy-start(bf16[3,3,96,96]{3,2,1,0:T(8,128)(2,1)} %param.10) | copy-start | bytes 497668
  6.7 17.0 %copy-start.3 = (bf16[3,3,96,96]{3,2,1,0:T(8,128)(2,1)S(1)}, bf16[3,3,96,96]{3,2,1,0:T(8,128)(2,1)}, u32[]{:S(2)}) copy-start(bf16[3,3,96,96]{3,2,1,0:T(8,128)(2,1)} %param.11) | copy-start | bytes 497668
  8.5 15.2 %copy-start.1 = (bf16[384,1024]{1,0:T(8,128)(2,1)S(1)}, bf16[384,1024]{1,0:T(8,128)(2,1)}, u32[]{:S(2)}) copy-start(bf16[384,1024]{1,0:T(8,128)(2,1)} %constant.37.clone.refs_5_) | copy-start | bytes 2359300
  8.5 14.3 %all-to-all-start = ((bf16[32,24,96]{2,1,0:T(8,128)(2,1)}), bf16[32,24,96]{2,1,0:T(8,128)(2,1)S(1)}, u32[]{:S(2)}, u32[]{:S(2)}) async-start(bf16[32,24,96]{2,1,0:T(8,128)(2,1)} %bitcast.8), calls=%async_computation | async-start | bytes 393216 | tf_op jit(solution)/shard_map/all_to_all | solution.py:706
  12.6 11.1 %copy-start = (bf16[384,1024]{1,0:T(8,128)(2,1)S(1)}, bf16[384,1024]{1,0:T(8,128)(2,1)}, u32[]{:S(2)}) copy-start(bf16[384,1024]{1,0:T(8,128)(2,1)} %constant.38.clone.refs_6_) | copy-start | bytes 2359300
  12.8 10.9 %collective-permute-start.2 = (bf16[2,2,2,96,128]{4,3,2,1,0:T(8,128)(2,1)S(1)}, bf16[2,2,2,96,128]{4,3,2,1,0:T(8,128)(2,1)S(1)}, u32[]{:S(2)}, u32[]{:S(2)}) collective-permute-start(bf16[2,2,2,96,128]{4,3,2,1,0:T(8,128)(2,1)S(1)} %maximum_select_fusion), channel_id=1, source_target_pairs={{0,30},{2,4},{4,2},{6,8},{8,6},{10,12},{12,10},{14,16},{16,14},{18... | collective-permute-start | bytes 589832 | tf_op jit(solution)/shard_map/ppermute | solution.py:699
  17.1 6.6 %collective-permute-start.1 = (bf16[2,2,2,96,128]{4,3,2,1,0:T(8,128)(2,1)S(1)}, bf16[2,2,2,96,128]{4,3,2,1,0:T(8,128)(2,1)S(1)}, u32[]{:S(2)}, u32[]{:S(2)}) collective-permute-start(bf16[2,2,2,96,128]{4,3,2,1,0:T(8,128)(2,1)S(1)} %pad.4.columns_ref.refs_0_), channel_id=1, source_target_pairs={{0,2},{2,0},{4,6},{6,4},{8,10},{10,8},{12,14},{14,12},{16,18},{18,... | collective-permute-start | bytes 589832 | tf_op jit(solution)/shard_map/ppermute | solution.py:698
  27.4 1.5 %collective-permute-start.3 = (bf16[4,176,128]{2,1,0:T(8,128)(2,1)S(1)}, bf16[4,176,128]{2,1,0:T(8,128)(2,1)S(1)}, u32[]{:S(2)}, u32[]{:S(2)}) collective-permute-start(bf16[4,176,128]{2,1,0:T(8,128)(2,1)S(1)} %get-tuple-element.49), channel_id=1, source_target_pairs={{0,2},{1,3},{2,0},{3,1},{4,6},{5,7},{6,4},{7,5},{8,10},{9,11},{10,... | collective-permute-start | bytes 540680 | tf_op jit(solution)/shard_map/ppermute | solution.py:716
  29.0 6.0 %collective-permute-start.6 = (bf16[176,128]{1,0:T(8,128)(2,1)S(1)}, bf16[176,128]{1,0:T(8,128)(2,1)S(1)}, u32[]{:S(2)}, u32[]{:S(2)}) collective-permute-start(bf16[176,128]{1,0:T(8,128)(2,1)S(1)} %get-tuple-element.86), channel_id=1, source_target_pairs={{0,5},{1,4},{2,7},{3,6},{4,1},{5,0},{6,3},{7,2},{8,13},{9,12},{10,... | collective-permute-start | bytes 135176 | tf_op jit(solution)/shard_map/ppermute | solution.py:716
  30.5 4.5 %collective-permute-start.5 = (bf16[176,128]{1,0:T(8,128)(2,1)S(1)}, bf16[176,128]{1,0:T(8,128)(2,1)S(1)}, u32[]{:S(2)}, u32[]{:S(2)}) collective-permute-start(bf16[176,128]{1,0:T(8,128)(2,1)S(1)} %get-tuple-element.87), channel_id=1, source_target_pairs={{0,4},{1,5},{2,6},{3,7},{4,0},{5,1},{6,2},{7,3},{8,12},{9,13},{10,... | collective-permute-start | bytes 135176 | tf_op jit(solution)/shard_map/ppermute | solution.py:716
  31.9 4.0 %collective-permute-start.4 = (bf16[176,128]{1,0:T(8,128)(2,1)S(1)}, bf16[176,128]{1,0:T(8,128)(2,1)S(1)}, u32[]{:S(2)}, u32[]{:S(2)}) collective-permute-start(bf16[176,128]{1,0:T(8,128)(2,1)S(1)} %get-tuple-element.88), channel_id=1, source_target_pairs={{0,1},{1,0},{2,3},{3,2},{4,5},{5,4},{6,7},{7,6},{8,9},{9,8},{10,11... | collective-permute-start | bytes 135176 | tf_op jit(solution)/shard_map/ppermute | solution.py:716
  36.0 6.7 %collective-permute-start.9 = (bf16[176,128]{1,0:T(8,128)(2,1)S(1)}, bf16[176,128]{1,0:T(8,128)(2,1)S(1)}, u32[]{:S(2)}, u32[]{:S(2)}) collective-permute-start(bf16[176,128]{1,0:T(8,128)(2,1)S(1)} %fusion.2), channel_id=1, source_target_pairs={{0,24},{1,25},{2,26},{3,27},{4,28},{5,29},{6,30},{7,31},{8,16},{9,... | collective-permute-start | bytes 135176 | tf_op jit(solution)/shard_map/ppermute | solution.py:716
  37.1 5.8 %collective-permute-start.8 = (bf16[176,128]{1,0:T(8,128)(2,1)S(1)}, bf16[176,128]{1,0:T(8,128)(2,1)S(1)}, u32[]{:S(2)}, u32[]{:S(2)}) collective-permute-start(bf16[176,128]{1,0:T(8,128)(2,1)S(1)} %fusion.2), channel_id=1, source_target_pairs={{0,16},{1,17},{2,18},{3,19},{4,20},{5,21},{6,22},{7,23},{8,24},{9,... | collective-permute-start | bytes 135176 | tf_op jit(solution)/shard_map/ppermute | solution.py:716
  38.1 4.8 %collective-permute-start.7 = (bf16[176,128]{1,0:T(8,128)(2,1)S(1)}, bf16[176,128]{1,0:T(8,128)(2,1)S(1)}, u32[]{:S(2)}, u32[]{:S(2)}) collective-permute-start(bf16[176,128]{1,0:T(8,128)(2,1)S(1)} %fusion.2), channel_id=1, source_target_pairs={{0,8},{1,9},{2,10},{3,11},{4,12},{5,13},{6,14},{7,15},{8,0},{9,1},... | collective-permute-start | bytes 135176 | tf_op jit(solution)/shard_map/ppermute | solution.py:716
  42.9 6.7 %collective-permute-start.12 = (bf16[176,128]{1,0:T(8,128)(2,1)S(1)}, bf16[176,128]{1,0:T(8,128)(2,1)S(1)}, u32[]{:S(2)}, u32[]{:S(2)}) collective-permute-start(bf16[176,128]{1,0:T(8,128)(2,1)S(1)} %add_convert_fusion), channel_id=1, source_target_pairs={{0,5},{1,4},{2,7},{3,6},{4,1},{5,0},{6,3},{7,2},{8,13},{9,12},{10,... | collective-permute-start | bytes 135176 | tf_op jit(solution)/shard_map/ppermute | solution.py:716
  43.9 5.8 %collective-permute-start.11 = (bf16[176,128]{1,0:T(8,128)(2,1)S(1)}, bf16[176,128]{1,0:T(8,128)(2,1)S(1)}, u32[]{:S(2)}, u32[]{:S(2)}) collective-permute-start(bf16[176,128]{1,0:T(8,128)(2,1)S(1)} %add_convert_fusion), channel_id=1, source_target_pairs={{0,4},{1,5},{2,6},{3,7},{4,0},{5,1},{6,2},{7,3},{8,12},{9,13},{10,... | collective-permute-start | bytes 135176 | tf_op jit(solution)/shard_map/ppermute | solution.py:716
  45.2 4.5 %collective-permute-start.10 = (bf16[176,128]{1,0:T(8,128)(2,1)S(1)}, bf16[176,128]{1,0:T(8,128)(2,1)S(1)}, u32[]{:S(2)}, u32[]{:S(2)}) collective-permute-start(bf16[176,128]{1,0:T(8,128)(2,1)S(1)} %add_convert_fusion), channel_id=1, source_target_pairs={{0,1},{1,0},{2,3},{3,2},{4,5},{5,4},{6,7},{7,6},{8,9},{9,8},{10,11... | collective-permute-start | bytes 135176 | tf_op jit(solution)/shard_map/ppermute | solution.py:716
  49.7 1.5 %collective-permute-start.13 = (bf16[4,176,128]{2,1,0:T(8,128)(2,1)S(1)}, bf16[4,176,128]{2,1,0:T(8,128)(2,1)S(1)}, u32[]{:S(2)}, u32[]{:S(2)}) collective-permute-start(bf16[4,176,128]{2,1,0:T(8,128)(2,1)S(1)} %pad_maximum_fusion.mine_ref), channel_id=1, source_target_pairs={{0,2},{1,3},{2,0},{3,1},{4,6},{5,7},{6,4},{7,5},{8,10},{9,11},{10,... | collective-permute-start | bytes 540680 | tf_op jit(solution)/shard_map/ppermute | solution.py:716

commit v5 on v4

--- a/solution.py
+++ b/solution.py
@@ -36,6 +36,8 @@
         self.kinds = 2 if self.stacks > 1 else 1
         self.inner = self.stacks * w
         self.outer = self.stacks * 2 + 1
+        self.lines = up_to(16 * self.stacks, 32)
+        assert self.lines + self.stacks * self.side <= self.lanes
         self.near = 2
         self.mid = 2 * self.faces
         self.far = self.tiles // 4
@@ -128,8 +130,9 @@
     wanted = table_ref[ids_ref[5]]
     cell = lax.broadcasted_iota(jnp.int32, (flat[0].shape[1], wanted.shape[1]), 0)
     pick = jnp.where(cell == wanted, 1.0, 0.0).astype(BF16)
-    picked = [jnp.transpose(product(x, pick, 1, 0)) for x in flat]
-    both = picked[0] + pltpu.roll(picked[1], plan.cells, 0)
+    picked = product(jnp.concatenate(flat, axis=0), pick, 1, 0)
+    channels = flat[0].shape[0]
+    both = jnp.transpose(picked[:channels] + pltpu.roll(picked[channels:], plan.cells, 1))
     both = both.reshape(t, plan.kinds, c, both.shape[-1])
     for dest in range(plan.faces):
         if plan.kinds == 2:
@@ -303,12 +306,12 @@
             put(a, b, plan.inner + plan.outer - 1, shift(by_a[a], -b) if b else by_a[a])
 
 
-def wide_backward(plan, found, taps_ref, inner):
+def wide_backward(plan, found, taps_ref, inner, edge_ref=None):
     stacks, rim, lane, first, last = found
     w, n, side, high, c = plan.cols, plan.lanes, plan.side, plan.height, plan.channels
 
     def put(row, segment, value):
-        if (segment < plan.inner) != inner:
+        if (segment < plan.inner) != inner or (inner and row >= 9):
             return
         segment -= 0 if inner else plan.inner
         taps_ref[row * c : (row + 1) * c, segment * n : (segment + 1) * n] = value.astype(BF16)
@@ -316,6 +319,7 @@
     zero = jnp.zeros(lane.shape, F32)
     rows_l = lane < side
     rows_r = (lane >= 2 * side) & (lane < high)
+    lines = []
     for g, h in enumerate(stacks):
         raw = h["raw"]
         z = list(raw)
@@ -332,6 +336,7 @@
         line_r = [jnp.where(rows_r, y, 0.0) for y in h["row_r"]]
         line_l = [line_l[1], line_l[0], zero]
         line_r = [zero, line_r[0], line_r[1]]
+        lines.append((line_l[1], line_r[1]))
         keep = (lane >= side) & (lane <= high + 1)
         deep_l = [zero] + [jnp.where(keep, h["col_l"][i], 0.0) for i in (1, 0)]
         keep = (lane < 2 * side) | (lane >= n - 2)
@@ -386,6 +391,22 @@
                     put(9 + 3 * i + b, segment, y)
     line, deep, ends = rim["line"], rim["deep"], rim["ends"]
     is_top = rim["is_top"]
+    if inner:
+        here = (rim["spot"] >= 1) & (rim["spot"] <= w) & (lane < plan.lines)
+        for b in range(3):
+            near = jnp.where(here, shift(line, b - 2), 0.0)
+            left = right = zero
+            for g, (line_l, line_r) in enumerate(lines):
+                at = plan.lines + g * side
+                y = jnp.where(first & rows_l, shift(line_l, b - 1), 0.0)
+                left += shift(y, at)
+                y = jnp.where(last & rows_r, shift(line_r, b - 1), 0.0)
+                right += shift(y, at - 2 * side)
+            top, bottom = jnp.where(is_top, near, 0.0), jnp.where(is_top, 0.0, near)
+            for i, y in enumerate((top, bottom, left, right)):
+                row = (3 * i + b) * c
+                edge_ref[row : row + c, :] = y.astype(BF16)
+        return
     tops = [jnp.where(is_top, y, 0.0) for y in (deep, ends)]
     bottoms = [jnp.where(is_top, 0.0, y) for y in (deep, ends)]
     by_a = (tops[0], line, bottoms[0])
@@ -517,9 +538,56 @@
                 taps_ref[(18 + b) * c : (19 + b) * c, at : at + n] = y
 
 
+TAPS = list(range(9))
+SEAMS = [0, 1, 2, 6, 7, 8, 0, 3, 6, 2, 5, 8]
+
+
+def tap_weights(kernel_ref, order):
+    return jnp.concatenate([kernel_ref[tap] for tap in order], axis=1)
+
+
 def seam_weights(kernel_ref):
-    order = list(range(9)) + [0, 1, 2, 6, 7, 8, 0, 3, 6, 2, 5, 8]
-    return jnp.concatenate([kernel_ref[tap] for tap in order], axis=1)
+    return tap_weights(kernel_ref, TAPS + SEAMS)
+
+
+def from_edges(plan, ids_ref, edges):
+    w, n, side, high = plan.cols, plan.lanes, plan.side, plan.height
+    first = ids_ref[0] == 0
+    last = ids_ref[0] == plan.tiles - 1
+    lane = lax.broadcasted_iota(jnp.int32, edges.shape, 1)
+    result = []
+    for g in range(plan.stacks):
+        at = plan.lines + g * side
+        for j in range(1, w + 1):
+            top, bottom = 16 * g + j, 16 * g + 8 + j
+            y = jnp.where(lane == 0, edges[:, top : top + 1], 0.0)
+            y = jnp.where(lane == high - 1, edges[:, bottom : bottom + 1], y)
+            if j == 1:
+                y += jnp.where(first & (lane < side), shift(edges, -at), 0.0)
+            if j == w:
+                rows_r = last & (lane >= 2 * side) & (lane < high)
+                y += jnp.where(rows_r, shift(edges, 2 * side - at), 0.0)
+            result.append(y)
+    return jnp.concatenate(result, axis=1)
+
+
+def to_edges(plan, ids_ref, flat):
+    w, n, side, high = plan.cols, plan.lanes, plan.side, plan.height
+    first = ids_ref[0] == 0
+    result = jnp.zeros((flat.shape[0], n), F32)
+    lane = lax.broadcasted_iota(jnp.int32, result.shape, 1)
+    for g in range(plan.stacks):
+        own = [flat[:, (g * w + i) * n : (g * w + i + 1) * n] for i in range(w)]
+        at = plan.lines + g * side
+        line_l = shift(jnp.where(lane < side, own[0], 0.0), at)
+        rows_r = (lane >= 2 * side) & (lane < high)
+        line_r = shift(jnp.where(rows_r, own[-1], 0.0), at - 2 * side)
+        result += jnp.where(first, line_l, line_r)
+        for j in range(1, w + 1):
+            top, bottom = 16 * g + j, 16 * g + 8 + j
+            result = jnp.where(lane == top, own[j - 1][:, :1], result)
+            result = jnp.where(lane == bottom, own[j - 1][:, high - 1 : high], result)
+    return result.astype(BF16)
 
 
 def own_columns(plan, ref):
@@ -561,9 +629,14 @@
     return jnp.where(inside, pre * half, 0.0).astype(BF16), slope
 
 
-def go_back(plan, ids_ref, around, weight, slope, bwd_ref, inner):
-    wide_backward(plan, surroundings(plan, ids_ref, 1, *around), bwd_ref, inner)
-    grad = product(seam_weights(weight), bwd_ref[...], 1, 0)
+def go_back(plan, ids_ref, around, weight, slope, bwd_ref, inner, edge_ref=None):
+    wide_backward(plan, surroundings(plan, ids_ref, 1, *around), bwd_ref, inner, edge_ref)
+    if inner:
+        edges = product(tap_weights(weight, SEAMS), edge_ref[...], 1, 0)
+        grad = product(tap_weights(weight, TAPS), bwd_ref[...], 1, 0)
+        grad += from_edges(plan, ids_ref, edges)
+    else:
+        grad = product(seam_weights(weight), bwd_ref[...], 1, 0)
     inside = kept_lanes(plan, ids_ref, grad.shape, inner)
     return jnp.where(inside, grad * slope, 0.0).astype(BF16)
 
@@ -583,15 +656,19 @@
 def inner_kernel(plan, ids_ref, *refs):
     c = plan.channels
     around, tables, weights, refs = refs[:5], refs[5:8], refs[8:10], refs[10:]
-    hidden_ref, pre_grad_ref, mine_ref, theirs_ref, fwd_ref, bwd_ref, sums_ref, packed_ref = refs
+    hidden_ref, pre_grad_ref, mine_ref, theirs_ref, *refs = refs
+    fwd_ref, bwd_ref, edge_ref, sums_ref, packed_ref = refs
     around = with_seams(plan, ids_ref, around, tables)
     hidden, slope = go_forward(plan, ids_ref, around, weights[0], fwd_ref, True)
-    pre_grad = go_back(plan, ids_ref, around, weights[1], slope, bwd_ref, True)
+    pre_grad = go_back(plan, ids_ref, around, weights[1], slope, bwd_ref, True, edge_ref)
     hidden_ref[...] = hidden
     pre_grad_ref[...] = pre_grad
     terms = product(fwd_ref[...], pre_grad, 1, 1)
     turned = product(bwd_ref[...], hidden, 1, 1)
-    tap = [turned[i * c : (i + 1) * c] for i in range(21)]
+    edge_cells = to_edges(plan, ids_ref, hidden.astype(F32))
+    edges = product(edge_ref[...], edge_cells, 1, 1)
+    tap = [turned[i * c : (i + 1) * c] for i in range(9)]
+    tap += [edges[i * c : (i + 1) * c] for i in range(12)]
     for b in range(3):
         tap[b] = tap[b] + tap[9 + b]
         tap[6 + b] = tap[6 + b] + tap[12 + b]
@@ -639,25 +716,30 @@
             back_ref[:, g, i, :] = back[:, at : at + plan.height]
 
 
-def sum_kernel(plan, scale, ids_ref, mine_ref, theirs_ref, one_ref, two_ref, packed_ref, sums_ref):
+def sum_kernel(plan, scale, ids_ref, mine_ref, theirs_ref, one_ref, two_ref, packed_ref):
     near, mid = ids_ref[3], ids_ref[4]
     for d in range(plan.mid):
         spot = jnp.bitwise_xor(mid, d)
         for other, ref in ((0, mine_ref), (1, theirs_ref)):
             at = (jnp.bitwise_xor(near, other) * plan.mid + spot) * plan.piece
             packed_ref[pl.ds(pl.multiple_of(at, 16), plan.piece), :] = ref[d].astype(F32) * scale
-    c, shared = plan.channels, (plan.folds - 1) * plan.fold_rows
+    c, rows = plan.channels, one_ref.shape[0]
+
+    def store(at, value):
+        for start, ref in ((0, one_ref), (rows, two_ref)):
+            low = max(at, start)
+            high = min(at + value.shape[0], start + rows)
+            if low < high:
+                ref[low - start : high - start, :] = value[low - at : high - at]
+
     more = []
     for i in range(max(plan.folds - 1, 1)):
         at = i * plan.fold_rows
         block = packed_ref[at : at + plan.fold_rows, :]
-        sums_ref[at : at + plan.fold_rows, :] = block[:, :c]
+        store(at, block[:, :c])
         more.append(block[:, c:])
     if plan.folds > 1:
-        sums_ref[shared : shared + plan.fold_rows, :] = jnp.concatenate(more, axis=1)
-    rows = one_ref.shape[0]
-    one_ref[...] = sums_ref[:rows]
-    two_ref[...] = sums_ref[rows : 2 * rows]
+        store((plan.folds - 1) * plan.fold_rows, jnp.concatenate(more, axis=1))
 
 
 VMEM = pl.BlockSpec(memory_space=pltpu.VMEM)
@@ -780,7 +862,8 @@
         given + [fwd_one, bwd_two],
         [jax.ShapeDtypeStruct((c, inner), BF16)] * 2
         + [jax.ShapeDtypeStruct(piece, F32), jax.ShapeDtypeStruct(piece, BF16)],
-        taps(inner)
+        [pltpu.VMEM((9 * c, inner), BF16)] * 2
+        + [pltpu.VMEM((12 * c, n), BF16)]
         + [pltpu.VMEM((plan.terms, c), F32), pltpu.VMEM((rows, plan.wide), F32)],
     )
     theirs, given, hidden, pre_grad = lax.optimization_barrier((theirs, given, hidden, pre_grad))
@@ -823,7 +906,7 @@
         ids,
         [mine, theirs],
         [jax.ShapeDtypeStruct((9 * c, c), F32)] * 2,
-        [pltpu.VMEM((rows, plan.wide), F32), pltpu.VMEM((plan.terms, c), F32)],
+        [pltpu.VMEM((rows, plan.wide), F32)],
     )
     grads = []
     for i in range(2):

time: 53.1 us -> 52.7 us (level)
  no operation moved by 1% of the time
where the time goes in v5:
time: 52.7 us; the launch traced here: 52.4 us
  starting transfers between devices  25 us (47%)
  Pallas kernels  14.7 us (28%)
  waiting for transfers between devices  10.5 us (20%)
  local copies, waits for them, and re-layouts  1.16 us (2%)
  between operations  0.87 us (2%)
    pallas_call x6, Pallas kernels, call(): pl.pallas_call(body, out_shape=outs, in_specs=[SMEM] + [VMEM] * len(input...  14.7 us
    ppermute x11, starting transfers between devices, swapped(): return lax.ppermute(x, BOTH, pairs)  11.7 us
    all_to_all x1, waiting for transfers between devices, spread_blocks(): return lax.all_to_all(flat, BOTH, 0, 0, tiled=True).reshape(blocks.shape)  5.7 us
    ppermute x1, starting transfers between devices, across_faces(): return lax.ppermute(sent, BOTH, pairs)  4.85 us
    ppermute x1, starting transfers between devices, pair_up(): lax.ppermute(outer, 'tile', [(i, (i + 1 ^ 1) - 1 if i else t - 1) for i i...  4.37 us
    all_to_all x1, starting transfers between devices, spread_blocks(): return lax.all_to_all(flat, BOTH, 0, 0, tiled=True).reshape(blocks.shape)  4.08 us
    ppermute x11, waiting for transfers between devices, swapped(): return lax.ppermute(x, BOTH, pairs)  3.91 us
  transfers between devices with their start and end apart: 15, of which 6 were waited for; matrix products, arithmetic and copies ran while one was open for 0% of the time, Pallas kernels for 18%

profile of v5, /device:TPU:0, one launch (start us, length us, event | category | flops | bytes accessed | tf_op | source)
XLA Modules:
  0.0 52.4 jit_solution(14479132077323658916)
XLA Ops:
  0.6 1.0 %copy_bitcast_fusion = (bf16[1,96,2,2,96]{4,1,2,0,3:T(8,128)(2,1)S(1)}, bf16[1,96,2,2,96]{4,1,2,0,3:T(8,128)(2,1)S(1)}) fusion(bf16[96,2,2,96]{3,2,1,0:T(2,128)(2,1)} %param.9, bf16[96,2,2,96]{3,2,1,0:T(2,128)(2,1)} %param.8), kind=kLoop, calls=%fused_computation.5 | loop fusion | bytes 294912 | tf_op jit(solution)/shard_map/stack | solution.py:835
  1.7 0.0 copy-start.5
  1.7 4.8 %collective-permute-start = (bf16[2,2,2,96,128]{4,3,2,1,0:T(8,128)(2,1)S(1)}, bf16[2,2,2,96,128]{4,3,2,1,0:T(8,128)(2,1)S(1)}, u32[]{:S(2)}, u32[]{:S(2)}) collective-permute-start(bf16[2,2,2,96,128]{4,3,2,1,0:T(8,128)(2,1)S(1)} %pad.4.columns_ref.refs_0_), channel_id=1, source_target_pairs={{30,31},{31,30},{1,0},{0,1}} | collective-permute-start | bytes 589832 | tf_op jit(solution)/shard_map/ppermute | solution.py:766
  6.6 0.0 copy-start.4
  6.6 0.1 stack.48.ids_ref
  6.7 0.0 copy-done.5
  6.7 0.0 copy-start.2
  6.7 0.0 copy-start.3
  6.7 1.8 %shard_map.111 = bf16[16,2,24,96]{3,2,1,0:T(8,128)(2,1)} custom-call(s32[6]{0:T(128)S(1)} %stack.48.ids_ref, s32[3,1,768]{2,1,0:T(1,128)S(1)} %copy-done.5, bf16[2,2,2,96,128]{4,3,2,1,0:T(8,128)(2,1)S(1)} %pad.4.columns_ref.refs_0_), custom_call_target="tpu_custom_call" | custom-call | tf_op jit(solution)/shard_map/pallas_call | solution.py:750
  8.5 0.0 copy-start.1
  8.5 4.1 %all-to-all-start = ((bf16[32,24,96]{2,1,0:T(8,128)(2,1)}), bf16[32,24,96]{2,1,0:T(8,128)(2,1)S(1)}, u32[]{:S(2)}, u32[]{:S(2)}) async-start(bf16[32,24,96]{2,1,0:T(8,128)(2,1)} %bitcast.8), calls=%async_computation | async-start | bytes 393216 | tf_op jit(solution)/shard_map/all_to_all | solution.py:788
  12.6 0.0 copy-start
  12.6 0.0 collective-permute-done.refs_3_
  12.7 4.4 %collective-permute-start.2 = (bf16[2,2,2,96,128]{4,3,2,1,0:T(8,128)(2,1)S(1)}, bf16[2,2,2,96,128]{4,3,2,1,0:T(8,128)(2,1)S(1)}, u32[]{:S(2)}, u32[]{:S(2)}) collective-permute-start(bf16[2,2,2,96,128]{4,3,2,1,0:T(8,128)(2,1)S(1)} %maximum_select_fusion), channel_id=1, source_target_pairs={{0,30},{2,4},{4,2},{6,8},{8,6},{10,12},{12,10},{14,16},{16,14},{18... | collective-permute-start | bytes 589832 | tf_op jit(solution)/shard_map/ppermute | solution.py:781
  17.0 0.0 collective-permute-start.1
  17.0 5.7 %all-to-all-done = bf16[32,24,96]{2,1,0:T(8,128)(2,1)S(1)} async-done(((bf16[32,24,96]{2,1,0:T(8,128)(2,1)}), bf16[32,24,96]{2,1,0:T(8,128)(2,1)S(1)}, u32[]{:S(2)}, u32[]{:S(2)}) %all-to-all-start) | async-done | bytes 147488 | tf_op jit(solution)/shard_map/all_to_all | solution.py:788
  22.7 0.9 %collective-permute-done.2.refs_2_ = bf16[2,2,2,96,128]{4,3,2,1,0:T(8,128)(2,1)S(1)} collective-permute-done((bf16[2,2,2,96,128]{4,3,2,1,0:T(8,128)(2,1)S(1)}, bf16[2,2,2,96,128]{4,3,2,1,0:T(8,128)(2,1)S(1)}, u32[]{:S(2)}, u32[]{:S(2)}) %collective-permute-start.2) | collective-permute-done | bytes 196640 | tf_op jit(solution)/shard_map/ppermute | solution.py:781
  23.6 0.0 collective-permute-done.1.refs_1_
  23.6 0.0 copy-done.4
  23.6 0.0 copy-done.2
  23.6 0.0 copy-done.3
  23.6 0.0 copy-done.1
  23.6 0.0 copy-done
  23.6 3.5 %shard_map.112 = (bf16[96,512]{1,0:T(8,128)(2,1)S(1)}, bf16[96,512]{1,0:T(8,128)(2,1)S(1)}, f32[4,176,128]{2,1,0:T(8,128)S(1)}, bf16[4,176,128]{2,1,0:T(8,128)(2,1)S(1)}) custom-call(s32[6]{0:T(128)S(1)} %stack.48.ids_ref, bf16[2,2,2,96,128]{4,3,2,1,0:T(8,128)(2,1)S(1)} %pad.4.columns_ref.refs_0_, ...), custom_call_target="tpu_custom_call" | custom-call | tf_op jit(solution)/shard_map/pallas_call | solution.py:750
  27.1 0.1 collective-permute-start.3
  27.2 1.4 %collective-permute-done.3 = bf16[4,176,128]{2,1,0:T(8,128)(2,1)S(1)} collective-permute-done((bf16[4,176,128]{2,1,0:T(8,128)(2,1)S(1)}, bf16[4,176,128]{2,1,0:T(8,128)(2,1)S(1)}, u32[]{:S(2)}, u32[]{:S(2)}) %collective-permute-start.3) | collective-permute-done | bytes 180256 | tf_op jit(solution)/shard_map/ppermute | solution.py:798
  28.6 0.1 fusion.3
  28.7 1.5 %collective-permute-start.6 = (bf16[176,128]{1,0:T(8,128)(2,1)S(1)}, bf16[176,128]{1,0:T(8,128)(2,1)S(1)}, u32[]{:S(2)}, u32[]{:S(2)}) collective-permute-start(bf16[176,128]{1,0:T(8,128)(2,1)S(1)} %get-tuple-element.86), channel_id=1, source_target_pairs={{0,5},{1,4},{2,7},{3,6},{4,1},{5,0},{6,3},{7,2},{8,13},{9,12},{10,... | collective-permute-start | bytes 135176 | tf_op jit(solution)/shard_map/ppermute | solution.py:798
  30.2 1.4 %collective-permute-start.5 = (bf16[176,128]{1,0:T(8,128)(2,1)S(1)}, bf16[176,128]{1,0:T(8,128)(2,1)S(1)}, u32[]{:S(2)}, u32[]{:S(2)}) collective-permute-start(bf16[176,128]{1,0:T(8,128)(2,1)S(1)} %get-tuple-element.87), channel_id=1, source_target_pairs={{0,4},{1,5},{2,6},{3,7},{4,0},{5,1},{6,2},{7,3},{8,12},{9,13},{10,... | collective-permute-start | bytes 135176 | tf_op jit(solution)/shard_map/ppermute | solution.py:798
  31.6 0.7 %collective-permute-start.4 = (bf16[176,128]{1,0:T(8,128)(2,1)S(1)}, bf16[176,128]{1,0:T(8,128)(2,1)S(1)}, u32[]{:S(2)}, u32[]{:S(2)}) collective-permute-start(bf16[176,128]{1,0:T(8,128)(2,1)S(1)} %get-tuple-element.88), channel_id=1, source_target_pairs={{0,1},{1,0},{2,3},{3,2},{4,5},{5,4},{6,7},{7,6},{8,9},{9,8},{10,11... | collective-permute-start | bytes 135176 | tf_op jit(solution)/shard_map/ppermute | solution.py:798
  32.2 2.4 %shard_map.113 = (bf16[96,640]{1,0:T(8,128)(2,1)S(1)}, f32[96,640]{1,0:T(8,128)S(1)}) custom-call(s32[6]{0:T(128)S(1)} %stack.48.ids_ref, bf16[2,2,2,96,128]{4,3,2,1,0:T(8,128)(2,1)S(1)} %pad.4.columns_ref.refs_0_, bf16[2,2,2,96,128]{4,3,2,1,0:T(8,128)(2,1)S(1)} %collective-permute-done.1.refs_1_, ...), custom_call_target="tpu_custom_call" | custom-call | tf_op jit(solution)/shard_map/pallas_call | solution.py:750
  34.7 0.0 collective-permute-done.6
  34.7 0.0 collective-permute-done.5
  34.7 0.9 %collective-permute-done.4 = bf16[176,128]{1,0:T(8,128)(2,1)S(1)} collective-permute-done((bf16[176,128]{1,0:T(8,128)(2,1)S(1)}, bf16[176,128]{1,0:T(8,128)(2,1)S(1)}, u32[]{:S(2)}, u32[]{:S(2)}) %collective-permute-start.4) | collective-permute-done | bytes 45088 | tf_op jit(solution)/shard_map/ppermute | solution.py:798
  35.7 1.1 %collective-permute-start.9 = (bf16[176,128]{1,0:T(8,128)(2,1)S(1)}, bf16[176,128]{1,0:T(8,128)(2,1)S(1)}, u32[]{:S(2)}, u32[]{:S(2)}) collective-permute-start(bf16[176,128]{1,0:T(8,128)(2,1)S(1)} %fusion.2), channel_id=1, source_target_pairs={{0,24},{1,25},{2,26},{3,27},{4,28},{5,29},{6,30},{7,31},{8,16},{9,... | collective-permute-start | bytes 135176 | tf_op jit(solution)/shard_map/ppermute | solution.py:798
  36.8 0.9 %collective-permute-start.8 = (bf16[176,128]{1,0:T(8,128)(2,1)S(1)}, bf16[176,128]{1,0:T(8,128)(2,1)S(1)}, u32[]{:S(2)}, u32[]{:S(2)}) collective-permute-start(bf16[176,128]{1,0:T(8,128)(2,1)S(1)} %fusion.2), channel_id=1, source_target_pairs={{0,16},{1,17},{2,18},{3,19},{4,20},{5,21},{6,22},{7,23},{8,24},{9,... | collective-permute-start | bytes 135176 | tf_op jit(solution)/shard_map/ppermute | solution.py:798
  37.7 2.4 %collective-permute-start.7 = (bf16[176,128]{1,0:T(8,128)(2,1)S(1)}, bf16[176,128]{1,0:T(8,128)(2,1)S(1)}, u32[]{:S(2)}, u32[]{:S(2)}) collective-permute-start(bf16[176,128]{1,0:T(8,128)(2,1)S(1)} %fusion.2), channel_id=1, source_target_pairs={{0,8},{1,9},{2,10},{3,11},{4,12},{5,13},{6,14},{7,15},{8,0},{9,1},... | collective-permute-start | bytes 135176 | tf_op jit(solution)/shard_map/ppermute | solution.py:798
  40.1 2.3 %shard_map.114.pre_grad_out = bf16[96,640]{1,0:T(8,128)(2,1)S(1)} custom-call(s32[6]{0:T(128)S(1)} %stack.48.ids_ref, bf16[2,2,2,96,128]{4,3,2,1,0:T(8,128)(2,1)S(1)} %pad.4.columns_ref.refs_0_, bf16[2,2,2,96,128]{4,3,2,1,0:T(8,128)(2,1)S(1)} %collective-permute-done.1.refs_1_, bf16[2,2,2,96,128]{4,3,2,1,0:T(8,128)(2,1)S(1)} %collective-permute-done.2.refs_2_, ...), custom_call_target="tpu_custom_call" | custom-call | tf_op jit(solution)/shard_map/pallas_call | solution.py:750
  42.4 0.0 collective-permute-done.9
  42.4 0.2 collective-permute-done.8
  42.6 0.0 collective-permute-done.7
  42.6 0.9 %collective-permute-start.12 = (bf16[176,128]{1,0:T(8,128)(2,1)S(1)}, bf16[176,128]{1,0:T(8,128)(2,1)S(1)}, u32[]{:S(2)}, u32[]{:S(2)}) collective-permute-start(bf16[176,128]{1,0:T(8,128)(2,1)S(1)} %add_convert_fusion), channel_id=1, source_target_pairs={{0,5},{1,4},{2,7},{3,6},{4,1},{5,0},{6,3},{7,2},{8,13},{9,12},{10,... | collective-permute-start | bytes 135176 | tf_op jit(solution)/shard_map/ppermute | solution.py:798
  43.6 1.3 %collective-permute-start.11 = (bf16[176,128]{1,0:T(8,128)(2,1)S(1)}, bf16[176,128]{1,0:T(8,128)(2,1)S(1)}, u32[]{:S(2)}, u32[]{:S(2)}) collective-permute-start(bf16[176,128]{1,0:T(8,128)(2,1)S(1)} %add_convert_fusion), channel_id=1, source_target_pairs={{0,4},{1,5},{2,6},{3,7},{4,0},{5,1},{6,2},{7,3},{8,12},{9,13},{10,... | collective-permute-start | bytes 135176 | tf_op jit(solution)/shard_map/ppermute | solution.py:798
  44.8 1.3 %collective-permute-start.10 = (bf16[176,128]{1,0:T(8,128)(2,1)S(1)}, bf16[176,128]{1,0:T(8,128)(2,1)S(1)}, u32[]{:S(2)}, u32[]{:S(2)}) collective-permute-start(bf16[176,128]{1,0:T(8,128)(2,1)S(1)} %add_convert_fusion), channel_id=1, source_target_pairs={{0,1},{1,0},{2,3},{3,2},{4,5},{5,4},{6,7},{7,6},{8,9},{9,8},{10,11... | collective-permute-start | bytes 135176 | tf_op jit(solution)/shard_map/ppermute | solution.py:798
  46.2 3.1 %shard_map.115 = (bf16[96,2,2,96]{3,2,1,0:T(2,128)(2,1)}, bf16[96,2,2,96]{3,2,1,0:T(2,128)(2,1)}) custom-call(s32[6]{0:T(128)S(1)} %stack.48.ids_ref, bf16[96,512]{1,0:T(8,128)(2,1)S(1)} %get-tuple-element.68.hidden_ref, bf16[96,512]{1,0:T(8,128)(2,1)S(1)} %get-tuple-element.69.pre_grad_ref, bf16[96,640]{1,0:T(8,128)(2,1)S(1)} %get-tuple-element.70.hidden_out, ...), custom_call_target="tpu_custom_call" | custom-call | tf_op jit(solution)/shard_map/pallas_call | solution.py:750
  49.3 0.0 collective-permute-done.12
  49.3 0.0 collective-permute-done.11
  49.3 0.0 collective-permute-done.10
  49.4 0.1 collective-permute-start.13
  49.4 1.4 %collective-permute-done.13.theirs_ref = bf16[4,176,128]{2,1,0:T(8,128)(2,1)S(1)} collective-permute-done((bf16[4,176,128]{2,1,0:T(8,128)(2,1)S(1)}, bf16[4,176,128]{2,1,0:T(8,128)(2,1)S(1)}, u32[]{:S(2)}, u32[]{:S(2)}) %collective-permute-start.13) | collective-permute-done | bytes 180256 | tf_op jit(solution)/shard_map/ppermute | solution.py:798
  50.8 1.6 %shard_map.116 = (f32[864,96]{1,0:T(8,128)}, f32[864,96]{1,0:T(8,128)}) custom-call(s32[6]{0:T(128)S(1)} %stack.48.ids_ref, bf16[4,176,128]{2,1,0:T(8,128)(2,1)S(1)} %pad_maximum_fusion.mine_ref, bf16[4,176,128]{2,1,0:T(8,128)(2,1)S(1)} %collective-permute-done.13.theirs_ref), custom_call_target="tpu_custom_call" | custom-call | tf_op jit(solution)/shard_map/pallas_call | solution.py:750
  (9 shorter events, 0.2 us)
Async XLA Ops:
  1.7 5.0 %copy-start.5 = (s32[3,1,768]{2,1,0:T(1,128)S(1)}, s32[3,1,768]{2,1,0:T(1,128)}, u32[]{:S(2)}) copy-start(s32[3,1,768]{2,1,0:T(1,128)} %constant.36.clone.table_ref) | copy-start | bytes 27652
  1.7 10.9 %collective-permute-start = (bf16[2,2,2,96,128]{4,3,2,1,0:T(8,128)(2,1)S(1)}, bf16[2,2,2,96,128]{4,3,2,1,0:T(8,128)(2,1)S(1)}, u32[]{:S(2)}, u32[]{:S(2)}) collective-permute-start(bf16[2,2,2,96,128]{4,3,2,1,0:T(8,128)(2,1)S(1)} %pad.4.columns_ref.refs_0_), channel_id=1, source_target_pairs={{30,31},{31,30},{1,0},{0,1}} | collective-permute-start | bytes 589832 | tf_op jit(solution)/shard_map/ppermute | solution.py:766
  6.6 17.0 %copy-start.4 = (bf16[768,128]{1,0:T(8,128)(2,1)S(1)}, bf16[768,128]{1,0:T(8,128)(2,1)}, u32[]{:S(2)}) copy-start(bf16[768,128]{1,0:T(8,128)(2,1)} %constant.39.clone.refs_7_) | copy-start | bytes 589828
  6.7 16.9 %copy-start.2 = (bf16[3,3,96,96]{3,2,1,0:T(8,128)(2,1)S(1)}, bf16[3,3,96,96]{3,2,1,0:T(8,128)(2,1)}, u32[]{:S(2)}) copy-start(bf16[3,3,96,96]{3,2,1,0:T(8,128)(2,1)} %param.10) | copy-start | bytes 497668
  6.7 16.9 %copy-start.3 = (bf16[3,3,96,96]{3,2,1,0:T(8,128)(2,1)S(1)}, bf16[3,3,96,96]{3,2,1,0:T(8,128)(2,1)}, u32[]{:S(2)}) copy-start(bf16[3,3,96,96]{3,2,1,0:T(8,128)(2,1)} %param.11) | copy-start | bytes 497668
  8.5 15.2 %copy-start.1 = (bf16[384,1024]{1,0:T(8,128)(2,1)S(1)}, bf16[384,1024]{1,0:T(8,128)(2,1)}, u32[]{:S(2)}) copy-start(bf16[384,1024]{1,0:T(8,128)(2,1)} %constant.37.clone.refs_5_) | copy-start | bytes 2359300
  8.5 14.3 %all-to-all-start = ((bf16[32,24,96]{2,1,0:T(8,128)(2,1)}), bf16[32,24,96]{2,1,0:T(8,128)(2,1)S(1)}, u32[]{:S(2)}, u32[]{:S(2)}) async-start(bf16[32,24,96]{2,1,0:T(8,128)(2,1)} %bitcast.8), calls=%async_computation | async-start | bytes 393216 | tf_op jit(solution)/shard_map/all_to_all | solution.py:788
  12.6 11.1 %copy-start = (bf16[384,1024]{1,0:T(8,128)(2,1)S(1)}, bf16[384,1024]{1,0:T(8,128)(2,1)}, u32[]{:S(2)}) copy-start(bf16[384,1024]{1,0:T(8,128)(2,1)} %constant.38.clone.refs_6_) | copy-start | bytes 2359300
  12.7 10.9 %collective-permute-start.2 = (bf16[2,2,2,96,128]{4,3,2,1,0:T(8,128)(2,1)S(1)}, bf16[2,2,2,96,128]{4,3,2,1,0:T(8,128)(2,1)S(1)}, u32[]{:S(2)}, u32[]{:S(2)}) collective-permute-start(bf16[2,2,2,96,128]{4,3,2,1,0:T(8,128)(2,1)S(1)} %maximum_select_fusion), channel_id=1, source_target_pairs={{0,30},{2,4},{4,2},{6,8},{8,6},{10,12},{12,10},{14,16},{16,14},{18... | collective-permute-start | bytes 589832 | tf_op jit(solution)/shard_map/ppermute | solution.py:781
  17.0 6.6 %collective-permute-start.1 = (bf16[2,2,2,96,128]{4,3,2,1,0:T(8,128)(2,1)S(1)}, bf16[2,2,2,96,128]{4,3,2,1,0:T(8,128)(2,1)S(1)}, u32[]{:S(2)}, u32[]{:S(2)}) collective-permute-start(bf16[2,2,2,96,128]{4,3,2,1,0:T(8,128)(2,1)S(1)} %pad.4.columns_ref.refs_0_), channel_id=1, source_target_pairs={{0,2},{2,0},{4,6},{6,4},{8,10},{10,8},{12,14},{14,12},{16,18},{18,... | collective-permute-start | bytes 589832 | tf_op jit(solution)/shard_map/ppermute | solution.py:780
  27.1 1.5 %collective-permute-start.3 = (bf16[4,176,128]{2,1,0:T(8,128)(2,1)S(1)}, bf16[4,176,128]{2,1,0:T(8,128)(2,1)S(1)}, u32[]{:S(2)}, u32[]{:S(2)}) collective-permute-start(bf16[4,176,128]{2,1,0:T(8,128)(2,1)S(1)} %get-tuple-element.49), channel_id=1, source_target_pairs={{0,2},{1,3},{2,0},{3,1},{4,6},{5,7},{6,4},{7,5},{8,10},{9,11},{10,... | collective-permute-start | bytes 540680 | tf_op jit(solution)/shard_map/ppermute | solution.py:798
  28.7 6.0 %collective-permute-start.6 = (bf16[176,128]{1,0:T(8,128)(2,1)S(1)}, bf16[176,128]{1,0:T(8,128)(2,1)S(1)}, u32[]{:S(2)}, u32[]{:S(2)}) collective-permute-start(bf16[176,128]{1,0:T(8,128)(2,1)S(1)} %get-tuple-element.86), channel_id=1, source_target_pairs={{0,5},{1,4},{2,7},{3,6},{4,1},{5,0},{6,3},{7,2},{8,13},{9,12},{10,... | collective-permute-start | bytes 135176 | tf_op jit(solution)/shard_map/ppermute | solution.py:798
  30.2 4.5 %collective-permute-start.5 = (bf16[176,128]{1,0:T(8,128)(2,1)S(1)}, bf16[176,128]{1,0:T(8,128)(2,1)S(1)}, u32[]{:S(2)}, u32[]{:S(2)}) collective-permute-start(bf16[176,128]{1,0:T(8,128)(2,1)S(1)} %get-tuple-element.87), channel_id=1, source_target_pairs={{0,4},{1,5},{2,6},{3,7},{4,0},{5,1},{6,2},{7,3},{8,12},{9,13},{10,... | collective-permute-start | bytes 135176 | tf_op jit(solution)/shard_map/ppermute | solution.py:798
  31.6 4.0 %collective-permute-start.4 = (bf16[176,128]{1,0:T(8,128)(2,1)S(1)}, bf16[176,128]{1,0:T(8,128)(2,1)S(1)}, u32[]{:S(2)}, u32[]{:S(2)}) collective-permute-start(bf16[176,128]{1,0:T(8,128)(2,1)S(1)} %get-tuple-element.88), channel_id=1, source_target_pairs={{0,1},{1,0},{2,3},{3,2},{4,5},{5,4},{6,7},{7,6},{8,9},{9,8},{10,11... | collective-permute-start | bytes 135176 | tf_op jit(solution)/shard_map/ppermute | solution.py:798
  35.7 6.7 %collective-permute-start.9 = (bf16[176,128]{1,0:T(8,128)(2,1)S(1)}, bf16[176,128]{1,0:T(8,128)(2,1)S(1)}, u32[]{:S(2)}, u32[]{:S(2)}) collective-permute-start(bf16[176,128]{1,0:T(8,128)(2,1)S(1)} %fusion.2), channel_id=1, source_target_pairs={{0,24},{1,25},{2,26},{3,27},{4,28},{5,29},{6,30},{7,31},{8,16},{9,... | collective-permute-start | bytes 135176 | tf_op jit(solution)/shard_map/ppermute | solution.py:798
  36.8 5.8 %collective-permute-start.8 = (bf16[176,128]{1,0:T(8,128)(2,1)S(1)}, bf16[176,128]{1,0:T(8,128)(2,1)S(1)}, u32[]{:S(2)}, u32[]{:S(2)}) collective-permute-start(bf16[176,128]{1,0:T(8,128)(2,1)S(1)} %fusion.2), channel_id=1, source_target_pairs={{0,16},{1,17},{2,18},{3,19},{4,20},{5,21},{6,22},{7,23},{8,24},{9,... | collective-permute-start | bytes 135176 | tf_op jit(solution)/shard_map/ppermute | solution.py:798
  37.7 4.8 %collective-permute-start.7 = (bf16[176,128]{1,0:T(8,128)(2,1)S(1)}, bf16[176,128]{1,0:T(8,128)(2,1)S(1)}, u32[]{:S(2)}, u32[]{:S(2)}) collective-permute-start(bf16[176,128]{1,0:T(8,128)(2,1)S(1)} %fusion.2), channel_id=1, source_target_pairs={{0,8},{1,9},{2,10},{3,11},{4,12},{5,13},{6,14},{7,15},{8,0},{9,1},... | collective-permute-start | bytes 135176 | tf_op jit(solution)/shard_map/ppermute | solution.py:798
  42.6 6.7 %collective-permute-start.12 = (bf16[176,128]{1,0:T(8,128)(2,1)S(1)}, bf16[176,128]{1,0:T(8,128)(2,1)S(1)}, u32[]{:S(2)}, u32[]{:S(2)}) collective-permute-start(bf16[176,128]{1,0:T(8,128)(2,1)S(1)} %add_convert_fusion), channel_id=1, source_target_pairs={{0,5},{1,4},{2,7},{3,6},{4,1},{5,0},{6,3},{7,2},{8,13},{9,12},{10,... | collective-permute-start | bytes 135176 | tf_op jit(solution)/shard_map/ppermute | solution.py:798
  43.6 5.8 %collective-permute-start.11 = (bf16[176,128]{1,0:T(8,128)(2,1)S(1)}, bf16[176,128]{1,0:T(8,128)(2,1)S(1)}, u32[]{:S(2)}, u32[]{:S(2)}) collective-permute-start(bf16[176,128]{1,0:T(8,128)(2,1)S(1)} %add_convert_fusion), channel_id=1, source_target_pairs={{0,4},{1,5},{2,6},{3,7},{4,0},{5,1},{6,2},{7,3},{8,12},{9,13},{10,... | collective-permute-start | bytes 135176 | tf_op jit(solution)/shard_map/ppermute | solution.py:798
  44.8 4.5 %collective-permute-start.10 = (bf16[176,128]{1,0:T(8,128)(2,1)S(1)}, bf16[176,128]{1,0:T(8,128)(2,1)S(1)}, u32[]{:S(2)}, u32[]{:S(2)}) collective-permute-start(bf16[176,128]{1,0:T(8,128)(2,1)S(1)} %add_convert_fusion), channel_id=1, source_target_pairs={{0,1},{1,0},{2,3},{3,2},{4,5},{5,4},{6,7},{7,6},{8,9},{9,8},{10,11... | collective-permute-start | bytes 135176 | tf_op jit(solution)/shard_map/ppermute | solution.py:798
  49.4 1.5 %collective-permute-start.13 = (bf16[4,176,128]{2,1,0:T(8,128)(2,1)S(1)}, bf16[4,176,128]{2,1,0:T(8,128)(2,1)S(1)}, u32[]{:S(2)}, u32[]{:S(2)}) collective-permute-start(bf16[4,176,128]{2,1,0:T(8,128)(2,1)S(1)} %pad_maximum_fusion.mine_ref), channel_id=1, source_target_pairs={{0,2},{1,3},{2,0},{3,1},{4,6},{5,7},{6,4},{7,5},{8,10},{9,11},{10,... | collective-permute-start | bytes 540680 | tf_op jit(solution)/shard_map/ppermute | solution.py:798

commit v6 on v5

--- a/solution.py
+++ b/solution.py
@@ -139,7 +139,7 @@
             block = jnp.where(face == dest, both[:, 0], both[:, 1])
         else:
             block = both[:, 0]
-        blocks_ref[:, dest] = block.astype(BF16)
+        blocks_ref[dest] = block.astype(BF16)
 
 
 def product(x, y, x_dim, y_dim):
@@ -160,7 +160,7 @@
         face_b = face if g > 0 else before
         pair = []
         for at, table in ((face_a, tab_a), (face_b, tab_b)):
-            rows = got_ref[:, at].astype(F32)
+            rows = got_ref[at].astype(F32)
             rows = rows.reshape(plan.tiles * plan.block, rows.shape[-1])
             pair.append(product(rows.astype(BF16), table[...], 0, 0))
         result.append(pair)
@@ -785,7 +785,7 @@
 def spread_blocks(plan, blocks):
     count = plan.tiles * plan.faces
     flat = blocks.reshape((count,) + blocks.shape[2:])
-    return lax.all_to_all(flat, BOTH, 0, 0, tiled=True).reshape(blocks.shape)
+    return lax.all_to_all(flat, ("face", "tile"), 0, 0, tiled=True).reshape(blocks.shape)
 
 
 def swapped(plan, x, near=0, mid=0, far=0):
@@ -834,7 +834,7 @@
 
     both = jnp.stack([fields, upstream]).transpose(3, 0, 2, 1, 4)
     columns = jnp.pad(both, ((0, 0),) * 4 + ((0, n - h),))
-    blocks_shape = jax.ShapeDtypeStruct((plan.tiles, plan.faces, plan.block, c), BF16)
+    blocks_shape = jax.ShapeDtypeStruct((plan.faces, plan.tiles, plan.block, c), BF16)
     (blocks,) = call(
         functools.partial(first_kernel, plan), ids, [plan.send_table(), columns], [blocks_shape]
     )

time: 52.7 us -> 52.7 us (level)
    all_to_all x1, waiting for transfers between devices: 5.7 us -> 4.4 us  [spread_blocks(): lax.all_to_all(flat, ('face', 'tile'), 0, 0, tiled=True)]
    ppermute x1, waiting for transfers between devices: 0.86 us -> 2.1 us  [pair_up(): lax.ppermute(outer, 'tile', [(i, (i + 1 ^ 1) - 1 if i else t - 1) for i i...]
where the time goes in v6:
time: 52.7 us; the launch traced here: 52.4 us
  starting transfers between devices  25 us (47%)
  Pallas kernels  14.7 us (28%)
  waiting for transfers between devices  10.5 us (20%)
  local copies, waits for them, and re-layouts  1.16 us (2%)
  between operations  0.87 us (2%)
    pallas_call x6, Pallas kernels, call(): pl.pallas_call(body, out_shape=outs, in_specs=[SMEM] + [VMEM] * len(input...  14.7 us
    ppermute x11, starting transfers between devices, swapped(): return lax.ppermute(x, BOTH, pairs)  11.7 us
    ppermute x1, starting transfers between devices, across_faces(): return lax.ppermute(sent, BOTH, pairs)  4.85 us
    all_to_all x1, waiting for transfers between devices, spread_blocks(): lax.all_to_all(flat, ('face', 'tile'), 0, 0, tiled=True)  4.4 us
    ppermute x1, starting transfers between devices, pair_up(): lax.ppermute(outer, 'tile', [(i, (i + 1 ^ 1) - 1 if i else t - 1) for i i...  4.37 us
    all_to_all x1, starting transfers between devices, spread_blocks(): lax.all_to_all(flat, ('face', 'tile'), 0, 0, tiled=True)  4.08 us
    ppermute x11, waiting for transfers between devices, swapped(): return lax.ppermute(x, BOTH, pairs)  3.96 us
    ppermute x1, waiting for transfers between devices, pair_up(): lax.ppermute(outer, 'tile', [(i, (i + 1 ^ 1) - 1 if i else t - 1) for i i...  2.1 us
  transfers between devices with their start and end apart: 15, of which 6 were waited for; matrix products, arithmetic and copies ran while one was open for 0% of the time, Pallas kernels for 18%

profile of v6, /device:TPU:0, one launch (start us, length us, event | category | flops | bytes accessed | tf_op | source)
XLA Modules:
  0.0 52.4 jit_solution(14661798355636464102)
XLA Ops:
  0.6 1.0 %copy_bitcast_fusion = (bf16[1,96,2,2,96]{4,1,2,0,3:T(8,128)(2,1)S(1)}, bf16[1,96,2,2,96]{4,1,2,0,3:T(8,128)(2,1)S(1)}) fusion(bf16[96,2,2,96]{3,2,1,0:T(2,128)(2,1)} %param.9, bf16[96,2,2,96]{3,2,1,0:T(2,128)(2,1)} %param.8), kind=kLoop, calls=%fused_computation.5 | loop fusion | bytes 294912 | tf_op jit(solution)/shard_map/stack | solution.py:835
  1.7 0.0 copy-start.5
  1.7 4.8 %collective-permute-start = (bf16[2,2,2,96,128]{4,3,2,1,0:T(8,128)(2,1)S(1)}, bf16[2,2,2,96,128]{4,3,2,1,0:T(8,128)(2,1)S(1)}, u32[]{:S(2)}, u32[]{:S(2)}) collective-permute-start(bf16[2,2,2,96,128]{4,3,2,1,0:T(8,128)(2,1)S(1)} %pad.4.columns_ref.refs_0_), channel_id=1, source_target_pairs={{30,31},{31,30},{1,0},{0,1}} | collective-permute-start | bytes 589832 | tf_op jit(solution)/shard_map/ppermute | solution.py:766
  6.6 0.0 copy-start.4
  6.6 0.1 stack.48.ids_ref
  6.7 0.0 copy-done.5
  6.7 0.0 copy-start.2
  6.7 0.0 copy-start.3
  6.7 1.8 %shard_map.111 = bf16[2,16,24,96]{3,2,1,0:T(8,128)(2,1)} custom-call(s32[6]{0:T(128)S(1)} %stack.48.ids_ref, s32[3,1,768]{2,1,0:T(1,128)S(1)} %copy-done.5, bf16[2,2,2,96,128]{4,3,2,1,0:T(8,128)(2,1)S(1)} %pad.4.columns_ref.refs_0_), custom_call_target="tpu_custom_call" | custom-call | tf_op jit(solution)/shard_map/pallas_call | solution.py:750
  8.5 0.0 copy-start.1
  8.5 4.1 %all-to-all-start = ((bf16[32,24,96]{2,1,0:T(8,128)(2,1)}), bf16[32,24,96]{2,1,0:T(8,128)(2,1)S(1)}, u32[]{:S(2)}, u32[]{:S(2)}) async-start(bf16[32,24,96]{2,1,0:T(8,128)(2,1)} %bitcast.8), calls=%async_computation | async-start | bytes 393216 | tf_op jit(solution)/shard_map/all_to_all | solution.py:788
  12.6 0.0 copy-start
  12.6 0.0 collective-permute-done.refs_3_
  12.7 4.4 %collective-permute-start.2 = (bf16[2,2,2,96,128]{4,3,2,1,0:T(8,128)(2,1)S(1)}, bf16[2,2,2,96,128]{4,3,2,1,0:T(8,128)(2,1)S(1)}, u32[]{:S(2)}, u32[]{:S(2)}) collective-permute-start(bf16[2,2,2,96,128]{4,3,2,1,0:T(8,128)(2,1)S(1)} %maximum_select_fusion), channel_id=1, source_target_pairs={{0,30},{2,4},{4,2},{6,8},{8,6},{10,12},{12,10},{14,16},{16,14},{18... | collective-permute-start | bytes 589832 | tf_op jit(solution)/shard_map/ppermute | solution.py:781
  17.0 0.0 collective-permute-start.1
  17.0 4.4 %all-to-all-done = bf16[32,24,96]{2,1,0:T(8,128)(2,1)S(1)} async-done(((bf16[32,24,96]{2,1,0:T(8,128)(2,1)}), bf16[32,24,96]{2,1,0:T(8,128)(2,1)S(1)}, u32[]{:S(2)}, u32[]{:S(2)}) %all-to-all-start) | async-done | bytes 147488 | tf_op jit(solution)/shard_map/all_to_all | solution.py:788
  21.4 2.1 %collective-permute-done.2.refs_2_ = bf16[2,2,2,96,128]{4,3,2,1,0:T(8,128)(2,1)S(1)} collective-permute-done((bf16[2,2,2,96,128]{4,3,2,1,0:T(8,128)(2,1)S(1)}, bf16[2,2,2,96,128]{4,3,2,1,0:T(8,128)(2,1)S(1)}, u32[]{:S(2)}, u32[]{:S(2)}) %collective-permute-start.2) | collective-permute-done | bytes 196640 | tf_op jit(solution)/shard_map/ppermute | solution.py:781
  23.5 0.0 collective-permute-done.1.refs_1_
  23.5 0.0 copy-done.4
  23.5 0.0 copy-done.2
  23.5 0.0 copy-done.3
  23.6 0.0 copy-done.1
  23.6 0.0 copy-done
  23.6 3.5 %shard_map.112 = (bf16[96,512]{1,0:T(8,128)(2,1)S(1)}, bf16[96,512]{1,0:T(8,128)(2,1)S(1)}, f32[4,176,128]{2,1,0:T(8,128)S(1)}, bf16[4,176,128]{2,1,0:T(8,128)(2,1)S(1)}) custom-call(s32[6]{0:T(128)S(1)} %stack.48.ids_ref, bf16[2,2,2,96,128]{4,3,2,1,0:T(8,128)(2,1)S(1)} %pad.4.columns_ref.refs_0_, ...), custom_call_target="tpu_custom_call" | custom-call | tf_op jit(solution)/shard_map/pallas_call | solution.py:750
  27.1 0.1 collective-permute-start.3
  27.1 1.4 %collective-permute-done.3 = bf16[4,176,128]{2,1,0:T(8,128)(2,1)S(1)} collective-permute-done((bf16[4,176,128]{2,1,0:T(8,128)(2,1)S(1)}, bf16[4,176,128]{2,1,0:T(8,128)(2,1)S(1)}, u32[]{:S(2)}, u32[]{:S(2)}) %collective-permute-start.3) | collective-permute-done | bytes 180256 | tf_op jit(solution)/shard_map/ppermute | solution.py:798
  28.6 0.1 fusion.3
  28.6 1.5 %collective-permute-start.6 = (bf16[176,128]{1,0:T(8,128)(2,1)S(1)}, bf16[176,128]{1,0:T(8,128)(2,1)S(1)}, u32[]{:S(2)}, u32[]{:S(2)}) collective-permute-start(bf16[176,128]{1,0:T(8,128)(2,1)S(1)} %get-tuple-element.86), channel_id=1, source_target_pairs={{0,5},{1,4},{2,7},{3,6},{4,1},{5,0},{6,3},{7,2},{8,13},{9,12},{10,... | collective-permute-start | bytes 135176 | tf_op jit(solution)/shard_map/ppermute | solution.py:798
  30.2 1.4 %collective-permute-start.5 = (bf16[176,128]{1,0:T(8,128)(2,1)S(1)}, bf16[176,128]{1,0:T(8,128)(2,1)S(1)}, u32[]{:S(2)}, u32[]{:S(2)}) collective-permute-start(bf16[176,128]{1,0:T(8,128)(2,1)S(1)} %get-tuple-element.87), channel_id=1, source_target_pairs={{0,4},{1,5},{2,6},{3,7},{4,0},{5,1},{6,2},{7,3},{8,12},{9,13},{10,... | collective-permute-start | bytes 135176 | tf_op jit(solution)/shard_map/ppermute | solution.py:798
  31.6 0.6 %collective-permute-start.4 = (bf16[176,128]{1,0:T(8,128)(2,1)S(1)}, bf16[176,128]{1,0:T(8,128)(2,1)S(1)}, u32[]{:S(2)}, u32[]{:S(2)}) collective-permute-start(bf16[176,128]{1,0:T(8,128)(2,1)S(1)} %get-tuple-element.88), channel_id=1, source_target_pairs={{0,1},{1,0},{2,3},{3,2},{4,5},{5,4},{6,7},{7,6},{8,9},{9,8},{10,11... | collective-permute-start | bytes 135176 | tf_op jit(solution)/shard_map/ppermute | solution.py:798
  32.2 2.4 %shard_map.113 = (bf16[96,640]{1,0:T(8,128)(2,1)S(1)}, f32[96,640]{1,0:T(8,128)S(1)}) custom-call(s32[6]{0:T(128)S(1)} %stack.48.ids_ref, bf16[2,2,2,96,128]{4,3,2,1,0:T(8,128)(2,1)S(1)} %pad.4.columns_ref.refs_0_, bf16[2,2,2,96,128]{4,3,2,1,0:T(8,128)(2,1)S(1)} %collective-permute-done.1.refs_1_, ...), custom_call_target="tpu_custom_call" | custom-call | tf_op jit(solution)/shard_map/pallas_call | solution.py:750
  34.6 0.0 collective-permute-done.6
  34.6 0.0 collective-permute-done.5
  34.7 0.9 %collective-permute-done.4 = bf16[176,128]{1,0:T(8,128)(2,1)S(1)} collective-permute-done((bf16[176,128]{1,0:T(8,128)(2,1)S(1)}, bf16[176,128]{1,0:T(8,128)(2,1)S(1)}, u32[]{:S(2)}, u32[]{:S(2)}) %collective-permute-start.4) | collective-permute-done | bytes 45088 | tf_op jit(solution)/shard_map/ppermute | solution.py:798
  35.6 1.2 %collective-permute-start.9 = (bf16[176,128]{1,0:T(8,128)(2,1)S(1)}, bf16[176,128]{1,0:T(8,128)(2,1)S(1)}, u32[]{:S(2)}, u32[]{:S(2)}) collective-permute-start(bf16[176,128]{1,0:T(8,128)(2,1)S(1)} %fusion.2), channel_id=1, source_target_pairs={{0,24},{1,25},{2,26},{3,27},{4,28},{5,29},{6,30},{7,31},{8,16},{9,... | collective-permute-start | bytes 135176 | tf_op jit(solution)/shard_map/ppermute | solution.py:798
  36.8 1.0 %collective-permute-start.8 = (bf16[176,128]{1,0:T(8,128)(2,1)S(1)}, bf16[176,128]{1,0:T(8,128)(2,1)S(1)}, u32[]{:S(2)}, u32[]{:S(2)}) collective-permute-start(bf16[176,128]{1,0:T(8,128)(2,1)S(1)} %fusion.2), channel_id=1, source_target_pairs={{0,16},{1,17},{2,18},{3,19},{4,20},{5,21},{6,22},{7,23},{8,24},{9,... | collective-permute-start | bytes 135176 | tf_op jit(solution)/shard_map/ppermute | solution.py:798
  37.8 2.3 %collective-permute-start.7 = (bf16[176,128]{1,0:T(8,128)(2,1)S(1)}, bf16[176,128]{1,0:T(8,128)(2,1)S(1)}, u32[]{:S(2)}, u32[]{:S(2)}) collective-permute-start(bf16[176,128]{1,0:T(8,128)(2,1)S(1)} %fusion.2), channel_id=1, source_target_pairs={{0,8},{1,9},{2,10},{3,11},{4,12},{5,13},{6,14},{7,15},{8,0},{9,1},... | collective-permute-start | bytes 135176 | tf_op jit(solution)/shard_map/ppermute | solution.py:798
  40.1 2.3 %shard_map.114.pre_grad_out = bf16[96,640]{1,0:T(8,128)(2,1)S(1)} custom-call(s32[6]{0:T(128)S(1)} %stack.48.ids_ref, bf16[2,2,2,96,128]{4,3,2,1,0:T(8,128)(2,1)S(1)} %pad.4.columns_ref.refs_0_, bf16[2,2,2,96,128]{4,3,2,1,0:T(8,128)(2,1)S(1)} %collective-permute-done.1.refs_1_, bf16[2,2,2,96,128]{4,3,2,1,0:T(8,128)(2,1)S(1)} %collective-permute-done.2.refs_2_, ...), custom_call_target="tpu_custom_call" | custom-call | tf_op jit(solution)/shard_map/pallas_call | solution.py:750
  42.4 0.0 collective-permute-done.9
  42.4 0.2 collective-permute-done.8
  42.6 0.0 collective-permute-done.7
  42.6 1.5 %collective-permute-start.12 = (bf16[176,128]{1,0:T(8,128)(2,1)S(1)}, bf16[176,128]{1,0:T(8,128)(2,1)S(1)}, u32[]{:S(2)}, u32[]{:S(2)}) collective-permute-start(bf16[176,128]{1,0:T(8,128)(2,1)S(1)} %add_convert_fusion), channel_id=1, source_target_pairs={{0,5},{1,4},{2,7},{3,6},{4,1},{5,0},{6,3},{7,2},{8,13},{9,12},{10,... | collective-permute-start | bytes 135176 | tf_op jit(solution)/shard_map/ppermute | solution.py:798
  44.1 0.7 %collective-permute-start.11 = (bf16[176,128]{1,0:T(8,128)(2,1)S(1)}, bf16[176,128]{1,0:T(8,128)(2,1)S(1)}, u32[]{:S(2)}, u32[]{:S(2)}) collective-permute-start(bf16[176,128]{1,0:T(8,128)(2,1)S(1)} %add_convert_fusion), channel_id=1, source_target_pairs={{0,4},{1,5},{2,6},{3,7},{4,0},{5,1},{6,2},{7,3},{8,12},{9,13},{10,... | collective-permute-start | bytes 135176 | tf_op jit(solution)/shard_map/ppermute | solution.py:798
  44.8 1.4 %collective-permute-start.10 = (bf16[176,128]{1,0:T(8,128)(2,1)S(1)}, bf16[176,128]{1,0:T(8,128)(2,1)S(1)}, u32[]{:S(2)}, u32[]{:S(2)}) collective-permute-start(bf16[176,128]{1,0:T(8,128)(2,1)S(1)} %add_convert_fusion), channel_id=1, source_target_pairs={{0,1},{1,0},{2,3},{3,2},{4,5},{5,4},{6,7},{7,6},{8,9},{9,8},{10,11... | collective-permute-start | bytes 135176 | tf_op jit(solution)/shard_map/ppermute | solution.py:798
  46.2 3.1 %shard_map.115 = (bf16[96,2,2,96]{3,2,1,0:T(2,128)(2,1)}, bf16[96,2,2,96]{3,2,1,0:T(2,128)(2,1)}) custom-call(s32[6]{0:T(128)S(1)} %stack.48.ids_ref, bf16[96,512]{1,0:T(8,128)(2,1)S(1)} %get-tuple-element.68.hidden_ref, bf16[96,512]{1,0:T(8,128)(2,1)S(1)} %get-tuple-element.69.pre_grad_ref, bf16[96,640]{1,0:T(8,128)(2,1)S(1)} %get-tuple-element.70.hidden_out, ...), custom_call_target="tpu_custom_call" | custom-call | tf_op jit(solution)/shard_map/pallas_call | solution.py:750
  49.3 0.0 collective-permute-done.12
  49.3 0.0 collective-permute-done.11
  49.3 0.0 collective-permute-done.10
  49.3 0.1 collective-permute-start.13
  49.4 1.4 %collective-permute-done.13.theirs_ref = bf16[4,176,128]{2,1,0:T(8,128)(2,1)S(1)} collective-permute-done((bf16[4,176,128]{2,1,0:T(8,128)(2,1)S(1)}, bf16[4,176,128]{2,1,0:T(8,128)(2,1)S(1)}, u32[]{:S(2)}, u32[]{:S(2)}) %collective-permute-start.13) | collective-permute-done | bytes 180256 | tf_op jit(solution)/shard_map/ppermute | solution.py:798
  50.8 1.6 %shard_map.116 = (f32[864,96]{1,0:T(8,128)}, f32[864,96]{1,0:T(8,128)}) custom-call(s32[6]{0:T(128)S(1)} %stack.48.ids_ref, bf16[4,176,128]{2,1,0:T(8,128)(2,1)S(1)} %pad_maximum_fusion.mine_ref, bf16[4,176,128]{2,1,0:T(8,128)(2,1)S(1)} %collective-permute-done.13.theirs_ref), custom_call_target="tpu_custom_call" | custom-call | tf_op jit(solution)/shard_map/pallas_call | solution.py:750
  (9 shorter events, 0.2 us)
Async XLA Ops:
  1.7 5.0 %copy-start.5 = (s32[3,1,768]{2,1,0:T(1,128)S(1)}, s32[3,1,768]{2,1,0:T(1,128)}, u32[]{:S(2)}) copy-start(s32[3,1,768]{2,1,0:T(1,128)} %constant.36.clone.table_ref) | copy-start | bytes 27652
  1.7 10.9 %collective-permute-start = (bf16[2,2,2,96,128]{4,3,2,1,0:T(8,128)(2,1)S(1)}, bf16[2,2,2,96,128]{4,3,2,1,0:T(8,128)(2,1)S(1)}, u32[]{:S(2)}, u32[]{:S(2)}) collective-permute-start(bf16[2,2,2,96,128]{4,3,2,1,0:T(8,128)(2,1)S(1)} %pad.4.columns_ref.refs_0_), channel_id=1, source_target_pairs={{30,31},{31,30},{1,0},{0,1}} | collective-permute-start | bytes 589832 | tf_op jit(solution)/shard_map/ppermute | solution.py:766
  6.6 17.0 %copy-start.4 = (bf16[768,128]{1,0:T(8,128)(2,1)S(1)}, bf16[768,128]{1,0:T(8,128)(2,1)}, u32[]{:S(2)}) copy-start(bf16[768,128]{1,0:T(8,128)(2,1)} %constant.39.clone.refs_7_) | copy-start | bytes 589828
  6.7 16.9 %copy-start.2 = (bf16[3,3,96,96]{3,2,1,0:T(8,128)(2,1)S(1)}, bf16[3,3,96,96]{3,2,1,0:T(8,128)(2,1)}, u32[]{:S(2)}) copy-start(bf16[3,3,96,96]{3,2,1,0:T(8,128)(2,1)} %param.10) | copy-start | bytes 497668
  6.7 16.9 %copy-start.3 = (bf16[3,3,96,96]{3,2,1,0:T(8,128)(2,1)S(1)}, bf16[3,3,96,96]{3,2,1,0:T(8,128)(2,1)}, u32[]{:S(2)}) copy-start(bf16[3,3,96,96]{3,2,1,0:T(8,128)(2,1)} %param.11) | copy-start | bytes 497668
  8.5 15.1 %copy-start.1 = (bf16[384,1024]{1,0:T(8,128)(2,1)S(1)}, bf16[384,1024]{1,0:T(8,128)(2,1)}, u32[]{:S(2)}) copy-start(bf16[384,1024]{1,0:T(8,128)(2,1)} %constant.37.clone.refs_5_) | copy-start | bytes 2359300
  8.5 13.0 %all-to-all-start = ((bf16[32,24,96]{2,1,0:T(8,128)(2,1)}), bf16[32,24,96]{2,1,0:T(8,128)(2,1)S(1)}, u32[]{:S(2)}, u32[]{:S(2)}) async-start(bf16[32,24,96]{2,1,0:T(8,128)(2,1)} %bitcast.8), calls=%async_computation | async-start | bytes 393216 | tf_op jit(solution)/shard_map/all_to_all | solution.py:788
  12.6 11.0 %copy-start = (bf16[384,1024]{1,0:T(8,128)(2,1)S(1)}, bf16[384,1024]{1,0:T(8,128)(2,1)}, u32[]{:S(2)}) copy-start(bf16[384,1024]{1,0:T(8,128)(2,1)} %constant.38.clone.refs_6_) | copy-start | bytes 2359300
  12.7 10.9 %collective-permute-start.2 = (bf16[2,2,2,96,128]{4,3,2,1,0:T(8,128)(2,1)S(1)}, bf16[2,2,2,96,128]{4,3,2,1,0:T(8,128)(2,1)S(1)}, u32[]{:S(2)}, u32[]{:S(2)}) collective-permute-start(bf16[2,2,2,96,128]{4,3,2,1,0:T(8,128)(2,1)S(1)} %maximum_select_fusion), channel_id=1, source_target_pairs={{0,30},{2,4},{4,2},{6,8},{8,6},{10,12},{12,10},{14,16},{16,14},{18... | collective-permute-start | bytes 589832 | tf_op jit(solution)/shard_map/ppermute | solution.py:781
  17.0 6.5 %collective-permute-start.1 = (bf16[2,2,2,96,128]{4,3,2,1,0:T(8,128)(2,1)S(1)}, bf16[2,2,2,96,128]{4,3,2,1,0:T(8,128)(2,1)S(1)}, u32[]{:S(2)}, u32[]{:S(2)}) collective-permute-start(bf16[2,2,2,96,128]{4,3,2,1,0:T(8,128)(2,1)S(1)} %pad.4.columns_ref.refs_0_), channel_id=1, source_target_pairs={{0,2},{2,0},{4,6},{6,4},{8,10},{10,8},{12,14},{14,12},{16,18},{18,... | collective-permute-start | bytes 589832 | tf_op jit(solution)/shard_map/ppermute | solution.py:780
  27.1 1.5 %collective-permute-start.3 = (bf16[4,176,128]{2,1,0:T(8,128)(2,1)S(1)}, bf16[4,176,128]{2,1,0:T(8,128)(2,1)S(1)}, u32[]{:S(2)}, u32[]{:S(2)}) collective-permute-start(bf16[4,176,128]{2,1,0:T(8,128)(2,1)S(1)} %get-tuple-element.49), channel_id=1, source_target_pairs={{0,2},{1,3},{2,0},{3,1},{4,6},{5,7},{6,4},{7,5},{8,10},{9,11},{10,... | collective-permute-start | bytes 540680 | tf_op jit(solution)/shard_map/ppermute | solution.py:798
  28.6 6.0 %collective-permute-start.6 = (bf16[176,128]{1,0:T(8,128)(2,1)S(1)}, bf16[176,128]{1,0:T(8,128)(2,1)S(1)}, u32[]{:S(2)}, u32[]{:S(2)}) collective-permute-start(bf16[176,128]{1,0:T(8,128)(2,1)S(1)} %get-tuple-element.86), channel_id=1, source_target_pairs={{0,5},{1,4},{2,7},{3,6},{4,1},{5,0},{6,3},{7,2},{8,13},{9,12},{10,... | collective-permute-start | bytes 135176 | tf_op jit(solution)/shard_map/ppermute | solution.py:798
  30.2 4.5 %collective-permute-start.5 = (bf16[176,128]{1,0:T(8,128)(2,1)S(1)}, bf16[176,128]{1,0:T(8,128)(2,1)S(1)}, u32[]{:S(2)}, u32[]{:S(2)}) collective-permute-start(bf16[176,128]{1,0:T(8,128)(2,1)S(1)} %get-tuple-element.87), channel_id=1, source_target_pairs={{0,4},{1,5},{2,6},{3,7},{4,0},{5,1},{6,2},{7,3},{8,12},{9,13},{10,... | collective-permute-start | bytes 135176 | tf_op jit(solution)/shard_map/ppermute | solution.py:798
  31.6 4.0 %collective-permute-start.4 = (bf16[176,128]{1,0:T(8,128)(2,1)S(1)}, bf16[176,128]{1,0:T(8,128)(2,1)S(1)}, u32[]{:S(2)}, u32[]{:S(2)}) collective-permute-start(bf16[176,128]{1,0:T(8,128)(2,1)S(1)} %get-tuple-element.88), channel_id=1, source_target_pairs={{0,1},{1,0},{2,3},{3,2},{4,5},{5,4},{6,7},{7,6},{8,9},{9,8},{10,11... | collective-permute-start | bytes 135176 | tf_op jit(solution)/shard_map/ppermute | solution.py:798
  35.6 6.7 %collective-permute-start.9 = (bf16[176,128]{1,0:T(8,128)(2,1)S(1)}, bf16[176,128]{1,0:T(8,128)(2,1)S(1)}, u32[]{:S(2)}, u32[]{:S(2)}) collective-permute-start(bf16[176,128]{1,0:T(8,128)(2,1)S(1)} %fusion.2), channel_id=1, source_target_pairs={{0,24},{1,25},{2,26},{3,27},{4,28},{5,29},{6,30},{7,31},{8,16},{9,... | collective-permute-start | bytes 135176 | tf_op jit(solution)/shard_map/ppermute | solution.py:798
  36.8 5.7 %collective-permute-start.8 = (bf16[176,128]{1,0:T(8,128)(2,1)S(1)}, bf16[176,128]{1,0:T(8,128)(2,1)S(1)}, u32[]{:S(2)}, u32[]{:S(2)}) collective-permute-start(bf16[176,128]{1,0:T(8,128)(2,1)S(1)} %fusion.2), channel_id=1, source_target_pairs={{0,16},{1,17},{2,18},{3,19},{4,20},{5,21},{6,22},{7,23},{8,24},{9,... | collective-permute-start | bytes 135176 | tf_op jit(solution)/shard_map/ppermute | solution.py:798
  37.8 4.8 %collective-permute-start.7 = (bf16[176,128]{1,0:T(8,128)(2,1)S(1)}, bf16[176,128]{1,0:T(8,128)(2,1)S(1)}, u32[]{:S(2)}, u32[]{:S(2)}) collective-permute-start(bf16[176,128]{1,0:T(8,128)(2,1)S(1)} %fusion.2), channel_id=1, source_target_pairs={{0,8},{1,9},{2,10},{3,11},{4,12},{5,13},{6,14},{7,15},{8,0},{9,1},... | collective-permute-start | bytes 135176 | tf_op jit(solution)/shard_map/ppermute | solution.py:798
  42.6 6.7 %collective-permute-start.12 = (bf16[176,128]{1,0:T(8,128)(2,1)S(1)}, bf16[176,128]{1,0:T(8,128)(2,1)S(1)}, u32[]{:S(2)}, u32[]{:S(2)}) collective-permute-start(bf16[176,128]{1,0:T(8,128)(2,1)S(1)} %add_convert_fusion), channel_id=1, source_target_pairs={{0,5},{1,4},{2,7},{3,6},{4,1},{5,0},{6,3},{7,2},{8,13},{9,12},{10,... | collective-permute-start | bytes 135176 | tf_op jit(solution)/shard_map/ppermute | solution.py:798
  44.1 5.2 %collective-permute-start.11 = (bf16[176,128]{1,0:T(8,128)(2,1)S(1)}, bf16[176,128]{1,0:T(8,128)(2,1)S(1)}, u32[]{:S(2)}, u32[]{:S(2)}) collective-permute-start(bf16[176,128]{1,0:T(8,128)(2,1)S(1)} %add_convert_fusion), channel_id=1, source_target_pairs={{0,4},{1,5},{2,6},{3,7},{4,0},{5,1},{6,2},{7,3},{8,12},{9,13},{10,... | collective-permute-start | bytes 135176 | tf_op jit(solution)/shard_map/ppermute | solution.py:798
  44.8 4.5 %collective-permute-start.10 = (bf16[176,128]{1,0:T(8,128)(2,1)S(1)}, bf16[176,128]{1,0:T(8,128)(2,1)S(1)}, u32[]{:S(2)}, u32[]{:S(2)}) collective-permute-start(bf16[176,128]{1,0:T(8,128)(2,1)S(1)} %add_convert_fusion), channel_id=1, source_target_pairs={{0,1},{1,0},{2,3},{3,2},{4,5},{5,4},{6,7},{7,6},{8,9},{9,8},{10,11... | collective-permute-start | bytes 135176 | tf_op jit(solution)/shard_map/ppermute | solution.py:798
  49.3 1.5 %collective-permute-start.13 = (bf16[4,176,128]{2,1,0:T(8,128)(2,1)S(1)}, bf16[4,176,128]{2,1,0:T(8,128)(2,1)S(1)}, u32[]{:S(2)}, u32[]{:S(2)}) collective-permute-start(bf16[4,176,128]{2,1,0:T(8,128)(2,1)S(1)} %pad_maximum_fusion.mine_ref), channel_id=1, source_target_pairs={{0,2},{1,3},{2,0},{3,1},{4,6},{5,7},{6,4},{7,5},{8,10},{9,11},{10,... | collective-permute-start | bytes 540680 | tf_op jit(solution)/shard_map/ppermute | solution.py:798
